TPU v7x, 256 devices: a whole 4x4x8 slice. The times are simulated.
256 devices in a mesh: grp: 16 (over x, y), beam: 16 (over z, core).
Axes of the slice: x: 4, y: 4, z: 8, core: 2. Of those that a mesh axis runs over, the one named last changes fastest.
Arguments:
- subimages: float32 [2, 16, 2048, 2048], P(None, 'grp', 'beam'), may hold values from -6 to 6
- beam_weights: float32 [2, 2, 2, 4], replicated, may hold values from -3 to 3
- range_tiles: float32 [2, 3, 512, 512], replicated, may hold values from -0.15625 to 0.15625
- tile_offsets: int32 [2, 2, 128], P(None, None, 'beam'), may hold values from 0 to 2
- phase_rates: float32 [2, 2, 2048], P(None, None, 'beam'), may hold values from -3 to 3
Outputs:
- merged: float32 [2, 16, 2048, 2048], P(None, 'grp', 'beam')
All inputs are finite; a program needn't handle non-finite values.
Results may differ from a plain program's by a relative error of at most 0.0001.
Values sent between devices are 32-bit elements; how exact they have to be, the bound alone decides.
No kernel may reach another device: no remote copies, remote signals or barrier semaphores. Data moves between devices by JAX's collectives and lax.ppermute only.
A program may use at most 128 MiB of HBM per device.

v0:
```python
import jax
import jax.numpy as jnp
from jax import lax
from jax.sharding import PartitionSpec as P

TILE = 512
TAPS = 3
BLK = 16
BIT1 = 0
BIT2 = 1


def from_partner(value, axis, distance):
    return lax.ppermute(value, axis, [(i, i ^ 1 << distance) for i in range(lax.axis_size(axis))])


def padded_2(cells, sides, width):
    for axis, dim in sides:
        count = lax.axis_size(axis)
        ends = count - 1
        head = lax.slice_in_dim(cells, 0, width, axis=dim)
        tail = lax.slice_in_dim(cells, cells.shape[dim] - width, cells.shape[dim], axis=dim)
        cells = jnp.concatenate(
            [
                lax.ppermute(tail, axis, [(i, (i + 1) % count) for i in range(ends)]),
                cells,
                lax.ppermute(head, axis, [((i + 1) % count, i) for i in range(ends)]),
            ],
            axis=dim,
        )
    return cells


def range_interp(rows, offsets, tiles):
    beams_here = rows.shape[1]
    width = rows.shape[2]
    padded = jnp.pad(rows, ((0, 0), (0, 0), (TILE, 3 * TILE)))

    def block_step(block_index, result):
        rows_block = lax.dynamic_slice_in_dim(padded, block_index * BLK, BLK, 1)
        shift_tiles = offsets[block_index]
        summed = jnp.zeros((2, BLK, width // TILE, TILE), jnp.float32)
        for tap_no in range(TAPS):
            window = lax.dynamic_slice_in_dim(rows_block, (shift_tiles + tap_no) * TILE, width, 2)
            window = window.reshape(2, BLK, width // TILE, TILE)
            summed = summed + jnp.einsum(
                "cbnt,tu->cbnu", window, tiles[tap_no], precision=lax.Precision.HIGHEST
            )
        return lax.dynamic_update_slice_in_dim(
            result, summed.reshape(2, BLK, width), block_index * BLK, 1
        )

    result = jnp.zeros((2, beams_here, width), jnp.float32)
    return lax.fori_loop(0, beams_here // BLK, block_step, result)


def contribute(
    rimmed, section_no, parity_out, child_bit, beam_weights, range_tiles, tile_offsets, phase_rates
):
    beams_here = rimmed.shape[1] - 4
    width = rimmed.shape[2]
    weights = beam_weights[section_no][parity_out, child_bit]
    blended = weights[0] * rimmed[:, 1 : 1 + beams_here]
    for beam_tap in range(1, 4):
        blended = blended + weights[beam_tap] * rimmed[:, 1 + beam_tap : 1 + beam_tap + beams_here]
    ranged = range_interp(blended, tile_offsets[section_no][child_bit], range_tiles[section_no])
    column_pos = jnp.arange(width, dtype=jnp.float32) / TILE
    angles = phase_rates[section_no][child_bit][:, None] * column_pos[None, :]
    cosine = jnp.cos(angles)
    sine_part = jnp.sin(angles)
    real_part = ranged[0] * cosine - ranged[1] * sine_part
    imag_part = ranged[0] * sine_part + ranged[1] * cosine
    return jnp.stack((real_part, imag_part))


def section_raw(current, section_no, bit_pos, parity, params):
    partner = from_partner(current, "grp", bit_pos)
    lower_child = jnp.where(parity == 0, current, partner)
    upper_child = jnp.where(parity == 0, partner, current)
    rimmed = padded_2(jnp.stack((lower_child, upper_child)), (("beam", 2),), 2)
    lower_term = contribute(rimmed[0], section_no, parity, 0, *params)
    upper_term = contribute(rimmed[1], section_no, parity, 1, *params)
    return lower_term + upper_term


def per_device(subimages, beam_weights, range_tiles, tile_offsets, phase_rates):
    params = (beam_weights, range_tiles, tile_offsets, phase_rates)
    current = subimages[:, 0]
    group_id = lax.axis_index("grp")
    for section_no, bit_pos in ((0, BIT1), (1, BIT2)):
        parity = group_id >> bit_pos & 1
        current = section_raw(current, section_no, bit_pos, parity, params)
    return current[:, None]


def solution(mesh):
    return jax.shard_map(
        per_device,
        mesh=mesh,
        in_specs=(
            P(None, "grp", "beam", None),
            P(),
            P(),
            P(None, None, "beam"),
            P(None, None, "beam"),
        ),
        out_specs=P(None, "grp", "beam", None),
        check_vma=False,
    )
```

profile of v0, /device:TPU:97, one launch (start us, length us, event | category | flops | bytes accessed | tf_op | source)
XLA Modules:
  0.0 437.0 jit_solution(6489822522949563126)
XLA Ops:
  4.8 5.7 %slice_bitcast_fusion = (f32[3,512,512]{2,1,0:T(8,128)S(1)}, f32[3,512,512]{2,1,0:T(8,128)}) fusion(f32[2,3,512,512]{3,2,1,0:T(8,128)} %param.15), kind=kLoop, calls=%fused_computation.82 | loop fusion | bytes 12582912 | tf_op jit(solution)/shard_map/squeeze | solution.py:66
  10.6 36.2 %collective-permute-done = f32[2,128,2048]{2,1,0:T(8,128)} collective-permute-done((f32[2,128,2048]{2,1,0:T(8,128)}, f32[2,128,2048]{2,1,0:T(8,128)}, u32[]{:S(2)}, u32[]{:S(2)}) %collective-permute-start) | collective-permute-done | bytes 2097184 | tf_op jit(solution)/shard_map/ppermute | solution.py:14
  48.9 6.2 %collective-permute-start.1 = (f32[2,2,2,2048]{3,2,1,0:T(2,128)S(1)}, f32[2,2,2,2048]{3,2,1,0:T(2,128)S(1)}, u32[]{:S(2)}, u32[]{:S(2)}) collective-permute-start(f32[2,2,2,2048]{3,2,1,0:T(2,128)S(1)} %get-tuple-element.679), channel_id=1, source_target_pairs={{0,1},{1,2},{2,3},{3,4},{4,5},{5,6},{6,7},{7,8},{8,9},{9,10},{10,1... | collective-permute-start | bytes 196616 | tf_op jit(solution)/shard_map/ppermute | solution.py:25
  57.0 4.8 %collective-permute-done.2 = f32[2,2,2,2048]{3,2,1,0:T(2,128)S(1)} collective-permute-done((f32[2,2,2,2048]{3,2,1,0:T(2,128)S(1)}, f32[2,2,2,2048]{3,2,1,0:T(2,128)S(1)}, u32[]{:S(2)}, u32[]{:S(2)}) %collective-permute-start.2) | collective-permute-done | bytes 65568 | tf_op jit(solution)/shard_map/ppermute | solution.py:27
  64.4 3.6 fusion.65
  68.0 2.5 pad.13
  72.0 66.5 %while.64 = (s32[]{:T(128)}, f32[2,128,2048]{2,1,0:T(8,128)}, s32[8]{0:T(128)S(1)}, f32[2,128,4096]{2,1,0:T(8,128)}, f32[3,512,512]{2,1,0:T(8,128)}, /*index=5*/...) while((s32[]{:T(128)}, f32[2,128,2048]{2,1,0:T(8,128)}, ...), condition=%wide.region_1.2_spmd, body=%wide.region_0.1_spmd.sunk | while | flops 1208090624 | bytes 20447704 | solution.py:54
  138.5 7.6 %fusion.62 = f32[2,128,2048]{2,1,0:T(8,128)S(1)} fusion(f32[2,132,2048]{2,1,0:T(8,128)} %get-tuple-element.673, f32[]{:T(128)} %bitcast.66, f32[]{:T(128)} %bitcast.65, f32[]{:T(128)} %bitcast.64, f32[]{:T(128)} %bitcast.62), kind=kLoop, calls=%fused_computation.103 | loop fusion | flops 3670016 | bytes 10485776 | tf_op jit(solution)/shard_map/add | solution.py:65
  146.1 2.5 pad.14
  150.1 68.9 %while.65 = (s32[]{:T(128)}, f32[2,128,2048]{2,1,0:T(8,128)}, s32[8]{0:T(128)S(1)}, f32[2,128,4096]{2,1,0:T(8,128)}, f32[3,512,512]{2,1,0:T(8,128)}, /*index=5*/...) while((s32[]{:T(128)}, f32[2,128,2048]{2,1,0:T(8,128)}, ...), condition=%wide.region_3.4_spmd, body=%wide.region_2.3_spmd.sunk | while | flops 1208090624 | bytes 20447704 | solution.py:54
  219.0 9.6 %fusion.92 = (f32[1,128,2048]{2,1,0:T(8,128)S(1)}, f32[1,128,2048]{2,1,0:T(8,128)S(1)}, f32[1,128,2048]{2,1,0:T(8,128)S(1)}, f32[1,128,2048]{2,1,0:T(8,128)S(1)}) fusion(f32[2,128,2048]{2,1,0:T(8,128)} %get-tuple-element.614, f32[128]{0:T(128)S(1)} %get-tuple-element.698, f32[2048]{0:T(1024)S(1)} %iota_multiply_fusion, ...), kind=kLoop, calls=%fused_computation.154 | loop fusion | flops 3670016 | bytes 8397824 | tf_op jit(solution)/shard_map/sub | solution.py:71
  231.3 2.9 collective-permute-start.3
  234.9 42.4 %collective-permute-done.3 = f32[2,128,2048]{2,1,0:T(8,128)} collective-permute-done((f32[2,128,2048]{2,1,0:T(8,128)}, f32[2,128,2048]{2,1,0:T(8,128)}, u32[]{:S(2)}, u32[]{:S(2)}) %collective-permute-start.3) | collective-permute-done | bytes 2097184 | tf_op jit(solution)/shard_map/ppermute | solution.py:14
  277.3 3.4 select_bitcast_fusion.1
  280.8 5.1 %collective-permute-start.4 = (f32[2,2,2,2048]{3,2,1,0:T(2,128)S(1)}, f32[2,2,2,2048]{3,2,1,0:T(2,128)S(1)}, u32[]{:S(2)}, u32[]{:S(2)}) collective-permute-start(f32[2,2,2,2048]{3,2,1,0:T(2,128)S(1)} %get-tuple-element.675), channel_id=1, source_target_pairs={{0,1},{1,2},{2,3},{3,4},{4,5},{5,6},{6,7},{7,8},{8,9},{9,10},{10,1... | collective-permute-start | bytes 196616 | tf_op jit(solution)/shard_map/ppermute | solution.py:25
  285.9 2.1 collective-permute-start.5
  288.7 4.1 collective-permute-done.5
  295.6 3.6 fusion.59
  299.2 2.5 pad.15
  303.3 54.7 %while.66 = (s32[]{:T(128)}, f32[2,128,2048]{2,1,0:T(8,128)}, s32[8]{0:T(128)S(1)}, f32[2,128,4096]{2,1,0:T(8,128)}, f32[3,512,512]{2,1,0:T(8,128)S(1)}, /*index...) while((s32[]{:T(128)}, f32[2,128,2048]{2,1,0:T(8,128)}, ...), condition=%wide.region_5.6_spmd, body=%wide.region_4.5_spmd.sunk | while | flops 1208090624 | bytes 7864765 | solution.py:54
  358.0 7.4 %fusion.56 = f32[2,128,2048]{2,1,0:T(8,128)S(1)} fusion(f32[2,132,2048]{2,1,0:T(8,128)} %get-tuple-element.671, f32[]{:T(128)} %bitcast.83, f32[]{:T(128)} %bitcast.82, f32[]{:T(128)} %bitcast.81, f32[]{:T(128)} %bitcast.79), kind=kLoop, calls=%fused_computation.89 | loop fusion | flops 3670016 | bytes 10485776 | tf_op jit(solution)/shard_map/add | solution.py:65
  365.4 2.5 pad.16
  369.5 56.3 %while.67 = (s32[]{:T(128)}, f32[2,128,2048]{2,1,0:T(8,128)}, s32[8]{0:T(128)S(1)}, f32[2,128,4096]{2,1,0:T(8,128)}, f32[3,512,512]{2,1,0:T(8,128)S(1)}, /*index...) while((s32[]{:T(128)}, f32[2,128,2048]{2,1,0:T(8,128)}, ...), condition=%wide.region_7.8_spmd, body=%wide.region_6.7_spmd.sunk | while | flops 1208090624 | bytes 7864765 | solution.py:54
  425.8 9.6 %fusion.85 = (f32[1,1,128,2048]{3,2,1,0:T(8,128)S(1)}, f32[1,1,128,2048]{3,2,1,0:T(8,128)S(1)}, f32[1,1,128,2048]{3,2,1,0:T(8,128)S(1)}, f32[1,1,128,2048]{3,2,1,0:T(8,128)S(1)}) fusion(f32[2,128,2048]{2,1,0:T(8,128)} %get-tuple-element.616, f32[128]{0:T(128)S(1)} %get-tuple-element.697, f32[2048]{0:T(1024)S(1)} %iota_multiply_fusion, ...), kind=kLoop, calls=%fused_computation.147 | loop fusion | flops 3670016 | bytes 8397824 | tf_op jit(solution)/shard_map/stack | solution.py:73
  (292 shorter events, 209.7 us)
Async XLA Ops:
  0.0 46.8 %collective-permute-start = (f32[2,128,2048]{2,1,0:T(8,128)}, f32[2,128,2048]{2,1,0:T(8,128)}, u32[]{:S(2)}, u32[]{:S(2)}) collective-permute-start(f32[2,128,2048]{2,1,0:T(8,128)} %bitcast.347), channel_id=1, source_target_pairs={{0,16},{16,0},{32,48},{48,32},{64,80},{80,64},{96,112},{112,96},{1... | collective-permute-start | bytes 6291464 | tf_op jit(solution)/shard_map/ppermute | solution.py:14
  4.8 42.0 %copy-start.6 = (f32[2,1,128,2048]{3,2,1,0:T(8,128)S(1)}, f32[2,1,128,2048]{3,2,1,0:T(8,128)}, u32[]{:S(2)}) copy-start(f32[2,1,128,2048]{3,2,1,0:T(8,128)} %param.13) | copy-start | bytes 6291460
  48.9 8.1 %collective-permute-start.1 = (f32[2,2,2,2048]{3,2,1,0:T(2,128)S(1)}, f32[2,2,2,2048]{3,2,1,0:T(2,128)S(1)}, u32[]{:S(2)}, u32[]{:S(2)}) collective-permute-start(f32[2,2,2,2048]{3,2,1,0:T(2,128)S(1)} %get-tuple-element.679), channel_id=1, source_target_pairs={{0,1},{1,2},{2,3},{3,4},{4,5},{5,6},{6,7},{7,8},{8,9},{9,10},{10,1... | collective-permute-start | bytes 196616 | tf_op jit(solution)/shard_map/ppermute | solution.py:25
  55.1 6.8 %collective-permute-start.2 = (f32[2,2,2,2048]{3,2,1,0:T(2,128)S(1)}, f32[2,2,2,2048]{3,2,1,0:T(2,128)S(1)}, u32[]{:S(2)}, u32[]{:S(2)}) collective-permute-start(f32[2,2,2,2048]{3,2,1,0:T(2,128)S(1)} %get-tuple-element.680), channel_id=1, source_target_pairs={{1,0},{2,1},{3,2},{4,3},{5,4},{6,5},{7,6},{8,7},{9,8},{10,9},{11,1... | collective-permute-start | bytes 196616 | tf_op jit(solution)/shard_map/ppermute | solution.py:27
  74.5 3.7 copy-start
  82.8 3.6 copy-start
  91.2 3.6 copy-start
  99.5 3.7 copy-start
  107.8 3.6 copy-start
  116.1 3.7 copy-start
  124.5 3.7 copy-start
  132.8 3.5 copy-start
  152.9 3.7 copy-start.1
  161.5 3.6 copy-start.1
  170.1 3.6 copy-start.1
  178.8 3.6 copy-start.1
  187.4 3.7 copy-start.1
  196.0 3.7 copy-start.1
  204.7 3.6 copy-start.1
  213.3 3.5 copy-start.1
  228.7 2.6 copy-start.5
  231.3 46.0 %collective-permute-start.3 = (f32[2,128,2048]{2,1,0:T(8,128)}, f32[2,128,2048]{2,1,0:T(8,128)}, u32[]{:S(2)}, u32[]{:S(2)}) collective-permute-start(f32[2,128,2048]{2,1,0:T(8,128)} %maximum_add_fusion), channel_id=1, source_target_pairs={{0,32},{16,48},{32,0},{48,16},{64,96},{80,112},{96,64},{112,80},{1... | collective-permute-start | bytes 6291464 | tf_op jit(solution)/shard_map/ppermute | solution.py:14
  280.8 7.9 %collective-permute-start.4 = (f32[2,2,2,2048]{3,2,1,0:T(2,128)S(1)}, f32[2,2,2,2048]{3,2,1,0:T(2,128)S(1)}, u32[]{:S(2)}, u32[]{:S(2)}) collective-permute-start(f32[2,2,2,2048]{3,2,1,0:T(2,128)S(1)} %get-tuple-element.675), channel_id=1, source_target_pairs={{0,1},{1,2},{2,3},{3,4},{4,5},{5,6},{6,7},{7,8},{8,9},{9,10},{10,1... | collective-permute-start | bytes 196616 | tf_op jit(solution)/shard_map/ppermute | solution.py:25
  285.9 6.8 %collective-permute-start.5 = (f32[2,2,2,2048]{3,2,1,0:T(2,128)S(1)}, f32[2,2,2,2048]{3,2,1,0:T(2,128)S(1)}, u32[]{:S(2)}, u32[]{:S(2)}) collective-permute-start(f32[2,2,2,2048]{3,2,1,0:T(2,128)S(1)} %get-tuple-element.676), channel_id=1, source_target_pairs={{1,0},{2,1},{3,2},{4,3},{5,4},{6,5},{7,6},{8,7},{9,8},{10,9},{11,1... | collective-permute-start | bytes 196616 | tf_op jit(solution)/shard_map/ppermute | solution.py:27
  (3 other events, 6.0 us)
where the time goes:
time: 439 us; the launch traced here: 437 us
  local copies, waits for them, and re-layouts  127 us (29%)
  matrix products  87.9 us (20%)
  waiting for transfers between devices  87.6 us (20%)
  loops' own time  62.7 us (14%)
  other arithmetic  51.7 us (12%)
  starting transfers between devices  19.6 us (4%)
    dot_general x96, matrix products, block_step(): jnp.einsum('cbnt,tu->cbnu', window, tiles[tap_no], precision=lax.Precisio...  87.9 us
    ppermute x2, waiting for transfers between devices, from_partner(): lax.ppermute(value, axis, [(i, i ^ 1 << distance) for i in range(lax.axis...  78.6 us
    another operation x4, loops' own time, range_interp(): return lax.fori_loop(0, beams_here // BLK, block_step, result)  62.7 us
    dynamic_slice x32, local copies, waits for them, and re-layouts, block_step(): lax.dynamic_slice_in_dim(rows_block, (shift_tiles + tap_no) * TILE, width...  52.3 us
    dynamic_update_slice x32, local copies, waits for them, and re-layouts, block_step(): lax.dynamic_update_slice_in_dim(result, summed.reshape(2, BLK, width), bl...  23.2 us
    add x4, other arithmetic, contribute(): blended + weights[beam_tap] * rimmed[:, 1 + beam_tap:1 + beam_tap + beams...  22.1 us
    dynamic_slice x32, local copies, waits for them, and re-layouts, block_step(): shift_tiles = offsets[block_index]  19.5 us
    ppermute x2, starting transfers between devices, padded_2(): lax.ppermute(tail, axis, [(i, (i + 1) % count) for i in range(ends)])  11.3 us
  transfers between devices with their start and end apart: 6, of which 4 were waited for; matrix products, arithmetic and copies ran while one was open for 2% of the time, Pallas kernels for 0%

commit v1 on v0

v1 whole, which is shorter than its diff:
```python
import functools

import jax
import jax.numpy as jnp
from jax import lax
from jax.experimental import pallas as pl
from jax.experimental.pallas import tpu as pltpu
from jax.sharding import PartitionSpec as P

TILE = 512
TAPS = 3
BLK = 16
RING = 4
QROWS = 32
EDGE = 8
ROWS = QROWS + EDGE
WIDTH = 2048
TILES = WIDTH // TILE
FULL = WIDTH + 2 * TILE
LANES = 256
SPANS = ((0, 16), (16, 32), (32, 40))
HBM = pl.BlockSpec(memory_space=pl.ANY)
VMEM = pl.BlockSpec(memory_space=pltpu.VMEM)
SMEM = pl.BlockSpec(memory_space=pltpu.SMEM)
IMAGE = pltpu.VMEM((2 * ROWS, WIDTH), jnp.float32)
PHASE_ROWS = ROWS + QROWS
PHASES = ((2, 2, PHASE_ROWS, TILE), (2, TILES, 2, PHASE_ROWS, 128))
MATRIX = pltpu.VMEM((TAPS * TILE, TILE), jnp.bfloat16)


def exchange(value, distance):
    count = lax.axis_size("grp")
    return lax.ppermute(value, "grp", [(i, i ^ distance) for i in range(count)])


def split(value):
    high = value.astype(jnp.bfloat16)
    low = (value - high.astype(jnp.float32)).astype(jnp.bfloat16)
    return high, low


def fetch(sems, pairs):
    copies = [pltpu.make_async_copy(a, b, sems.at[i]) for i, (a, b) in enumerate(pairs)]
    for copy in copies:
        copy.start()
    return copies


def range_products(high, low, t_high, t_low, full, count):
    rows = count * 2 * ROWS
    dot = functools.partial(jnp.dot, preferred_element_type=jnp.float32)
    for index in range(5):
        first = index - 1
        taps = [t for t in range(TAPS) if 0 <= first + t < TILES]
        k0, k1 = taps[0] * TILE, (taps[-1] + 1) * TILE
        a0, a1 = k0 + first * TILE, k1 + first * TILE
        a_high = high[:count, :, a0:a1].reshape(rows, a1 - a0)
        a_low = low[:count, :, a0:a1].reshape(rows, a1 - a0)
        summed = dot(a_high, t_high[k0:k1, :]) + (
            dot(a_high, t_low[k0:k1, :]) + dot(a_low, t_high[k0:k1, :])
        )
        full[:count, :, index * TILE : (index + 1) * TILE] = summed.reshape(count, 2 * ROWS, TILE)
    full[:count, :, 5 * TILE :] = jnp.zeros((count, 2 * ROWS, TILE), jnp.float32)


def shifted(tiles):
    rows = tiles.shape[0]
    return [
        (tiles if k == 1 else pltpu.roll(tiles, (1 - k) % rows, 0))[8 : rows - 8] for k in range(4)
    ]


def unit(phases, e, row, count, lane):
    within, across = phases
    at = pl.ds(pl.multiple_of(lane % TILE, 128), LANES)
    n = lane // TILE
    c, s = (within[i, e, row : row + count, at] for i in range(2))
    cn, sn = (
        jnp.concatenate([across[i, n, e, row : row + count, :]] * (LANES // 128), 1)
        for i in range(2)
    )
    return c * cn - s * sn, s * cn + c * sn


def merge(section, block, lane, fulls, children, halves, offsets, w_ref, phases):
    r0, r1 = SPANS[block]
    out = [[None, None], [None, None]]
    for full, e in zip(fulls, children):

        def rows_at(offset, row, count):
            start = pl.multiple_of(offset * TILE + lane, 128)
            return full[row : row + count, pl.ds(start, LANES)]

        parts = []
        for base in (0, ROWS):
            if block == 0:
                o = offsets[section, e, 0]
                tiles = [rows_at(o, base + 32, 8), rows_at(o, base, 24)]
            elif block == 1:
                tiles = [rows_at(offsets[section, e, 1], base + 8, 32)]
            else:
                after, before = offsets[section, e, 2], offsets[section, e, 3]
                row = lax.broadcasted_iota(jnp.int32, (EDGE, LANES), 0)
                middle = jnp.where(
                    row < 4, rows_at(after, base + 32, 8), rows_at(before, base + 32, 8)
                )
                tiles = [rows_at(after, base + 24, 8), middle, rows_at(before, base, 8)]
            parts.append(shifted(jnp.concatenate(tiles, 0) if len(tiles) > 1 else tiles[0]))
        cosine, sine = unit(phases, e, section * ROWS + r0, r1 - r0, lane)
        for i, h in enumerate(halves):
            w = [w_ref[section, h, e, k] for k in range(4)]
            real, imag = (
                (w[0] * part[0] + w[1] * part[1]) + (w[2] * part[2] + w[3] * part[3])
                for part in parts
            )
            new = (real * cosine - imag * sine, real * sine + imag * cosine)
            out[i] = [n if o is None else o + n for o, n in zip(out[i], new)]
    return out


def first_merges(fulls, children, halves, where, offsets, w_ref, phases, high, low):
    @pl.loop(0, WIDTH, step=LANES)
    def _(lane):
        at = pl.ds(pl.multiple_of(lane, 128), LANES)
        blocks = [
            merge(0, b, lane, fulls, children, halves, offsets, w_ref, phases)
            for b in range(3)
        ]
        row = lax.broadcasted_iota(jnp.int32, (EDGE, LANES), 0)
        keep = jnp.where(row < 4, where[3], where[2]) > 0
        for i in range(2):
            merged = jnp.concatenate(
                [
                    jnp.where(keep, blocks[b][i][comp], 0.0) if b == 2 else blocks[b][i][comp]
                    for comp in range(2)
                    for b in range(3)
                ],
                0,
            )
            high[i, :, at], low[i, :, at] = split(merged)


def second_merges(fulls, children, halves, offsets, w_ref, phases, outs):
    @pl.loop(0, WIDTH, step=LANES)
    def _(lane):
        at = pl.ds(pl.multiple_of(lane, 128), LANES)
        for b in range(2):
            r0, r1 = SPANS[b]
            merged = merge(1, b, lane, fulls, children, halves, offsets, w_ref, phases)
            for i in range(2):
                for comp in range(2):
                    outs[i][comp, r0:r1, at] = merged[i][comp]


def ends_kernel(rates_in, offs_in, image, tail, head, edges, rates, offs, sems):
    copies = fetch(
        sems,
        [
            (image.at[:, 0:8], edges.at[0]), (image.at[:, 120:128], edges.at[1]),
            (rates_in.at[0], rates), (offs_in.at[0], offs),
        ],
    )
    lane = lax.broadcasted_iota(jnp.int32, (1, WIDTH), 1)

    def line(*values):
        out = jnp.zeros((1, WIDTH), jnp.float32)
        for i, value in enumerate(values):
            out = jnp.where(lane == i, value, out)
        return out

    for copy in copies:
        copy.wait()

    def offset(e, block):
        return offs[e, block].astype(jnp.float32)

    tail[0:2] = edges[1, 0, 6:8]
    tail[2:4] = edges[1, 1, 6:8]
    tail[4:5] = line(rates[0, 127], rates[1, 127], offset(0, 7), offset(1, 7))
    tail[5:8] = jnp.zeros((3, WIDTH), jnp.float32)
    head[0:4] = edges[0, 0, 0:4]
    head[4:8] = edges[0, 1, 0:4]
    head[8:9] = line(rates[0, 0], rates[0, 1], rates[1, 0], rates[1, 1], offset(0, 0), offset(1, 0))
    head[9:16] = jnp.zeros((7, WIDTH), jnp.float32)


def quarters_kernel(distances, where, image, before, after, *refs):
    count = len(distances)
    outs, (stages, rows, sems, out_sems) = refs[:count], refs[-4:]
    copies = []
    for n, d in enumerate(distances):
        q = where[4] ^ d
        trail = pl.multiple_of(jnp.minimum(q * QROWS + QROWS, 120), 8)
        lead = pl.multiple_of(jnp.maximum(q * QROWS - 8, 0), 8)
        part = pl.ds(pl.multiple_of(q * QROWS, QROWS), QROWS)
        copies.append((image.at[:, pl.ds(trail, 8)], rows.at[n, 0]))
        copies.append((image.at[:, pl.ds(lead, 8)], rows.at[n, 1]))
        copies.append((image.at[:, part], stages.at[n, :, :QROWS]))
    copies = fetch(sems, copies)
    writes = []
    for n, d in enumerate(distances):
        q = where[4] ^ d
        copies[3 * n].wait()
        copies[3 * n + 1].wait()
        for comp in range(2):
            stages[n, comp, QROWS : QROWS + 4] = jnp.where(
                q == 3, after[4 * comp : 4 * comp + 4], rows[n, 0, comp, 0:4]
            )
            stages[n, comp, QROWS + 4 : QROWS + 6] = jnp.zeros((2, WIDTH), jnp.float32)
            stages[n, comp, QROWS + 6 :] = jnp.where(
                q == 0, before[2 * comp : 2 * comp + 2], rows[n, 1, comp, 6:8]
            )
        copies[3 * n + 2].wait()
        writes += fetch(out_sems.at[n : n + 1], [(stages.at[n], outs[n])])
    for copy in writes:
        copy.wait()


def split_tiles(values, high, low):
    @pl.loop(0, TAPS * TILE, step=64)
    def _(row):
        at = pl.ds(pl.multiple_of(row, 64), 64)
        high[at], low[at] = split(values[at])


def own_kernel(tiles, q0, full1_out, t_high, t_low, high, low, full, t1, t2, th, tl, sems, out_sems):
    copies = fetch(sems, [(tiles.at[0], t1), (tiles.at[1], t2)])
    high[0], low[0] = split(q0[...].reshape(2 * ROWS, WIDTH))
    copies[0].wait()
    split_tiles(t1, th.at[0], tl.at[0])
    outs = fetch(out_sems, [(th.at[0], t_high.at[0]), (tl.at[0], t_low.at[0])])
    range_products(high, low, th.at[0], tl.at[0], full, 1)
    outs += fetch(out_sems.at[2:3], [(full.at[0], full1_out)])
    copies[1].wait()
    split_tiles(t2, th.at[1], tl.at[1])
    outs += fetch(out_sems.at[3:5], [(th.at[1], t_high.at[1]), (tl.at[1], t_low.at[1])])
    for copy in outs:
        copy.wait()


def early_kernel(
    where, offsets, w_ref, full1_in, m1, m3, t_high, t_low, within, across,
    full1_out, full2_out,
    image1, image3, high, low, full, full2, ph1, ph2, th1, tl1, th2, tl2, sems, out_sems,
):
    copies = fetch(
        sems,
        [
            (m1, image1), (m3, image3), (t_high.at[0], th1), (t_low.at[0], tl1),
            (full1_in, full.at[2]), (within, ph1), (across, ph2),
            (t_high.at[1], th2), (t_low.at[1], tl2),
        ],
    )
    phases = (ph1, ph2)
    bit = where[0]
    for slot, image in enumerate((image1, image3)):
        copies[slot].wait()
        high[slot], low[slot] = split(image[...].reshape(2 * ROWS, WIDTH))
    copies[2].wait()
    copies[3].wait()
    range_products(high, low, th1, tl1, full, 2)
    outs = fetch(out_sems, [(full.at[1], full1_out)])
    for copy in copies[4:7]:
        copy.wait()
    first_merges(
        (full.at[2], full.at[0]), (bit, 1 - bit), (bit, 1 - bit),
        where, offsets, w_ref, phases, high, low,
    )
    copies[7].wait()
    copies[8].wait()
    range_products(high, low, th2, tl2, full2, 2)
    outs += fetch(out_sems.at[1:2], [(full2, full2_out)])
    for copy in outs:
        copy.wait()


def middle_kernel(
    where, offsets, w_ref, image, full1_in, full2_in, t_high, t_low, within, across,
    d2, result, full2_out,
    rows, fulls, ph1, ph2, high, low, full2, d0, th1, tl1, th2, tl2, sems, out_sems,
):
    copies = fetch(
        sems,
        [
            (image, rows), (t_high.at[0], th1), (t_low.at[0], tl1), (full1_in, fulls.at[1]),
            (within, ph1), (across, ph2), (t_high.at[1], th2), (t_low.at[1], tl2),
            (full2_in.at[0], fulls.at[2]),
        ],
    )
    phases = (ph1, ph2)
    bit, bit2 = where[0], where[1]
    copies[0].wait()
    high[0], low[0] = split(rows[...].reshape(2 * ROWS, WIDTH))
    copies[1].wait()
    copies[2].wait()
    range_products(high, low, th1, tl1, fulls, 1)
    for copy in copies[3:6]:
        copy.wait()
    first_merges(
        (fulls.at[0], fulls.at[1]), (bit, 1 - bit), (bit, 1 - bit),
        where, offsets, w_ref, phases, high, low,
    )
    copies[6].wait()
    copies[7].wait()
    range_products(high, low, th2, tl2, full2, 2)
    out = pltpu.make_async_copy(full2.at[1], full2_out, out_sems.at[0])
    out.start()
    copies[8].wait()
    second_merges(
        (fulls.at[2], full2.at[0]), (bit2, 1 - bit2), (bit2, 1 - bit2),
        offsets, w_ref, phases, (d0, d2),
    )
    at = pl.ds(pl.multiple_of(where[4] * QROWS, QROWS), QROWS)
    kept = pltpu.make_async_copy(d0, result.at[:, at], out_sems.at[1])
    kept.start()
    out.wait()
    kept.wait()


def late_kernel(
    where, offsets, w_ref, full2_in, full_b, within, across, d1, d3, fa, fb, ph1, ph2, sems
):
    bit2 = where[1]
    copies = fetch(
        sems, [(full2_in.at[1], fa), (full_b, fb), (within, ph1), (across, ph2)]
    )
    for copy in copies:
        copy.wait()
    second_merges(
        (fa, fb), (bit2, 1 - bit2), (bit2, 1 - bit2), offsets, w_ref, (ph1, ph2), (d1, d3)
    )


def place_kernel(distances, where, *refs):
    pieces, out, sems = refs[: len(distances)], refs[-2], refs[-1]
    copies = []
    for i, d in enumerate(distances):
        at = pl.ds(pl.multiple_of((where[4] ^ d) * QROWS, QROWS), QROWS)
        copies.append(pltpu.make_async_copy(pieces[i], out.at[:, at], sems.at[i]))
        copies[-1].start()
    for copy in copies:
        copy.wait()


def call(kernel, name, outs, in_specs, out_specs, scratch, flops, moved, aliases=None):
    return pl.pallas_call(
        kernel,
        out_shape=[jax.ShapeDtypeStruct(shape, kind) for shape, kind in outs],
        in_specs=in_specs,
        out_specs=out_specs,
        scratch_shapes=scratch,
        input_output_aliases=aliases or {},
        compiler_params=pltpu.CompilerParams(vmem_limit_bytes=52 * 2**20),
        cost_estimate=pl.CostEstimate(flops=flops, bytes_accessed=moved, transcendentals=0),
        name=name,
    )


def halves_scratch(count):
    return [pltpu.VMEM((count, 2 * ROWS, WIDTH), jnp.bfloat16)] * 2


def full_scratch(count):
    return pltpu.VMEM((count, 2 * ROWS, FULL), jnp.float32)


def per_device(subimages, beam_weights, range_tiles, tile_offsets, phase_rates):
    f32, bf16 = jnp.float32, jnp.bfloat16
    dma = pltpu.SemaphoreType.DMA
    mine = lax.axis_index("grp") & 3
    beam = lax.axis_index("beam")
    beams = lax.axis_size("beam")
    image = subimages.reshape(2, RING * QROWS, WIDTH)
    first = jnp.logical_and(beam == 0, mine == 0)
    last = jnp.logical_and(beam == beams - 1, mine == 3)
    where = jnp.stack(
        [mine & 1, mine >> 1, 1 - first.astype(jnp.int32), 1 - last.astype(jnp.int32), mine]
    ).astype(jnp.int32)
    piece_shape = ((2, QROWS, WIDTH), f32)
    quarter_shape = ((2, ROWS, WIDTH), f32)
    tail, head = call(
        ends_kernel, "ends", [((8, WIDTH), f32), ((16, WIDTH), f32)], [HBM] * 3, [VMEM] * 2,
        [pltpu.VMEM((2, 2, 8, WIDTH), f32), pltpu.SMEM((2, 4 * QROWS), f32)]
        + [pltpu.SMEM((2, 8), jnp.int32), dma((4,))],
        10**6, 2**20,
    )(phase_rates, tile_offsets, image)
    before = lax.ppermute(tail, "beam", [(i, i + 1) for i in range(beams - 1)])
    after = lax.ppermute(head, "beam", [(i + 1, i) for i in range(beams - 1)])

    def quarters(*distances):
        count = len(distances)
        return call(
            functools.partial(quarters_kernel, distances), "quarters", [quarter_shape] * count,
            [SMEM, HBM, VMEM, VMEM], [HBM] * count,
            [pltpu.VMEM((count, 2, ROWS, WIDTH), f32), pltpu.VMEM((count, 2, 2, 8, WIDTH), f32)]
            + [dma((3 * count,)), dma((count,))],
            10**6, 3 * 2**20,
        )(where, image, before, after)

    q1, q3 = quarters(1, 3)
    m1 = exchange(q1, 1)
    m3 = exchange(q3, 3)
    q2, q0 = quarters(2, 0)
    q2, m1 = lax.optimization_barrier((q2, m1))
    m2 = exchange(q2, 2)

    before_values, after_values = before[4, :4].reshape(2, 2), after[8, :6]
    line = jnp.concatenate([before_values[0][:, None], phase_rates[0], after_values[:4].reshape(2, 2)], 1)
    line = lax.dynamic_slice_in_dim(line, mine * QROWS, QROWS + 3, 1)
    rates_b = lax.dynamic_slice_in_dim(phase_rates[1], mine * QROWS, QROWS, 1)
    rates = jnp.concatenate([line[:, 1:], jnp.zeros((2, 5), f32), line[:, :1], rates_b], 1)
    offs = tile_offsets[0].astype(f32)
    line = jnp.concatenate([before_values[1][:, None], offs, after_values[4:][:, None]], 1)
    line = lax.dynamic_slice_in_dim(line, mine * 2, 4, 1).astype(jnp.int32)
    offs_a = jnp.stack([line[:, 1], line[:, 2], line[:, 3], line[:, 0]], 1)
    offs_b = jnp.pad(lax.dynamic_slice_in_dim(tile_offsets[1], mine * 2, 2, 1), ((0, 0), (0, 2)))
    offsets = jnp.clip(jnp.stack([offs_a, offs_b]), 0, 2)
    angles = rates[:, :, None] * (jnp.arange(TILE, dtype=f32) / TILE)
    within = jnp.stack([jnp.cos(angles), jnp.sin(angles)])
    angles = jnp.arange(TILES, dtype=f32)[:, None, None, None] * rates[:, :, None]
    angles = jnp.broadcast_to(angles, (TILES, 2, PHASE_ROWS, 128))
    across = jnp.stack([jnp.cos(angles), jnp.sin(angles)])

    scalars = (where, offsets, beam_weights)
    full_shape = (2 * ROWS, FULL)
    tables = [pltpu.VMEM(shape, f32) for shape in PHASES]
    matrix_shape = ((2, TAPS * TILE, TILE), bf16)
    full1_0, t_high, t_low = call(
        own_kernel, "own", [(full_shape, f32), matrix_shape, matrix_shape], [HBM, VMEM], [HBM] * 3,
        halves_scratch(1) + [full_scratch(1)] + [pltpu.VMEM((TAPS * TILE, TILE), f32)] * 2
        + [pltpu.VMEM(*matrix_shape)] * 2 + [dma((2,)), dma((5,))],
        5 * 10**9, 14 * 2**20,
    )(range_tiles.reshape(2, TAPS * TILE, TILE), q0)
    full1, full2 = call(
        early_kernel, "early", [(full_shape, f32), ((2, *full_shape), f32)],
        [SMEM] * 3 + [HBM] * 7, [HBM] * 2,
        [pltpu.VMEM(*quarter_shape)] * 2 + halves_scratch(2) + [full_scratch(3), full_scratch(2)]
        + tables + [MATRIX] * 4 + [dma((9,)), dma((2,))],
        10 * 10**9, 16 * 2**20,
    )(*scalars, full1_0, m1, m3, t_high, t_low, within, across)
    d2, result, full2_3 = call(
        middle_kernel, "middle",
        [piece_shape, ((2, RING * QROWS, WIDTH), f32), (full_shape, f32)],
        [SMEM] * 3 + [HBM] * 7, [VMEM] + [HBM] * 2,
        [pltpu.VMEM((2, ROWS, WIDTH), f32), full_scratch(3), *tables]
        + halves_scratch(2) + [full_scratch(2), pltpu.VMEM((2, QROWS, WIDTH), f32)]
        + [MATRIX] * 4 + [dma((9,)), dma((2,))],
        9 * 10**9, 10 * 2**20,
    )(*scalars, m2, full1, full2, t_high, t_low, within, across)
    r2 = exchange(d2, 2)
    d1, d3 = call(
        late_kernel, "late", [piece_shape] * 2, [SMEM] * 3 + [HBM] * 4, [VMEM] * 2,
        [pltpu.VMEM(full_shape, f32)] * 2 + tables + [dma((4,))],
        4 * 10**9, 4 * 2**20,
    )(*scalars, full2, full2_3, within, across)
    r1 = exchange(d1, 1)
    r3 = exchange(d3, 3)

    for distances, pieces, flops in (((2,), (r2,), 10**11), ((1, 3), (r1, r3), 10**5)):
        (result,) = call(
            functools.partial(place_kernel, distances), "place", [(result.shape, f32)],
            [SMEM] + [HBM] * (len(pieces) + 1), [HBM], [dma((len(pieces),))],
            flops, 2**21, {1 + len(pieces): 0},
        )(where, *pieces, result)
    return result[:, None]


def solution(mesh):
    return jax.shard_map(
        per_device,
        mesh=mesh,
        in_specs=(
            P(None, "grp", "beam", None),
            P(),
            P(),
            P(None, None, "beam"),
            P(None, None, "beam"),
        ),
        out_specs=P(None, "grp", "beam", None),
        check_vma=False,
    )
```

time: 439 us -> 93 us (0.21)
  local copies, waits for them, and re-layouts: 127 us -> 5.26 us
  matrix products: 87.9 us -> 0 us
  loops' own time: 62.7 us -> 0 us
  waiting for transfers between devices: 87.6 us -> 25.5 us
  other arithmetic: 51.7 us -> 1.67 us
  Pallas kernels: 0 us -> 44.6 us
  starting transfers between devices: 19.6 us -> 15.2 us
    dot_general x96 -> x0, matrix products: 87.9 us -> none  [block_step(): jnp.einsum('cbnt,tu->cbnu', window, tiles[tap_no], precision=lax.Precisio...]
    dynamic_slice x65 -> x2, local copies, waits for them, and re-layouts: 71.9 us -> 0.15 us  [the longest x1 0.08 us: per_device(): lax.dynamic_slice_in_dim(tile_offsets[1], mine * 2, 2, 1)]
    another operation x4 -> x0, loops' own time: 62.7 us -> none  [range_interp(): return lax.fori_loop(0, beams_here // BLK, block_step, result)]
    ppermute x6 -> x8, waiting for transfers between devices: 87.6 us -> 25.5 us  [the longest x6 20.6 us: exchange(): return lax.ppermute(value, 'grp', [(i, i ^ distance) for i in range(count)])]
    pallas_call x0 -> x9, Pallas kernels: none -> 44.6 us  [the longest x1 12.6 us: per_device(): call(middle_kernel, 'middle', [piece_shape, ((2, RING * QROWS, WIDTH), f3...]
    add x6 -> x0, other arithmetic: 25.4 us -> none  [the longest x4 22.1 us: contribute(): blended + weights[beam_tap] * rimmed[:, 1 + beam_tap:1 + beam_tap + beams...]
    dynamic_update_slice x32 -> x0, local copies, waits for them, and re-layouts: 23.2 us -> none  [block_step(): lax.dynamic_update_slice_in_dim(result, summed.reshape(2, BLK, width), bl...]
    another operation x3, other arithmetic: 15.1 us -> 0.16 us  [the longest x1 0.07 us: per_device(): offsets = jnp.clip(jnp.stack([offs_a, offs_b]), 0, 2)]
  transfers between devices with their start and end apart: 6 -> 8, of which waited for: 4 -> 5; matrix products, arithmetic and copies ran while one was open for 2% -> 1% of each run, Pallas kernels for 0% -> 29%
where the time goes in v1:
time: 93 us; the launch traced here: 92.7 us
  Pallas kernels  44.6 us (48%)
  waiting for transfers between devices  25.5 us (27%)
  starting transfers between devices  15.2 us (16%)
  local copies, waits for them, and re-layouts  5.26 us (6%)
  other arithmetic  1.67 us (2%)
    ppermute x6, waiting for transfers between devices, exchange(): return lax.ppermute(value, 'grp', [(i, i ^ distance) for i in range(count)])  20.6 us
    pallas_call x1, Pallas kernels, per_device(): call(middle_kernel, 'middle', [piece_shape, ((2, RING * QROWS, WIDTH), f3...  12.6 us
    pallas_call x1, Pallas kernels, per_device(): call(early_kernel, 'early', [(full_shape, f32), ((2, *full_shape), f32)],...  12 us
    pallas_call x1, Pallas kernels, per_device(): call(own_kernel, 'own', [(full_shape, f32), matrix_shape, matrix_shape],...  8 us
    ppermute x6, starting transfers between devices, exchange(): return lax.ppermute(value, 'grp', [(i, i ^ distance) for i in range(count)])  7.98 us
    ppermute x1, starting transfers between devices, per_device(): before = lax.ppermute(tail, 'beam', [(i, i + 1) for i in range(beams - 1)])  5.32 us
    ppermute x1, waiting for transfers between devices, per_device(): after = lax.ppermute(head, 'beam', [(i + 1, i) for i in range(beams - 1)])  4.9 us
    pallas_call x2, Pallas kernels, quarters(): call(functools.partial(quarters_kernel, distances), 'quarters', [quarter_...  4.53 us
  transfers between devices with their start and end apart: 8, of which 5 were waited for; matrix products, arithmetic and copies ran while one was open for 1% of the time, Pallas kernels for 29%

profile of v1, /device:TPU:97, one launch (start us, length us, event | category | flops | bytes accessed | tf_op | source)
XLA Modules:
  0.0 92.7 jit_solution(4641102151484163358)
XLA Ops:
  1.4 1.1 %ends.1 = (f32[8,2048]{1,0:T(8,128)S(1)}, f32[16,2048]{1,0:T(8,128)S(1)}) custom-call(f32[2,2,128]{2,1,0:T(2,128)S(1)} %copy-done.3, s32[2,2,8]{2,1,0:T(2,128)S(1)} %copy-done.1, f32[2,128,2048]{2,1,0:T(8,128)} %bitcast.30), custom_call_target="tpu_custom_call" | custom-call | flops 1000000 | bytes 1048576 | tf_op jit(solution)/shard_map/ends/pallas_call | solution.py:381
  2.5 5.3 %collective-permute-start = (f32[8,2048]{1,0:T(8,128)S(1)}, f32[8,2048]{1,0:T(8,128)S(1)}, u32[]{:S(2)}, u32[]{:S(2)}) collective-permute-start(f32[8,2048]{1,0:T(8,128)S(1)} %get-tuple-element.23), channel_id=1, source_target_pairs={{0,1},{1,2},{2,3},{3,4},{4,5},{5,6},{6,7},{7,8},{8,9},{9,10},{10,1... | collective-permute-start | bytes 196616 | tf_op jit(solution)/shard_map/ppermute | solution.py:387
  7.8 1.9 %collective-permute-start.1 = (f32[16,2048]{1,0:T(8,128)S(1)}, f32[16,2048]{1,0:T(8,128)S(1)}, u32[]{:S(2)}, u32[]{:S(2)}) collective-permute-start(f32[16,2048]{1,0:T(8,128)S(1)} %get-tuple-element.24), channel_id=1, source_target_pairs={{1,0},{2,1},{3,2},{4,3},{5,4},{6,5},{7,6},{8,7},{9,8},{10,9},{11,1... | collective-permute-start | bytes 393224 | tf_op jit(solution)/shard_map/ppermute | solution.py:388
  10.4 4.9 %collective-permute-done.1.after = f32[16,2048]{1,0:T(8,128)S(1)} collective-permute-done((f32[16,2048]{1,0:T(8,128)S(1)}, f32[16,2048]{1,0:T(8,128)S(1)}, u32[]{:S(2)}, u32[]{:S(2)}) %collective-permute-start.1) | collective-permute-done | bytes 131104 | tf_op jit(solution)/shard_map/ppermute | solution.py:388
  16.1 1.1 %multiply_cosine_fusion = (f32[1,2,72,512]{3,2,1,0:T(8,128)S(1)}, f32[1,2,72,512]{3,2,1,0:T(8,128)S(1)}) fusion(f32[512]{0:T(512)S(1)} %iota_multiply_fusion.1, f32[2,72]{1,0:T(2,128)S(1)} %pad_maximum_fusion.3), kind=kLoop, calls=%fused_computation.3 | loop fusion | flops 73728 | bytes 592448 | tf_op jit(solution)/shard_map/cos | solution.py:419
  17.2 2.3 %quarters.3 = (f32[2,40,2048]{2,1,0:T(8,128)S(1)}, f32[2,40,2048]{2,1,0:T(8,128)S(1)}) custom-call(s32[5]{0:T(128)S(1)} %stack.50.where, f32[2,128,2048]{2,1,0:T(8,128)} %bitcast.31, f32[8,2048]{1,0:T(8,128)S(1)} %collective-permute-done.before, f32[16,2048]{1,0:T(8,128)S(1)} %collective-permute-done.1.after), custom_call_target="tpu_custom_call" | custom-call | flops 1000000 | bytes 3145728 | tf_op jit(solution)/shard_map/quarters/pallas_call | solution.py:392
  19.5 1.4 %collective-permute-start.2 = (f32[2,40,2048]{2,1,0:T(8,128)S(1)}, f32[2,40,2048]{2,1,0:T(8,128)S(1)}, u32[]{:S(2)}, u32[]{:S(2)}) collective-permute-start(f32[2,40,2048]{2,1,0:T(8,128)S(1)} %get-tuple-element.28), channel_id=1, source_target_pairs={{0,16},{16,0},{32,48},{48,32},{64,80},{80,64},{96,112},{112,96},{1... | collective-permute-start | bytes 1966088 | tf_op jit(solution)/shard_map/ppermute | solution.py:33
  20.9 1.9 %collective-permute-start.3 = (f32[2,40,2048]{2,1,0:T(8,128)S(1)}, f32[2,40,2048]{2,1,0:T(8,128)S(1)}, u32[]{:S(2)}, u32[]{:S(2)}) collective-permute-start(f32[2,40,2048]{2,1,0:T(8,128)S(1)} %get-tuple-element.30), channel_id=1, source_target_pairs={{0,48},{16,32},{32,16},{48,0},{64,112},{80,96},{96,80},{112,64},{1... | collective-permute-start | bytes 1966088 | tf_op jit(solution)/shard_map/ppermute | solution.py:33
  23.2 2.3 %quarters.2 = (f32[2,40,2048]{2,1,0:T(8,128)S(1)}, f32[2,40,2048]{2,1,0:T(8,128)S(1)}) custom-call(s32[5]{0:T(128)S(1)} %stack.50.where, f32[2,128,2048]{2,1,0:T(8,128)} %bitcast.32, f32[8,2048]{1,0:T(8,128)S(1)} %collective-permute-done.before, f32[16,2048]{1,0:T(8,128)S(1)} %collective-permute-done.1.after), custom_call_target="tpu_custom_call" | custom-call | flops 1000000 | bytes 3145728 | tf_op jit(solution)/shard_map/quarters/pallas_call | solution.py:392
  25.5 8.0 %own.1 = (f32[80,3072]{1,0:T(8,128)S(1)}, bf16[2,1536,512]{2,1,0:T(8,128)(2,1)}, bf16[2,1536,512]{2,1,0:T(8,128)(2,1)}) custom-call(f32[2,1536,512]{2,1,0:T(8,128)} %bitcast.35, f32[2,40,2048]{2,1,0:T(8,128)S(1)} %get-tuple-element.25.q0), custom_call_target="tpu_custom_call" | custom-call | flops 5000000000 | bytes 14680064 | tf_op jit(solution)/shard_map/own/pallas_call | solution.py:428
  33.6 0.9 %copy-done.6 = f32[80,3072]{1,0:T(8,128)} copy-done((f32[80,3072]{1,0:T(8,128)}, f32[80,3072]{1,0:T(8,128)S(1)}, u32[]{:S(2)}) %copy-start.6) | copy-done | bytes 983064
  34.5 0.8 collective-permute-start.4
  35.3 12.7 %collective-permute-done.3.m3 = f32[2,40,2048]{2,1,0:T(8,128)S(1)} collective-permute-done((f32[2,40,2048]{2,1,0:T(8,128)S(1)}, f32[2,40,2048]{2,1,0:T(8,128)S(1)}, u32[]{:S(2)}, u32[]{:S(2)}) %collective-permute-start.3) | collective-permute-done | bytes 655392 | tf_op jit(solution)/shard_map/ppermute | solution.py:33
  48.0 0.8 copy-done.7
  48.9 12.0 %early.1 = (f32[80,3072]{1,0:T(8,128)}, f32[2,80,3072]{2,1,0:T(8,128)}) custom-call(s32[5]{0:T(128)S(1)} %stack.50.where, s32[2,2,4]{2,1,0:T(2,128)S(1)} %add_clamp_fusion.offsets, f32[2,2,2,4]{3,2,1,0:T(2,128)S(1)} %copy-done.5, f32[80,3072]{1,0:T(8,128)} %copy-done.6, f32[2,40,2048]{2,1,0:T(8,128)S(1)} %collective-permute-done.2.m1, ...), custom_call_target="tpu_custom_call" | custom-call | flops 10000000000 | bytes 16777216 | tf_op jit(solution)/shard_map/early/pallas_call | solution.py:434
  60.9 0.8 copy-done.8
  61.7 12.6 %middle.1 = (f32[2,32,2048]{2,1,0:T(8,128)S(1)}, f32[2,128,2048]{2,1,0:T(8,128)}, f32[80,3072]{1,0:T(8,128)}) custom-call(s32[5]{0:T(128)S(1)} %stack.50.where, s32[2,2,4]{2,1,0:T(2,128)S(1)} %add_clamp_fusion.offsets, f32[2,2,2,4]{3,2,1,0:T(2,128)S(1)} %copy-done.5, f32[2,40,2048]{2,1,0:T(8,128)} %copy-done.8, f32[80,3072]{1,0:T(8,128)} %get-tuple-element.35.full1_in, ...), custom_call_target="tpu_custom_call" | custom-call | flops 8999999488 | bytes 10485760 | tf_op jit(solution)/shard_map/middle/pallas_call | solution.py:441
  74.4 3.6 %late.1 = (f32[2,32,2048]{2,1,0:T(8,128)S(1)}, f32[2,32,2048]{2,1,0:T(8,128)S(1)}) custom-call(s32[5]{0:T(128)S(1)} %stack.50.where, s32[2,2,4]{2,1,0:T(2,128)S(1)} %add_clamp_fusion.offsets, f32[2,2,2,4]{3,2,1,0:T(2,128)S(1)} %copy-done.5, f32[2,80,3072]{2,1,0:T(8,128)} %get-tuple-element.33.full2_in, f32[80,3072]{1,0:T(8,128)} %get-tuple-element.36.full_b, ...), custom_call_target="tpu_custom_call" | custom-call | flops 4000000000 | bytes 4194304 | tf_op jit(solution)/shard_map/late/pallas_call | solution.py:451
  78.0 3.8 %collective-permute-start.5 = (f32[2,32,2048]{2,1,0:T(8,128)S(1)}, f32[2,32,2048]{2,1,0:T(8,128)S(1)}, u32[]{:S(2)}, u32[]{:S(2)}) collective-permute-start(f32[2,32,2048]{2,1,0:T(8,128)S(1)} %get-tuple-element.37), channel_id=1, source_target_pairs={{0,16},{16,0},{32,48},{48,32},{64,80},{80,64},{96,112},{112,96},{1... | collective-permute-start | bytes 1572872 | tf_op jit(solution)/shard_map/ppermute | solution.py:33
  81.8 2.2 %collective-permute-done.7.refs_0_ = f32[2,32,2048]{2,1,0:T(8,128)S(1)} collective-permute-done((f32[2,32,2048]{2,1,0:T(8,128)S(1)}, f32[2,32,2048]{2,1,0:T(8,128)S(1)}, u32[]{:S(2)}, u32[]{:S(2)}) %collective-permute-start.7) | collective-permute-done | bytes 524320 | tf_op jit(solution)/shard_map/ppermute | solution.py:33
  83.9 1.3 %place.2.refs_2_ = f32[2,128,2048]{2,1,0:T(8,128)} custom-call(s32[5]{0:T(128)S(1)} %stack.50.where, f32[2,32,2048]{2,1,0:T(8,128)S(1)} %collective-permute-done.7.refs_0_, f32[2,128,2048]{2,1,0:T(8,128)} %get-tuple-element.40.refs_1_), custom_call_target="tpu_custom_call", output_to_operand_aliasing={{}: (2, {})} | custom-call | flops 99999997952 | bytes 2097152 | tf_op jit(solution)/shard_map/place/pallas_call | solution.py:460
  85.3 5.0 %collective-permute-done.5.refs_0_ = f32[2,32,2048]{2,1,0:T(8,128)S(1)} collective-permute-done((f32[2,32,2048]{2,1,0:T(8,128)S(1)}, f32[2,32,2048]{2,1,0:T(8,128)S(1)}, u32[]{:S(2)}, u32[]{:S(2)}) %collective-permute-start.5) | collective-permute-done | bytes 524320 | tf_op jit(solution)/shard_map/ppermute | solution.py:33
  90.3 0.7 collective-permute-done.6.refs_1_
  91.0 1.5 %place.3 = f32[2,128,2048]{2,1,0:T(8,128)} custom-call(s32[5]{0:T(128)S(1)} %stack.50.where, f32[2,32,2048]{2,1,0:T(8,128)S(1)} %collective-permute-done.5.refs_0_, f32[2,32,2048]{2,1,0:T(8,128)S(1)} %collective-permute-done.6.refs_1_, f32[2,128,2048]{2,1,0:T(8,128)} %place.2.refs_2_), custom_call_target="tpu_custom_call", output_to_operand_aliasing={{}: (3, {})} | custom-call | flops 100000 | bytes 2097152 | tf_op jit(solution)/shard_map/place/pallas_call | solution.py:460
  (49 shorter events, 3.3 us)
Async XLA Ops:
  0.0 0.7 copy-start.1
  0.7 0.7 copy-start.3
  1.4 8.4 %copy-start.2 = (s32[2,2,8]{2,1,0:T(2,128)S(1)}, s32[2,2,8]{2,1,0:T(2,128)}, u32[]{:S(2)}) copy-start(s32[2,2,8]{2,1,0:T(2,128)} %offs_in.1) | copy-start | bytes 388
  1.4 8.4 %copy-start.4 = (f32[2,2,128]{2,1,0:T(2,128)S(1)}, f32[2,2,128]{2,1,0:T(2,128)}, u32[]{:S(2)}) copy-start(f32[2,2,128]{2,1,0:T(2,128)} %rates_in.1) | copy-start | bytes 6148
  2.5 7.7 %collective-permute-start = (f32[8,2048]{1,0:T(8,128)S(1)}, f32[8,2048]{1,0:T(8,128)S(1)}, u32[]{:S(2)}, u32[]{:S(2)}) collective-permute-start(f32[8,2048]{1,0:T(8,128)S(1)} %get-tuple-element.23), channel_id=1, source_target_pairs={{0,1},{1,2},{2,3},{3,4},{4,5},{5,6},{6,7},{7,8},{8,9},{9,10},{10,1... | collective-permute-start | bytes 196616 | tf_op jit(solution)/shard_map/ppermute | solution.py:387
  7.8 7.5 %collective-permute-start.1 = (f32[16,2048]{1,0:T(8,128)S(1)}, f32[16,2048]{1,0:T(8,128)S(1)}, u32[]{:S(2)}, u32[]{:S(2)}) collective-permute-start(f32[16,2048]{1,0:T(8,128)S(1)} %get-tuple-element.24), channel_id=1, source_target_pairs={{1,0},{2,1},{3,2},{4,3},{5,4},{6,5},{7,6},{8,7},{9,8},{10,9},{11,1... | collective-permute-start | bytes 393224 | tf_op jit(solution)/shard_map/ppermute | solution.py:388
  19.5 15.0 %collective-permute-start.2 = (f32[2,40,2048]{2,1,0:T(8,128)S(1)}, f32[2,40,2048]{2,1,0:T(8,128)S(1)}, u32[]{:S(2)}, u32[]{:S(2)}) collective-permute-start(f32[2,40,2048]{2,1,0:T(8,128)S(1)} %get-tuple-element.28), channel_id=1, source_target_pairs={{0,16},{16,0},{32,48},{48,32},{64,80},{80,64},{96,112},{112,96},{1... | collective-permute-start | bytes 1966088 | tf_op jit(solution)/shard_map/ppermute | solution.py:33
  20.9 27.2 %collective-permute-start.3 = (f32[2,40,2048]{2,1,0:T(8,128)S(1)}, f32[2,40,2048]{2,1,0:T(8,128)S(1)}, u32[]{:S(2)}, u32[]{:S(2)}) collective-permute-start(f32[2,40,2048]{2,1,0:T(8,128)S(1)} %get-tuple-element.30), channel_id=1, source_target_pairs={{0,48},{16,32},{32,16},{48,0},{64,112},{80,96},{96,80},{112,64},{1... | collective-permute-start | bytes 1966088 | tf_op jit(solution)/shard_map/ppermute | solution.py:33
  23.2 37.7 %copy-start = (f32[2,4,2,72,128]{4,3,2,1,0:T(8,128)}, f32[2,4,2,72,128]{4,3,2,1,0:T(8,128)S(1)}, u32[]{:S(2)}) copy-start(f32[2,4,2,72,128]{4,3,2,1,0:T(8,128)S(1)} %pad_maximum_fusion.1.across) | copy-start | bytes 1769476
  25.5 23.4 %copy-start.5 = (f32[2,2,2,4]{3,2,1,0:T(2,128)S(1)}, f32[2,2,2,4]{3,2,1,0:T(2,128)}, u32[]{:S(2)}) copy-start(f32[2,2,2,4]{3,2,1,0:T(2,128)} %w_ref.5) | copy-start | bytes 388
  33.5 0.9 %copy-start.6 = (f32[80,3072]{1,0:T(8,128)}, f32[80,3072]{1,0:T(8,128)S(1)}, u32[]{:S(2)}) copy-start(f32[80,3072]{1,0:T(8,128)S(1)} %get-tuple-element.26.full1_in) | copy-start | bytes 2949124
  34.5 26.4 %collective-permute-start.4 = (f32[2,40,2048]{2,1,0:T(8,128)S(1)}, f32[2,40,2048]{2,1,0:T(8,128)S(1)}, u32[]{:S(2)}, u32[]{:S(2)}) collective-permute-start(f32[2,40,2048]{2,1,0:T(8,128)S(1)} %get-tuple-element.34), channel_id=1, source_target_pairs={{0,32},{16,48},{32,0},{48,16},{64,96},{80,112},{96,64},{112,80},{1... | collective-permute-start | bytes 1966088 | tf_op jit(solution)/shard_map/ppermute | solution.py:33
  48.0 0.8 copy-start.7
  60.9 0.9 copy-start.8
  74.3 9.6 %collective-permute-start.7 = (f32[2,32,2048]{2,1,0:T(8,128)S(1)}, f32[2,32,2048]{2,1,0:T(8,128)S(1)}, u32[]{:S(2)}, u32[]{:S(2)}) collective-permute-start(f32[2,32,2048]{2,1,0:T(8,128)S(1)} %get-tuple-element.39), channel_id=1, source_target_pairs={{0,32},{16,48},{32,0},{48,16},{64,96},{80,112},{96,64},{112,80},{1... | collective-permute-start | bytes 1572872 | tf_op jit(solution)/shard_map/ppermute | solution.py:33
  78.0 12.3 %collective-permute-start.5 = (f32[2,32,2048]{2,1,0:T(8,128)S(1)}, f32[2,32,2048]{2,1,0:T(8,128)S(1)}, u32[]{:S(2)}, u32[]{:S(2)}) collective-permute-start(f32[2,32,2048]{2,1,0:T(8,128)S(1)} %get-tuple-element.37), channel_id=1, source_target_pairs={{0,16},{16,0},{32,48},{48,32},{64,80},{80,64},{96,112},{112,96},{1... | collective-permute-start | bytes 1572872 | tf_op jit(solution)/shard_map/ppermute | solution.py:33
  81.8 9.2 %collective-permute-start.6 = (f32[2,32,2048]{2,1,0:T(8,128)S(1)}, f32[2,32,2048]{2,1,0:T(8,128)S(1)}, u32[]{:S(2)}, u32[]{:S(2)}) collective-permute-start(f32[2,32,2048]{2,1,0:T(8,128)S(1)} %get-tuple-element.38), channel_id=1, source_target_pairs={{0,48},{16,32},{32,16},{48,0},{64,112},{80,96},{96,80},{112,64},{1... | collective-permute-start | bytes 1572872 | tf_op jit(solution)/shard_map/ppermute | solution.py:33

commit v2 on v1

v2 whole, which is shorter than its diff:
```python
import functools

import jax
import jax.numpy as jnp
from jax import lax
from jax.experimental import pallas as pl
from jax.experimental.pallas import tpu as pltpu
from jax.sharding import PartitionSpec as P

TILE = 512
TAPS = 3
BLK = 16
RING = 4
QROWS = 32
EDGE = 8
ROWS = QROWS + EDGE
WIDTH = 2048
TILES = WIDTH // TILE
FULL = WIDTH + 2 * TILE
LANES = 512
SPANS = ((0, 16), (16, 32), (32, 40))
HBM = pl.BlockSpec(memory_space=pltpu.HBM)
VMEM = pl.BlockSpec(memory_space=pltpu.VMEM)
SMEM = pl.BlockSpec(memory_space=pltpu.SMEM)
IMAGE = pltpu.VMEM((2 * ROWS, WIDTH), jnp.float32)
PHASE_ROWS = ROWS + QROWS
PHASES = ((2, 2, PHASE_ROWS, TILE), (2, TILES, 2, PHASE_ROWS, 128))
MATRIX = pltpu.VMEM((TAPS * TILE, TILE), jnp.bfloat16)


def exchange(value, distance):
    count = lax.axis_size("grp")
    return lax.ppermute(value, "grp", [(i, i ^ distance) for i in range(count)])


def split(value):
    high = value.astype(jnp.bfloat16)
    low = (value - high.astype(jnp.float32)).astype(jnp.bfloat16)
    return high, low


def fetch(sems, pairs):
    copies = [pltpu.make_async_copy(a, b, sems.at[i]) for i, (a, b) in enumerate(pairs)]
    for copy in copies:
        copy.start()
    return copies


def range_products(high, low, t_high, t_low, full, count):
    rows = count * 2 * ROWS
    dot = functools.partial(jnp.dot, preferred_element_type=jnp.float32)
    full[:count, :, 5 * TILE :] = jnp.zeros((count, 2 * ROWS, TILE), jnp.float32)
    if count == 1:
        parts = [
            [part[0, :, m * TILE : (m + 1) * TILE] for m in range(TILES)] for part in (high, low)
        ]
        for t in range(TAPS):
            uses = [m for m in range(TILES) if m - t >= -1]
            n = len(uses) * rows
            a_high, a_low = ([part[m] for m in uses] for part in parts)
            at = slice(t * TILE, (t + 1) * TILE)
            both = dot(jnp.concatenate(a_high + a_low, 0), t_high[at, :])
            summed = both[:n] + both[n:] + dot(jnp.concatenate(a_high, 0), t_low[at, :])
            for i, m in enumerate(uses):
                to = slice((m - t + 1) * TILE, (m - t + 2) * TILE)
                value = summed[i * rows : (i + 1) * rows]
                full[0, :, to] = value if t == 0 or m == 0 else full[0, :, to] + value
        return
    for index in range(5):
        first = index - 1
        taps = [t for t in range(TAPS) if 0 <= first + t < TILES]
        k0, k1 = taps[0] * TILE, (taps[-1] + 1) * TILE
        a0, a1 = k0 + first * TILE, k1 + first * TILE
        a_high = high[:count, :, a0:a1].reshape(rows, a1 - a0)
        a_low = low[:count, :, a0:a1].reshape(rows, a1 - a0)
        summed = dot(a_high, t_high[k0:k1, :]) + (
            dot(a_high, t_low[k0:k1, :]) + dot(a_low, t_high[k0:k1, :])
        )
        full[:count, :, index * TILE : (index + 1) * TILE] = summed.reshape(count, 2 * ROWS, TILE)


def shifted(tiles):
    rows = tiles.shape[0]
    return [
        (tiles if k == 1 else pltpu.roll(tiles, (1 - k) % rows, 0))[8 : rows - 8] for k in range(4)
    ]


def unit(phases, e, row, count, lane):
    within, across = phases
    at = pl.ds(pl.multiple_of(lane % TILE, 128), LANES)
    n = lane // TILE
    c, s = (within[i, e, row : row + count, at] for i in range(2))
    cn, sn = (
        jnp.concatenate([across[i, n, e, row : row + count, :]] * (LANES // 128), 1)
        for i in range(2)
    )
    return c * cn - s * sn, s * cn + c * sn


def merge(section, block, lane, fulls, children, halves, offsets, w_ref, phases):
    r0, r1 = SPANS[block]
    out = [[None, None] for _ in halves]
    for full, e in zip(fulls, children):

        def rows_at(offset, row, count):
            start = pl.multiple_of(offset * TILE + lane, 128)
            return full[row : row + count, pl.ds(start, LANES)]

        parts = []
        for base in (0, ROWS):
            if block == 0:
                o = offsets[section, e, 0]
                tiles = [rows_at(o, base + 32, 8), rows_at(o, base, 24)]
            elif block == 1:
                tiles = [rows_at(offsets[section, e, 1], base + 8, 32)]
            else:
                after, before = offsets[section, e, 2], offsets[section, e, 3]
                row = lax.broadcasted_iota(jnp.int32, (EDGE, LANES), 0)
                middle = jnp.where(
                    row < 4, rows_at(after, base + 32, 8), rows_at(before, base + 32, 8)
                )
                tiles = [rows_at(after, base + 24, 8), middle, rows_at(before, base, 8)]
            parts.append(shifted(jnp.concatenate(tiles, 0) if len(tiles) > 1 else tiles[0]))
        cosine, sine = unit(phases, e, section * ROWS + r0, r1 - r0, lane)
        for i, h in enumerate(halves):
            w = [w_ref[section, h, e, k] for k in range(4)]
            real, imag = (
                (w[0] * part[0] + w[1] * part[1]) + (w[2] * part[2] + w[3] * part[3])
                for part in parts
            )
            new = (real * cosine - imag * sine, real * sine + imag * cosine)
            out[i] = [n if o is None else o + n for o, n in zip(out[i], new)]
    return out


def first_merges(fulls, children, halves, where, offsets, w_ref, phases, high, low):
    @pl.loop(0, WIDTH, step=LANES)
    def _(lane):
        at = pl.ds(pl.multiple_of(lane, 128), LANES)
        blocks = [
            merge(0, b, lane, fulls, children, halves, offsets, w_ref, phases)
            for b in range(3)
        ]
        row = lax.broadcasted_iota(jnp.int32, (EDGE, LANES), 0)
        keep = jnp.where(row < 4, where[3], where[2]) > 0
        for i in range(len(halves)):
            merged = jnp.concatenate(
                [
                    jnp.where(keep, blocks[b][i][comp], 0.0) if b == 2 else blocks[b][i][comp]
                    for comp in range(2)
                    for b in range(3)
                ],
                0,
            )
            high[i, :, at], low[i, :, at] = split(merged)


def second_merges(fulls, children, halves, offsets, w_ref, phases, outs):
    @pl.loop(0, WIDTH, step=LANES)
    def _(lane):
        at = pl.ds(pl.multiple_of(lane, 128), LANES)
        for b in range(2):
            r0, r1 = SPANS[b]
            merged = merge(1, b, lane, fulls, children, halves, offsets, w_ref, phases)
            for i in range(len(halves)):
                for comp in range(2):
                    outs[i][comp, r0:r1, at] = merged[i][comp]


def pack_kernel(
    rates_in, offs_in, where, image, q1, q3, tail, head, edges, rates, offs, sems
):
    copies = fetch(
        sems,
        [
            (image.at[:, 0:8], edges.at[0]), (image.at[:, 120:128], edges.at[1]),
            (rates_in.at[0], rates), (offs_in.at[0], offs),
        ]
        + [
            (image.at[:, pl.ds(pl.multiple_of((where[4] ^ d) * QROWS, QROWS), QROWS)], out)
            for d, out in ((1, q1), (3, q3))
        ],
    )
    lane = lax.broadcasted_iota(jnp.int32, (1, WIDTH), 1)

    def line(*values):
        out = jnp.zeros((1, WIDTH), jnp.float32)
        for i, value in enumerate(values):
            out = jnp.where(lane == i, value, out)
        return out

    for copy in copies[:4]:
        copy.wait()

    def offset(e, block):
        return offs[e, block].astype(jnp.float32)

    tail[0:2] = edges[1, 0, 6:8]
    tail[2:4] = edges[1, 1, 6:8]
    tail[4:5] = line(rates[0, 127], rates[1, 127], offset(0, 7), offset(1, 7))
    tail[5:8] = jnp.zeros((3, WIDTH), jnp.float32)
    head[0:4] = edges[0, 0, 0:4]
    head[4:8] = edges[0, 1, 0:4]
    head[8:9] = line(rates[0, 0], rates[0, 1], rates[1, 0], rates[1, 1], offset(0, 0), offset(1, 0))
    head[9:16] = jnp.zeros((7, WIDTH), jnp.float32)
    for copy in copies[4:]:
        copy.wait()


def rims_kernel(where, image, before, after, e0, p1, p3, stage, rows, sems):
    copies = []
    for d in range(RING):
        q = where[4] ^ d
        trail = pl.multiple_of(jnp.minimum(q * QROWS + QROWS, 120), 8)
        lead = pl.multiple_of(jnp.maximum(q * QROWS - 8, 0), 8)
        copies.append((image.at[:, pl.ds(trail, 8)], rows.at[d, 0]))
        copies.append((image.at[:, pl.ds(lead, 8)], rows.at[d, 1]))
    part = pl.ds(pl.multiple_of((where[4] ^ 2) * QROWS, QROWS), QROWS)
    copies = fetch(sems, copies + [(image.at[:, part], stage.at[:, :QROWS])])
    for copy in copies:
        copy.wait()
    for d, (out, r) in enumerate(((e0, 0), (p1, 0), (stage, QROWS), (p3, 0))):
        q = where[4] ^ d
        for comp in range(2):
            out[comp, r : r + 4] = jnp.where(
                q == 3, after[4 * comp : 4 * comp + 4], rows[d, 0, comp, 0:4]
            )
            out[comp, r + 4 : r + 6] = jnp.zeros((2, WIDTH), jnp.float32)
            out[comp, r + 6 : r + 8] = jnp.where(
                q == 0, before[2 * comp : 2 * comp + 2], rows[d, 1, comp, 6:8]
            )


def split_tiles(values, high, low):
    @pl.loop(0, TAPS * TILE, step=64)
    def _(row):
        at = pl.ds(pl.multiple_of(row, 64), 64)
        high[at], low[at] = split(values[at])


def fill(image, rim, high, low):
    rows = jnp.concatenate([image[...], rim[...]], 1)
    high[...], low[...] = split(rows.reshape(2 * ROWS, WIDTH))


def own_kernel(where, tiles, image, e0, full1_0, th, tl, main, high, low, t1, sems):
    part = pl.ds(pl.multiple_of(where[4] * QROWS, QROWS), QROWS)
    copies = fetch(sems, [(tiles.at[0], t1), (image.at[:, part], main)])
    copies[1].wait()
    fill(main, e0, high.at[0], low.at[0])
    copies[0].wait()
    split_tiles(t1, th, tl)
    range_products(high, low, th, tl, full1_0, 1)


def early_kernel(
    where, offsets, w_ref, full1_0, m1, e1, m3, e3, th1, tl1, tiles, within, across,
    full1, full2, th2, tl2,
    high, low, t2, sems,
):
    copies = fetch(sems, [(tiles.at[1], t2)])
    bit = where[0]
    fill(m1, e1, high.at[0], low.at[0])
    fill(m3, e3, high.at[1], low.at[1])
    range_products(high, low, th1, tl1, full1, 2)
    first_merges(
        (full1_0.at[0], full1.at[0]), (bit, 1 - bit), (bit, 1 - bit),
        where, offsets, w_ref, (within, across), high, low,
    )
    copies[0].wait()
    split_tiles(t2, th2, tl2)
    range_products(high, low, th2, tl2, full2, 2)


def middle_kernel(
    where, offsets, w_ref, m2, full1, full2, th1, tl1, th2, tl2, within, across,
    d2, full1_2, full2_2,
    high, low,
):
    phases = (within, across)
    bit, bit2 = where[0], where[1]
    high[0], low[0] = split(m2[...].reshape(2 * ROWS, WIDTH))
    range_products(high, low, th1, tl1, full1_2, 1)
    first_merges(
        (full1_2.at[0], full1.at[1]), (bit, 1 - bit), (bit,),
        where, offsets, w_ref, phases, high, low,
    )
    range_products(high, low, th2, tl2, full2_2, 1)
    second_merges(
        (full2.at[0], full2_2.at[0]), (bit2, 1 - bit2), (1 - bit2,),
        offsets, w_ref, phases, (d2,),
    )


def late_kernel(
    where, offsets, w_ref, full1_2, full1, full2, th2, tl2, within, across,
    d1, d3,
    high, low, full2_3,
):
    phases = (within, across)
    bit, bit2 = where[0], where[1]
    first_merges(
        (full1_2.at[0], full1.at[1]), (bit, 1 - bit), (1 - bit,),
        where, offsets, w_ref, phases, high, low,
    )
    range_products(high, low, th2, tl2, full2_3, 1)
    second_merges(
        (full2.at[1], full2_3.at[0]), (bit2, 1 - bit2), (bit2, 1 - bit2),
        offsets, w_ref, phases, (d1, d3),
    )


def rest_kernel(where, offsets, w_ref, full2, full2_2, within, across, result, d0, sems):
    bit2 = where[1]
    second_merges(
        (full2.at[0], full2_2.at[0]), (bit2, 1 - bit2), (bit2,),
        offsets, w_ref, (within, across), (d0,),
    )
    at = pl.ds(pl.multiple_of(where[4] * QROWS, QROWS), QROWS)
    for copy in fetch(sems, [(d0, result.at[:, at])]):
        copy.wait()


def place_kernel(distances, where, *refs):
    pieces, (out, stages, sems, out_sems) = refs[: len(distances)], refs[-4:]
    reads, writes = [], []
    for i, d in enumerate(distances):
        for n in range(2):
            at = pl.ds(pl.multiple_of((where[4] ^ d) * QROWS + 16 * n, 16), 16)
            half = stages.at[i, :, 16 * n : 16 * n + 16]
            reads.append((pieces[i].at[:, 16 * n : 16 * n + 16], half))
            writes.append((half, out.at[:, at]))
    reads = fetch(sems, reads)
    copies = []
    for i, pair in enumerate(writes):
        reads[i].wait()
        copies += fetch(out_sems.at[i : i + 1], [pair])
    for copy in copies:
        copy.wait()


def call(kernel, name, outs, in_specs, out_specs, scratch, flops, moved, aliases=None, vmem=8):
    return pl.pallas_call(
        kernel,
        out_shape=[jax.ShapeDtypeStruct(shape, kind) for shape, kind in outs],
        in_specs=in_specs,
        out_specs=out_specs,
        scratch_shapes=scratch,
        input_output_aliases=aliases or {},
        compiler_params=pltpu.CompilerParams(vmem_limit_bytes=vmem * 2**20),
        cost_estimate=pl.CostEstimate(flops=flops, bytes_accessed=moved, transcendentals=0),
        name=name,
    )


def halves_scratch(count):
    return [pltpu.VMEM((count, 2 * ROWS, WIDTH), jnp.bfloat16)] * 2


def full_scratch(count):
    return pltpu.VMEM((count, 2 * ROWS, FULL), jnp.float32)


def per_device(subimages, beam_weights, range_tiles, tile_offsets, phase_rates):
    f32, bf16 = jnp.float32, jnp.bfloat16
    dma = pltpu.SemaphoreType.DMA
    mine = lax.axis_index("grp") & 3
    beam = lax.axis_index("beam")
    beams = lax.axis_size("beam")
    image = subimages.reshape(2, RING * QROWS, WIDTH)
    first = jnp.logical_and(beam == 0, mine == 0)
    last = jnp.logical_and(beam == beams - 1, mine == 3)
    where = jnp.stack(
        [mine & 1, mine >> 1, 1 - first.astype(jnp.int32), 1 - last.astype(jnp.int32), mine]
    ).astype(jnp.int32)
    piece_shape = ((2, QROWS, WIDTH), f32)
    quarter_shape = ((2, ROWS, WIDTH), f32)
    q1, q3, tail, head = call(
        pack_kernel, "pack", [piece_shape, piece_shape, ((8, WIDTH), f32), ((16, WIDTH), f32)],
        [HBM] * 2 + [SMEM] + [HBM], [VMEM] * 4,
        [pltpu.VMEM((2, 2, 8, WIDTH), f32), pltpu.SMEM((2, 4 * QROWS), f32)]
        + [pltpu.SMEM((2, 8), jnp.int32), dma((6,))],
        10**6, 2**20, vmem=62,
    )(phase_rates, tile_offsets, where, image)
    m1 = exchange(q1, 1)
    m3 = exchange(q3, 3)
    before = lax.ppermute(tail, "beam", [(i, i + 1) for i in range(beams - 1)])
    after = lax.ppermute(head, "beam", [(i + 1, i) for i in range(beams - 1)])
    rim_shape = ((2, EDGE, WIDTH), f32)
    e0, p1, p3, q2 = call(
        rims_kernel, "rims", [rim_shape] * 3 + [quarter_shape],
        [SMEM, HBM, VMEM, VMEM], [VMEM] * 4,
        [pltpu.VMEM((RING, 2, 2, 8, WIDTH), f32), dma((9,))],
        10**6, 3 * 2**20,
    )(where, image, before, after)
    e1 = exchange(p1, 1)
    e3 = exchange(p3, 3)
    q2, m1, e0 = lax.optimization_barrier((q2, m1, e0))
    m2 = exchange(q2, 2)

    before_values, after_values = before[4, :4].reshape(2, 2), after[8, :6]
    line = jnp.concatenate([before_values[0][:, None], phase_rates[0], after_values[:4].reshape(2, 2)], 1)
    line = lax.dynamic_slice_in_dim(line, mine * QROWS, QROWS + 3, 1)
    rates_b = lax.dynamic_slice_in_dim(phase_rates[1], mine * QROWS, QROWS, 1)
    rates = jnp.concatenate([line[:, 1:], jnp.zeros((2, 5), f32), line[:, :1], rates_b], 1)
    offs = tile_offsets[0].astype(f32)
    line = jnp.concatenate([before_values[1][:, None], offs, after_values[4:][:, None]], 1)
    line = lax.dynamic_slice_in_dim(line, mine * 2, 4, 1).astype(jnp.int32)
    offs_a = jnp.stack([line[:, 1], line[:, 2], line[:, 3], line[:, 0]], 1)
    offs_b = jnp.pad(lax.dynamic_slice_in_dim(tile_offsets[1], mine * 2, 2, 1), ((0, 0), (0, 2)))
    offsets = jnp.clip(jnp.stack([offs_a, offs_b]), 0, 2)
    angles = rates[:, :, None] * (jnp.arange(TILE, dtype=f32) / TILE)
    within = jnp.stack([jnp.cos(angles), jnp.sin(angles)])
    angles = jnp.arange(TILES, dtype=f32)[:, None, None, None] * rates[:, :, None]
    angles = jnp.broadcast_to(angles, (TILES, 2, PHASE_ROWS, 128))
    across = jnp.stack([jnp.cos(angles), jnp.sin(angles)])

    scalars = (where, offsets, beam_weights)
    full_shape = (2 * ROWS, FULL)
    one, two = ((1, *full_shape), f32), ((2, *full_shape), f32)
    matrix_shape = ((TAPS * TILE, TILE), bf16)
    matrices = range_tiles.reshape(2, TAPS * TILE, TILE)
    matrix_f32 = pltpu.VMEM((TAPS * TILE, TILE), f32)
    full1_0, t1h, t1l = call(
        own_kernel, "own", [one, matrix_shape, matrix_shape], [SMEM] + [HBM] * 2 + [VMEM],
        [VMEM] * 3, [pltpu.VMEM(*piece_shape)] + halves_scratch(1) + [matrix_f32, dma((2,))],
        30 * 10**9, 8 * 2**20, vmem=16,
    )(where, matrices, image, e0)
    full1, full2, t2h, t2l = call(
        early_kernel, "early", [two, two, matrix_shape, matrix_shape],
        [SMEM] * 3 + [VMEM] * 7 + [HBM] + [VMEM] * 2, [VMEM] * 4,
        halves_scratch(2) + [matrix_f32, dma((1,))],
        10**4, 10**4, vmem=28,
    )(*scalars, full1_0, m1, e1, m3, e3, t1h, t1l, matrices, within, across)
    d2, full1_2, full2_2 = call(
        middle_kernel, "middle", [piece_shape, one, one],
        [SMEM] * 3 + [VMEM] * 9, [VMEM] * 3, halves_scratch(1),
        9 * 10**9, 10 * 2**20, vmem=24,
    )(*scalars, m2, full1, full2, t1h, t1l, t2h, t2l, within, across)
    r2 = exchange(d2, 2)
    d1, d3 = call(
        late_kernel, "late", [piece_shape] * 2, [SMEM] * 3 + [VMEM] * 7, [VMEM] * 2,
        halves_scratch(1) + [full_scratch(1)],
        7 * 10**9, 4 * 2**20, vmem=20,
    )(*scalars, full1_2, full1, full2, t2h, t2l, within, across)
    r1 = exchange(d1, 1)
    r3 = exchange(d3, 3)
    (result,) = call(
        rest_kernel, "rest", [((2, RING * QROWS, WIDTH), f32)], [SMEM] * 3 + [VMEM] * 4, [HBM],
        [pltpu.VMEM(*piece_shape), dma((1,))],
        3 * 10**9, 3 * 2**20, vmem=12,
    )(*scalars, full2, full2_2, within, across)

    for distances, pieces, flops in (((2,), (r2,), 10**11), ((1, 3), (r1, r3), 10**5)):
        (result,) = call(
            functools.partial(place_kernel, distances), "place", [(result.shape, f32)],
            [SMEM] + [HBM] * (len(pieces) + 1), [HBM],
            [pltpu.VMEM((len(pieces), *piece_shape[0]), f32)] + [dma((2 * len(pieces),))] * 2,
            flops, 2**21, {1 + len(pieces): 0},
        )(where, *pieces, result)
    return result[:, None]


def solution(mesh):
    return jax.shard_map(
        per_device,
        mesh=mesh,
        in_specs=(
            P(None, "grp", "beam", None),
            P(),
            P(),
            P(None, None, "beam"),
            P(None, None, "beam"),
        ),
        out_specs=P(None, "grp", "beam", None),
        check_vma=False,
    )
```

time: 93 us -> 81 us (0.87)
  Pallas kernels: 44.6 us -> 32.5 us
  waiting for transfers between devices: 25.5 us -> 20.7 us
  starting transfers between devices: 15.2 us -> 19.4 us
  local copies, waits for them, and re-layouts: 5.26 us -> 6.23 us
    pallas_call x7, Pallas kernels: 41.8 us -> 29.4 us  [the longest x1 9.29 us: per_device(): call(early_kernel, 'early', [two, two, matrix_shape, matrix_shape], [SMEM...]
    ppermute x6 -> x8, starting transfers between devices: 7.98 us -> 12.1 us  [exchange(): return lax.ppermute(value, 'grp', [(i, i ^ distance) for i in range(count)])]
    ppermute x1, waiting for transfers between devices: 4.9 us -> 2.26 us  [per_device(): after = lax.ppermute(head, 'beam', [(i + 1, i) for i in range(beams - 1)])]
    ppermute x6 -> x8, waiting for transfers between devices: 20.6 us -> 18.5 us  [exchange(): return lax.ppermute(value, 'grp', [(i, i ^ distance) for i in range(count)])]
    unnamed x18 -> x16, local copies, waits for them, and re-layouts: 4 us -> 4.4 us
  transfers between devices with their start and end apart: 8 -> 10, of which waited for: 5 -> 5; matrix products, arithmetic and copies ran while one was open for 1% -> 4% of each run, Pallas kernels for 29% -> 27%
where the time goes in v2:
time: 81 us; the launch traced here: 80.8 us
  Pallas kernels  32.5 us (40%)
  waiting for transfers between devices  20.7 us (26%)
  starting transfers between devices  19.4 us (24%)
  local copies, waits for them, and re-layouts  6.23 us (8%)
  other arithmetic  1.66 us (2%)
    ppermute x8, waiting for transfers between devices, exchange(): return lax.ppermute(value, 'grp', [(i, i ^ distance) for i in range(count)])  18.5 us
    ppermute x8, starting transfers between devices, exchange(): return lax.ppermute(value, 'grp', [(i, i ^ distance) for i in range(count)])  12.1 us
    pallas_call x1, Pallas kernels, per_device(): call(early_kernel, 'early', [two, two, matrix_shape, matrix_shape], [SMEM...  9.29 us
    pallas_call x1, Pallas kernels, per_device(): call(middle_kernel, 'middle', [piece_shape, one, one], [SMEM] * 3 + [VMEM...  5.69 us
    ppermute x1, starting transfers between devices, per_device(): before = lax.ppermute(tail, 'beam', [(i, i + 1) for i in range(beams - 1)])  5.32 us
    pallas_call x1, Pallas kernels, per_device(): call(late_kernel, 'late', [piece_shape] * 2, [SMEM] * 3 + [VMEM] * 7, [VM...  4.52 us
    unnamed x16, local copies, waits for them, and re-layouts  4.4 us
    pallas_call x1, Pallas kernels, per_device(): call(pack_kernel, 'pack', [piece_shape, piece_shape, ((8, WIDTH), f32), (...  3.15 us
  transfers between devices with their start and end apart: 10, of which 5 were waited for; matrix products, arithmetic and copies ran while one was open for 4% of the time, Pallas kernels for 27%

profile of v2, /device:TPU:97, one launch (start us, length us, event | category | flops | bytes accessed | tf_op | source)
XLA Modules:
  0.0 80.8 jit_solution(6095410945380836572)
XLA Ops:
  0.7 3.2 %pack.1 = (f32[2,32,2048]{2,1,0:T(8,128)}, f32[2,32,2048]{2,1,0:T(8,128)}, f32[8,2048]{1,0:T(8,128)}, f32[16,2048]{1,0:T(8,128)}) custom-call(f32[2,2,128]{2,1,0:T(2,128)} %rates_in.1, s32[2,2,8]{2,1,0:T(2,128)} %offs_in.1, s32[5]{0:T(128)} %stack.50.where, f32[2,128,2048]{2,1,0:T(8,128)} %bitcast.30), custom_call_target="tpu_custom_call" | custom-call | flops 1000000 | bytes 1048576 | tf_op jit(solution)/shard_map/pack/pallas_call | solution.py:379
  3.8 5.3 %collective-permute-start = (f32[8,2048]{1,0:T(8,128)}, f32[8,2048]{1,0:T(8,128)S(1)}, u32[]{:S(2)}, u32[]{:S(2)}) collective-permute-start(f32[8,2048]{1,0:T(8,128)} %get-tuple-element.28), channel_id=1, source_target_pairs={{0,1},{1,2},{2,3},{3,4},{4,5},{5,6},{6,7},{7,8},{8,9},{9,10},{10,1... | collective-permute-start | bytes 196616 | tf_op jit(solution)/shard_map/ppermute | solution.py:388
  9.2 1.9 %collective-permute-start.1 = (f32[16,2048]{1,0:T(8,128)}, f32[16,2048]{1,0:T(8,128)S(1)}, u32[]{:S(2)}, u32[]{:S(2)}) collective-permute-start(f32[16,2048]{1,0:T(8,128)} %get-tuple-element.29), channel_id=1, source_target_pairs={{1,0},{2,1},{3,2},{4,3},{5,4},{6,5},{7,6},{8,7},{9,8},{10,9},{11,1... | collective-permute-start | bytes 393224 | tf_op jit(solution)/shard_map/ppermute | solution.py:389
  11.1 1.4 %collective-permute-start.2 = (f32[2,32,2048]{2,1,0:T(8,128)}, f32[2,32,2048]{2,1,0:T(8,128)S(1)}, u32[]{:S(2)}, u32[]{:S(2)}) collective-permute-start(f32[2,32,2048]{2,1,0:T(8,128)} %get-tuple-element.31), channel_id=1, source_target_pairs={{0,16},{16,0},{32,48},{48,32},{64,80},{80,64},{96,112},{112,96},{1... | collective-permute-start | bytes 1572872 | tf_op jit(solution)/shard_map/ppermute | solution.py:33
  12.5 1.9 %collective-permute-start.5 = (f32[2,32,2048]{2,1,0:T(8,128)}, f32[2,32,2048]{2,1,0:T(8,128)S(1)}, u32[]{:S(2)}, u32[]{:S(2)}) collective-permute-start(f32[2,32,2048]{2,1,0:T(8,128)} %get-tuple-element.38), channel_id=1, source_target_pairs={{0,48},{16,32},{32,16},{48,0},{64,112},{80,96},{96,80},{112,64},{1... | collective-permute-start | bytes 1572872 | tf_op jit(solution)/shard_map/ppermute | solution.py:33
  14.9 2.3 %collective-permute-done.1.after = f32[16,2048]{1,0:T(8,128)S(1)} collective-permute-done((f32[16,2048]{1,0:T(8,128)}, f32[16,2048]{1,0:T(8,128)S(1)}, u32[]{:S(2)}, u32[]{:S(2)}) %collective-permute-start.1) | collective-permute-done | bytes 131104 | tf_op jit(solution)/shard_map/ppermute | solution.py:389
  18.0 1.6 %copy-done = f32[2,1,128,2048]{3,2,1,0:T(8,128)S(1)} copy-done((f32[2,1,128,2048]{3,2,1,0:T(8,128)S(1)}, f32[2,1,128,2048]{3,2,1,0:T(8,128)}, u32[]{:S(2)}) %copy-start) | copy-done | bytes 2097176
  19.6 1.5 %rims.1 = (f32[2,8,2048]{2,1,0:T(8,128)S(1)}, f32[2,8,2048]{2,1,0:T(8,128)S(1)}, f32[2,8,2048]{2,1,0:T(8,128)S(1)}, f32[2,40,2048]{2,1,0:T(8,128)S(1)}) custom-call(s32[5]{0:T(128)S(1)} %copy-done.4, f32[2,128,2048]{2,1,0:T(8,128)S(1)} %bitcast.31, f32[8,2048]{1,0:T(8,128)S(1)} %collective-permute-done.before, f32[16,2048]{1,0:T(8,128)S(1)} %collective-permute-done.1.after), custom_call_target="tpu_custom_call" | custom-call | flops 1000000 | bytes 3145728 | tf_op jit(solution)/shard_map/rims/pallas_call | solution.py:391
  22.2 1.9 %collective-permute-start.6 = (f32[2,8,2048]{2,1,0:T(8,128)S(1)}, f32[2,8,2048]{2,1,0:T(8,128)S(1)}, u32[]{:S(2)}, u32[]{:S(2)}) collective-permute-start(f32[2,8,2048]{2,1,0:T(8,128)S(1)} %get-tuple-element.39), channel_id=1, source_target_pairs={{0,48},{16,32},{32,16},{48,0},{64,112},{80,96},{96,80},{112,64},{1... | collective-permute-start | bytes 393224 | tf_op jit(solution)/shard_map/ppermute | solution.py:33
  24.5 1.1 %multiply_cosine_fusion = (f32[1,2,72,512]{3,2,1,0:T(8,128)S(1)}, f32[1,2,72,512]{3,2,1,0:T(8,128)S(1)}) fusion(f32[512]{0:T(512)S(1)} %iota_multiply_fusion.1, f32[2,72]{1,0:T(2,128)S(1)} %pad_maximum_fusion.3), kind=kLoop, calls=%fused_computation.3 | loop fusion | flops 73728 | bytes 592448 | tf_op jit(solution)/shard_map/cos | solution.py:414
  25.7 2.5 %collective-permute-start.3 = (f32[2,40,2048]{2,1,0:T(8,128)S(1)}, f32[2,40,2048]{2,1,0:T(8,128)S(1)}, u32[]{:S(2)}, u32[]{:S(2)}) collective-permute-start(f32[2,40,2048]{2,1,0:T(8,128)S(1)} %get-tuple-element.33), channel_id=1, source_target_pairs={{0,32},{16,48},{32,0},{48,16},{64,96},{80,112},{96,64},{112,80},{1... | collective-permute-start | bytes 1966088 | tf_op jit(solution)/shard_map/ppermute | solution.py:33
  28.2 2.8 %copy-done.2 = f32[2,3,512,512]{3,2,1,0:T(8,128)S(1)} copy-done((f32[2,3,512,512]{3,2,1,0:T(8,128)S(1)}, f32[2,3,512,512]{3,2,1,0:T(8,128)}, u32[]{:S(2)}) %copy-start.2) | copy-done | bytes 6291480
  31.0 3.0 %own.1 = (f32[1,80,3072]{2,1,0:T(8,128)S(1)}, bf16[1536,512]{1,0:T(8,128)(2,1)S(1)}, bf16[1536,512]{1,0:T(8,128)(2,1)S(1)}) custom-call(s32[5]{0:T(128)S(1)} %copy-done.4, f32[2,1536,512]{2,1,0:T(8,128)S(1)} %bitcast.33, f32[2,128,2048]{2,1,0:T(8,128)S(1)} %bitcast.32, f32[2,8,2048]{2,1,0:T(8,128)S(1)} %get-tuple-element.34.e0), custom_call_target="tpu_custom_call" | custom-call | flops 30000001024 | bytes 8388608 | tf_op jit(solution)/shard_map/own/pallas_call | solution.py:425
  33.9 10.2 %collective-permute-done.6.e3 = f32[2,8,2048]{2,1,0:T(8,128)S(1)} collective-permute-done((f32[2,8,2048]{2,1,0:T(8,128)S(1)}, f32[2,8,2048]{2,1,0:T(8,128)S(1)}, u32[]{:S(2)}, u32[]{:S(2)}) %collective-permute-start.6) | collective-permute-done | bytes 131104 | tf_op jit(solution)/shard_map/ppermute | solution.py:33
  44.1 9.3 %early.1 = (f32[2,80,3072]{2,1,0:T(8,128)S(1)}, f32[2,80,3072]{2,1,0:T(8,128)S(1)}, bf16[1536,512]{1,0:T(8,128)(2,1)S(1)}, bf16[1536,512]{1,0:T(8,128)(2,1)S(1)}) custom-call(s32[5]{0:T(128)S(1)} %copy-done.4, s32[2,2,4]{2,1,0:T(2,128)S(1)} %add_clamp_fusion.offsets, f32[2,2,2,4]{3,2,1,0:T(2,128)S(1)} %copy-done.5, ...), custom_call_target="tpu_custom_call" | custom-call | flops 10000 | bytes 10000 | tf_op jit(solution)/shard_map/early/pallas_call | solution.py:430
  53.4 5.7 %middle.1 = (f32[2,32,2048]{2,1,0:T(8,128)S(1)}, f32[1,80,3072]{2,1,0:T(8,128)S(1)}, f32[1,80,3072]{2,1,0:T(8,128)S(1)}) custom-call(s32[5]{0:T(128)S(1)} %copy-done.4, s32[2,2,4]{2,1,0:T(2,128)S(1)} %add_clamp_fusion.offsets, f32[2,2,2,4]{3,2,1,0:T(2,128)S(1)} %copy-done.5, f32[2,40,2048]{2,1,0:T(8,128)S(1)} %collective-permute-done.3.m2, ...), custom_call_target="tpu_custom_call" | custom-call | flops 8999999488 | bytes 10485760 | tf_op jit(solution)/shard_map/middle/pallas_call | solution.py:436
  59.2 4.5 %late.1 = (f32[2,32,2048]{2,1,0:T(8,128)S(1)}, f32[2,32,2048]{2,1,0:T(8,128)S(1)}) custom-call(s32[5]{0:T(128)S(1)} %copy-done.4, s32[2,2,4]{2,1,0:T(2,128)S(1)} %add_clamp_fusion.offsets, f32[2,2,2,4]{3,2,1,0:T(2,128)S(1)} %copy-done.5, f32[1,80,3072]{2,1,0:T(8,128)S(1)} %get-tuple-element.46.full1_2, f32[2,80,3072]{2,1,0:T(8,128)S(1)} %get-tuple-element.42.full1, ...), custom_call_target="tpu_custom_call" | custom-call | flops 7000000000 | bytes 4194304 | tf_op jit(solution)/shard_map/late/pallas_call | solution.py:442
  63.8 2.6 %collective-permute-start.7 = (f32[2,32,2048]{2,1,0:T(8,128)S(1)}, f32[2,32,2048]{2,1,0:T(8,128)S(1)}, u32[]{:S(2)}, u32[]{:S(2)}) collective-permute-start(f32[2,32,2048]{2,1,0:T(8,128)S(1)} %get-tuple-element.47), channel_id=1, source_target_pairs={{0,16},{16,0},{32,48},{48,32},{64,80},{80,64},{96,112},{112,96},{1... | collective-permute-start | bytes 1572872 | tf_op jit(solution)/shard_map/ppermute | solution.py:33
  67.1 2.2 %rest.1.refs_1_ = f32[2,128,2048]{2,1,0:T(8,128)} custom-call(s32[5]{0:T(128)S(1)} %copy-done.4, s32[2,2,4]{2,1,0:T(2,128)S(1)} %add_clamp_fusion.offsets, f32[2,2,2,4]{3,2,1,0:T(2,128)S(1)} %copy-done.5, f32[2,80,3072]{2,1,0:T(8,128)S(1)} %get-tuple-element.43.full2, f32[1,80,3072]{2,1,0:T(8,128)S(1)} %get-tuple-element.50.full2_2, ...), custom_call_target="tpu_custom_call" | custom-call | flops 3000000000 | bytes 3145728 | tf_op jit(solution)/shard_map/rest/pallas_call | solution.py:449
  69.3 2.5 %collective-permute-done.9.refs_0_ = f32[2,32,2048]{2,1,0:T(8,128)S(1)} collective-permute-done((f32[2,32,2048]{2,1,0:T(8,128)S(1)}, f32[2,32,2048]{2,1,0:T(8,128)S(1)}, u32[]{:S(2)}, u32[]{:S(2)}) %collective-permute-start.9) | collective-permute-done | bytes 524320 | tf_op jit(solution)/shard_map/ppermute | solution.py:33
  71.9 1.4 %place.2.refs_2_ = f32[2,128,2048]{2,1,0:T(8,128)} custom-call(s32[5]{0:T(128)S(1)} %copy-done.4, f32[2,32,2048]{2,1,0:T(8,128)S(1)} %collective-permute-done.9.refs_0_, f32[2,128,2048]{2,1,0:T(8,128)} %rest.1.refs_1_), custom_call_target="tpu_custom_call", output_to_operand_aliasing={{}: (2, {})} | custom-call | flops 99999997952 | bytes 2097152 | tf_op jit(solution)/shard_map/place/pallas_call | solution.py:456
  73.3 3.8 %collective-permute-done.7.refs_0_ = f32[2,32,2048]{2,1,0:T(8,128)S(1)} collective-permute-done((f32[2,32,2048]{2,1,0:T(8,128)S(1)}, f32[2,32,2048]{2,1,0:T(8,128)S(1)}, u32[]{:S(2)}, u32[]{:S(2)}) %collective-permute-start.7) | collective-permute-done | bytes 524320 | tf_op jit(solution)/shard_map/ppermute | solution.py:33
  77.1 2.0 %collective-permute-done.8.refs_1_ = f32[2,32,2048]{2,1,0:T(8,128)S(1)} collective-permute-done((f32[2,32,2048]{2,1,0:T(8,128)S(1)}, f32[2,32,2048]{2,1,0:T(8,128)S(1)}, u32[]{:S(2)}, u32[]{:S(2)}) %collective-permute-start.8) | collective-permute-done | bytes 524320 | tf_op jit(solution)/shard_map/ppermute | solution.py:33
  79.0 1.6 %place.3 = f32[2,128,2048]{2,1,0:T(8,128)} custom-call(s32[5]{0:T(128)S(1)} %copy-done.4, f32[2,32,2048]{2,1,0:T(8,128)S(1)} %collective-permute-done.7.refs_0_, f32[2,32,2048]{2,1,0:T(8,128)S(1)} %collective-permute-done.8.refs_1_, f32[2,128,2048]{2,1,0:T(8,128)} %place.2.refs_2_), custom_call_target="tpu_custom_call", output_to_operand_aliasing={{}: (3, {})} | custom-call | flops 100000 | bytes 2097152 | tf_op jit(solution)/shard_map/place/pallas_call | solution.py:456
  (51 shorter events, 4.3 us)
Async XLA Ops:
  0.0 14.4 %copy-start.7 = (f32[2,2,128]{2,1,0:T(2,128)S(1)}, f32[2,2,128]{2,1,0:T(2,128)}, u32[]{:S(2)}) copy-start(f32[2,2,128]{2,1,0:T(2,128)} %rates_in.1) | copy-start | bytes 6148
  0.0 14.4 %copy-start.6 = (s32[2,2,8]{2,1,0:T(2,128)S(1)}, s32[2,2,8]{2,1,0:T(2,128)}, u32[]{:S(2)}) copy-start(s32[2,2,8]{2,1,0:T(2,128)} %offs_in.1) | copy-start | bytes 388
  0.7 17.3 %copy-start.4 = (s32[5]{0:T(128)S(1)}, s32[5]{0:T(128)}, u32[]{:S(2)}) copy-start(s32[5]{0:T(128)} %stack.50.where) | copy-start | bytes 64
  3.8 10.8 %collective-permute-start = (f32[8,2048]{1,0:T(8,128)}, f32[8,2048]{1,0:T(8,128)S(1)}, u32[]{:S(2)}, u32[]{:S(2)}) collective-permute-start(f32[8,2048]{1,0:T(8,128)} %get-tuple-element.28), channel_id=1, source_target_pairs={{0,1},{1,2},{2,3},{3,4},{4,5},{5,6},{6,7},{7,8},{8,9},{9,10},{10,1... | collective-permute-start | bytes 196616 | tf_op jit(solution)/shard_map/ppermute | solution.py:388
  9.2 8.0 %collective-permute-start.1 = (f32[16,2048]{1,0:T(8,128)}, f32[16,2048]{1,0:T(8,128)S(1)}, u32[]{:S(2)}, u32[]{:S(2)}) collective-permute-start(f32[16,2048]{1,0:T(8,128)} %get-tuple-element.29), channel_id=1, source_target_pairs={{1,0},{2,1},{3,2},{4,3},{5,4},{6,5},{7,6},{8,7},{9,8},{10,9},{11,1... | collective-permute-start | bytes 393224 | tf_op jit(solution)/shard_map/ppermute | solution.py:389
  11.1 14.6 %collective-permute-start.2 = (f32[2,32,2048]{2,1,0:T(8,128)}, f32[2,32,2048]{2,1,0:T(8,128)S(1)}, u32[]{:S(2)}, u32[]{:S(2)}) collective-permute-start(f32[2,32,2048]{2,1,0:T(8,128)} %get-tuple-element.31), channel_id=1, source_target_pairs={{0,16},{16,0},{32,48},{48,32},{64,80},{80,64},{96,112},{112,96},{1... | collective-permute-start | bytes 1572872 | tf_op jit(solution)/shard_map/ppermute | solution.py:33
  12.5 31.7 %collective-permute-start.5 = (f32[2,32,2048]{2,1,0:T(8,128)}, f32[2,32,2048]{2,1,0:T(8,128)S(1)}, u32[]{:S(2)}, u32[]{:S(2)}) collective-permute-start(f32[2,32,2048]{2,1,0:T(8,128)} %get-tuple-element.38), channel_id=1, source_target_pairs={{0,48},{16,32},{32,16},{48,0},{64,112},{80,96},{96,80},{112,64},{1... | collective-permute-start | bytes 1572872 | tf_op jit(solution)/shard_map/ppermute | solution.py:33
  18.0 1.6 %copy-start = (f32[2,1,128,2048]{3,2,1,0:T(8,128)S(1)}, f32[2,1,128,2048]{3,2,1,0:T(8,128)}, u32[]{:S(2)}) copy-start(f32[2,1,128,2048]{3,2,1,0:T(8,128)} %param.5) | copy-start | bytes 6291460
  21.1 7.0 %copy-start.1 = (f32[2,1,128,2048]{3,2,1,0:T(8,128)S(1)}, f32[2,1,128,2048]{3,2,1,0:T(8,128)}, u32[]{:S(2)}) copy-start(f32[2,1,128,2048]{3,2,1,0:T(8,128)} %param.5) | copy-start | bytes 6291460
  21.1 12.8 %collective-permute-start.4 = (f32[2,8,2048]{2,1,0:T(8,128)S(1)}, f32[2,8,2048]{2,1,0:T(8,128)S(1)}, u32[]{:S(2)}, u32[]{:S(2)}) collective-permute-start(f32[2,8,2048]{2,1,0:T(8,128)S(1)} %get-tuple-element.37), channel_id=1, source_target_pairs={{0,16},{16,0},{32,48},{48,32},{64,80},{80,64},{96,112},{112,96},{1... | collective-permute-start | bytes 393224 | tf_op jit(solution)/shard_map/ppermute | solution.py:33
  22.2 21.9 %collective-permute-start.6 = (f32[2,8,2048]{2,1,0:T(8,128)S(1)}, f32[2,8,2048]{2,1,0:T(8,128)S(1)}, u32[]{:S(2)}, u32[]{:S(2)}) collective-permute-start(f32[2,8,2048]{2,1,0:T(8,128)S(1)} %get-tuple-element.39), channel_id=1, source_target_pairs={{0,48},{16,32},{32,16},{48,0},{64,112},{80,96},{96,80},{112,64},{1... | collective-permute-start | bytes 393224 | tf_op jit(solution)/shard_map/ppermute | solution.py:33
  25.7 27.7 %collective-permute-start.3 = (f32[2,40,2048]{2,1,0:T(8,128)S(1)}, f32[2,40,2048]{2,1,0:T(8,128)S(1)}, u32[]{:S(2)}, u32[]{:S(2)}) collective-permute-start(f32[2,40,2048]{2,1,0:T(8,128)S(1)} %get-tuple-element.33), channel_id=1, source_target_pairs={{0,32},{16,48},{32,0},{48,16},{64,96},{80,112},{96,64},{112,80},{1... | collective-permute-start | bytes 1966088 | tf_op jit(solution)/shard_map/ppermute | solution.py:33
  28.2 2.8 %copy-start.2 = (f32[2,3,512,512]{3,2,1,0:T(8,128)S(1)}, f32[2,3,512,512]{3,2,1,0:T(8,128)}, u32[]{:S(2)}) copy-start(f32[2,3,512,512]{3,2,1,0:T(8,128)} %param.7) | copy-start | bytes 18874372
  31.0 13.2 %copy-start.3 = (f32[2,3,512,512]{3,2,1,0:T(8,128)S(1)}, f32[2,3,512,512]{3,2,1,0:T(8,128)}, u32[]{:S(2)}) copy-start(f32[2,3,512,512]{3,2,1,0:T(8,128)} %param.7) | copy-start | bytes 18874372
  31.0 13.2 %copy-start.5 = (f32[2,2,2,4]{3,2,1,0:T(2,128)S(1)}, f32[2,2,2,4]{3,2,1,0:T(2,128)}, u32[]{:S(2)}) copy-start(f32[2,2,2,4]{3,2,1,0:T(2,128)} %w_ref.7) | copy-start | bytes 388
  59.1 12.8 %collective-permute-start.9 = (f32[2,32,2048]{2,1,0:T(8,128)S(1)}, f32[2,32,2048]{2,1,0:T(8,128)S(1)}, u32[]{:S(2)}, u32[]{:S(2)}) collective-permute-start(f32[2,32,2048]{2,1,0:T(8,128)S(1)} %get-tuple-element.49), channel_id=1, source_target_pairs={{0,32},{16,48},{32,0},{48,16},{64,96},{80,112},{96,64},{112,80},{1... | collective-permute-start | bytes 1572872 | tf_op jit(solution)/shard_map/ppermute | solution.py:33
  63.8 13.3 %collective-permute-start.7 = (f32[2,32,2048]{2,1,0:T(8,128)S(1)}, f32[2,32,2048]{2,1,0:T(8,128)S(1)}, u32[]{:S(2)}, u32[]{:S(2)}) collective-permute-start(f32[2,32,2048]{2,1,0:T(8,128)S(1)} %get-tuple-element.47), channel_id=1, source_target_pairs={{0,16},{16,0},{32,48},{48,32},{64,80},{80,64},{96,112},{112,96},{1... | collective-permute-start | bytes 1572872 | tf_op jit(solution)/shard_map/ppermute | solution.py:33
  66.4 12.6 %collective-permute-start.8 = (f32[2,32,2048]{2,1,0:T(8,128)S(1)}, f32[2,32,2048]{2,1,0:T(8,128)S(1)}, u32[]{:S(2)}, u32[]{:S(2)}) collective-permute-start(f32[2,32,2048]{2,1,0:T(8,128)S(1)} %get-tuple-element.48), channel_id=1, source_target_pairs={{0,48},{16,32},{32,16},{48,0},{64,112},{80,96},{96,80},{112,64},{1... | collective-permute-start | bytes 1572872 | tf_op jit(solution)/shard_map/ppermute | solution.py:33

commit v3 on v2

--- a/solution.py
+++ b/solution.py
@@ -255,15 +255,14 @@
 
 
 def early_kernel(
-    where, offsets, w_ref, full1_0, m1, e1, m3, e3, th1, tl1, tiles, within, across,
-    full1, full2, th2, tl2,
-    high, low, t2, sems,
+    where, offsets, w_ref, full1_0, m1, e1, th1, tl1, tiles, within, across,
+    full2, th2, tl2,
+    high, low, full1, t2, sems,
 ):
     copies = fetch(sems, [(tiles.at[1], t2)])
     bit = where[0]
     fill(m1, e1, high.at[0], low.at[0])
-    fill(m3, e3, high.at[1], low.at[1])
-    range_products(high, low, th1, tl1, full1, 2)
+    range_products(high, low, th1, tl1, full1, 1)
     first_merges(
         (full1_0.at[0], full1.at[0]), (bit, 1 - bit), (bit, 1 - bit),
         where, offsets, w_ref, (within, across), high, low,
@@ -274,16 +273,17 @@
 
 
 def middle_kernel(
-    where, offsets, w_ref, m2, full1, full2, th1, tl1, th2, tl2, within, across,
-    d2, full1_2, full2_2,
+    where, offsets, w_ref, m2, m3, e3, full2, th1, tl1, th2, tl2, within, across,
+    d2, full1, full2_2,
     high, low,
 ):
     phases = (within, across)
     bit, bit2 = where[0], where[1]
     high[0], low[0] = split(m2[...].reshape(2 * ROWS, WIDTH))
-    range_products(high, low, th1, tl1, full1_2, 1)
+    fill(m3, e3, high.at[1], low.at[1])
+    range_products(high, low, th1, tl1, full1, 2)
     first_merges(
-        (full1_2.at[0], full1.at[1]), (bit, 1 - bit), (bit,),
+        (full1.at[0], full1.at[1]), (bit, 1 - bit), (bit,),
         where, offsets, w_ref, phases, high, low,
     )
     range_products(high, low, th2, tl2, full2_2, 1)
@@ -294,14 +294,14 @@
 
 
 def late_kernel(
-    where, offsets, w_ref, full1_2, full1, full2, th2, tl2, within, across,
+    where, offsets, w_ref, full1, full2, th2, tl2, within, across,
     d1, d3,
     high, low, full2_3,
 ):
     phases = (within, across)
     bit, bit2 = where[0], where[1]
     first_merges(
-        (full1_2.at[0], full1.at[1]), (bit, 1 - bit), (1 - bit,),
+        (full1.at[0], full1.at[1]), (bit, 1 - bit), (1 - bit,),
         where, offsets, w_ref, phases, high, low,
     )
     range_products(high, low, th2, tl2, full2_3, 1)
@@ -427,23 +427,23 @@
         [VMEM] * 3, [pltpu.VMEM(*piece_shape)] + halves_scratch(1) + [matrix_f32, dma((2,))],
         30 * 10**9, 8 * 2**20, vmem=16,
     )(where, matrices, image, e0)
-    full1, full2, t2h, t2l = call(
-        early_kernel, "early", [two, two, matrix_shape, matrix_shape],
-        [SMEM] * 3 + [VMEM] * 7 + [HBM] + [VMEM] * 2, [VMEM] * 4,
-        halves_scratch(2) + [matrix_f32, dma((1,))],
+    full2, t2h, t2l = call(
+        early_kernel, "early", [two, matrix_shape, matrix_shape],
+        [SMEM] * 3 + [VMEM] * 5 + [HBM] + [VMEM] * 2, [VMEM] * 3,
+        halves_scratch(2) + [full_scratch(1), matrix_f32, dma((1,))],
         10**4, 10**4, vmem=28,
-    )(*scalars, full1_0, m1, e1, m3, e3, t1h, t1l, matrices, within, across)
-    d2, full1_2, full2_2 = call(
-        middle_kernel, "middle", [piece_shape, one, one],
-        [SMEM] * 3 + [VMEM] * 9, [VMEM] * 3, halves_scratch(1),
+    )(*scalars, full1_0, m1, e1, t1h, t1l, matrices, within, across)
+    d2, full1, full2_2 = call(
+        middle_kernel, "middle", [piece_shape, two, one],
+        [SMEM] * 3 + [VMEM] * 10, [VMEM] * 3, halves_scratch(2),
         9 * 10**9, 10 * 2**20, vmem=24,
-    )(*scalars, m2, full1, full2, t1h, t1l, t2h, t2l, within, across)
+    )(*scalars, m2, m3, e3, full2, t1h, t1l, t2h, t2l, within, across)
     r2 = exchange(d2, 2)
     d1, d3 = call(
-        late_kernel, "late", [piece_shape] * 2, [SMEM] * 3 + [VMEM] * 7, [VMEM] * 2,
+        late_kernel, "late", [piece_shape] * 2, [SMEM] * 3 + [VMEM] * 6, [VMEM] * 2,
         halves_scratch(1) + [full_scratch(1)],
         7 * 10**9, 4 * 2**20, vmem=20,
-    )(*scalars, full1_2, full1, full2, t2h, t2l, within, across)
+    )(*scalars, full1, full2, t2h, t2l, within, across)
     r1 = exchange(d1, 1)
     r3 = exchange(d3, 3)
     (result,) = call(

time: 81 us -> 80 us (0.988)
  waiting for transfers between devices: 20.7 us -> 19.8 us
    ppermute x8, waiting for transfers between devices: 18.5 us -> 17.5 us  [exchange(): return lax.ppermute(value, 'grp', [(i, i ^ distance) for i in range(count)])]
  transfers between devices with their start and end apart: 10 -> 10, of which waited for: 5 -> 5; matrix products, arithmetic and copies ran while one was open for 4% -> 4% of each run, Pallas kernels for 27% -> 26%
where the time goes in v3:
time: 80 us; the launch traced here: 79.8 us
  Pallas kernels  32.3 us (40%)
  waiting for transfers between devices  19.8 us (25%)
  starting transfers between devices  19.4 us (24%)
  local copies, waits for them, and re-layouts  6.23 us (8%)
  other arithmetic  1.66 us (2%)
    ppermute x8, waiting for transfers between devices, exchange(): return lax.ppermute(value, 'grp', [(i, i ^ distance) for i in range(count)])  17.5 us
    ppermute x8, starting transfers between devices, exchange(): return lax.ppermute(value, 'grp', [(i, i ^ distance) for i in range(count)])  12.2 us
    pallas_call x1, Pallas kernels, per_device(): call(early_kernel, 'early', [two, matrix_shape, matrix_shape], [SMEM] * 3...  7.71 us
    pallas_call x1, Pallas kernels, per_device(): call(middle_kernel, 'middle', [piece_shape, two, one], [SMEM] * 3 + [VMEM...  7.17 us
    ppermute x1, starting transfers between devices, per_device(): before = lax.ppermute(tail, 'beam', [(i, i + 1) for i in range(beams - 1)])  5.32 us
    pallas_call x1, Pallas kernels, per_device(): call(late_kernel, 'late', [piece_shape] * 2, [SMEM] * 3 + [VMEM] * 6, [VM...  4.51 us
    unnamed x16, local copies, waits for them, and re-layouts  4.4 us
    pallas_call x1, Pallas kernels, per_device(): call(pack_kernel, 'pack', [piece_shape, piece_shape, ((8, WIDTH), f32), (...  3.15 us
  transfers between devices with their start and end apart: 10, of which 5 were waited for; matrix products, arithmetic and copies ran while one was open for 4% of the time, Pallas kernels for 26%

profile of v3, /device:TPU:97, one launch (start us, length us, event | category | flops | bytes accessed | tf_op | source)
XLA Modules:
  0.0 79.8 jit_solution(2752453438668497906)
XLA Ops:
  0.7 3.2 %pack.1 = (f32[2,32,2048]{2,1,0:T(8,128)}, f32[2,32,2048]{2,1,0:T(8,128)}, f32[8,2048]{1,0:T(8,128)}, f32[16,2048]{1,0:T(8,128)}) custom-call(f32[2,2,128]{2,1,0:T(2,128)} %rates_in.1, s32[2,2,8]{2,1,0:T(2,128)} %offs_in.1, s32[5]{0:T(128)} %stack.50.where, f32[2,128,2048]{2,1,0:T(8,128)} %bitcast.30), custom_call_target="tpu_custom_call" | custom-call | flops 1000000 | bytes 1048576 | tf_op jit(solution)/shard_map/pack/pallas_call | solution.py:379
  3.8 5.3 %collective-permute-start = (f32[8,2048]{1,0:T(8,128)}, f32[8,2048]{1,0:T(8,128)S(1)}, u32[]{:S(2)}, u32[]{:S(2)}) collective-permute-start(f32[8,2048]{1,0:T(8,128)} %get-tuple-element.27), channel_id=1, source_target_pairs={{0,1},{1,2},{2,3},{3,4},{4,5},{5,6},{6,7},{7,8},{8,9},{9,10},{10,1... | collective-permute-start | bytes 196616 | tf_op jit(solution)/shard_map/ppermute | solution.py:388
  9.2 1.9 %collective-permute-start.1 = (f32[16,2048]{1,0:T(8,128)}, f32[16,2048]{1,0:T(8,128)S(1)}, u32[]{:S(2)}, u32[]{:S(2)}) collective-permute-start(f32[16,2048]{1,0:T(8,128)} %get-tuple-element.28), channel_id=1, source_target_pairs={{1,0},{2,1},{3,2},{4,3},{5,4},{6,5},{7,6},{8,7},{9,8},{10,9},{11,1... | collective-permute-start | bytes 393224 | tf_op jit(solution)/shard_map/ppermute | solution.py:389
  11.1 1.4 %collective-permute-start.2 = (f32[2,32,2048]{2,1,0:T(8,128)}, f32[2,32,2048]{2,1,0:T(8,128)S(1)}, u32[]{:S(2)}, u32[]{:S(2)}) collective-permute-start(f32[2,32,2048]{2,1,0:T(8,128)} %get-tuple-element.30), channel_id=1, source_target_pairs={{0,16},{16,0},{32,48},{48,32},{64,80},{80,64},{96,112},{112,96},{1... | collective-permute-start | bytes 1572872 | tf_op jit(solution)/shard_map/ppermute | solution.py:33
  12.5 1.9 %collective-permute-start.4 = (f32[2,32,2048]{2,1,0:T(8,128)}, f32[2,32,2048]{2,1,0:T(8,128)S(1)}, u32[]{:S(2)}, u32[]{:S(2)}) collective-permute-start(f32[2,32,2048]{2,1,0:T(8,128)} %get-tuple-element.33), channel_id=1, source_target_pairs={{0,48},{16,32},{32,16},{48,0},{64,112},{80,96},{96,80},{112,64},{1... | collective-permute-start | bytes 1572872 | tf_op jit(solution)/shard_map/ppermute | solution.py:33
  14.9 2.3 %collective-permute-done.1.after = f32[16,2048]{1,0:T(8,128)S(1)} collective-permute-done((f32[16,2048]{1,0:T(8,128)}, f32[16,2048]{1,0:T(8,128)S(1)}, u32[]{:S(2)}, u32[]{:S(2)}) %collective-permute-start.1) | collective-permute-done | bytes 131104 | tf_op jit(solution)/shard_map/ppermute | solution.py:389
  18.0 1.6 %copy-done = f32[2,1,128,2048]{3,2,1,0:T(8,128)S(1)} copy-done((f32[2,1,128,2048]{3,2,1,0:T(8,128)S(1)}, f32[2,1,128,2048]{3,2,1,0:T(8,128)}, u32[]{:S(2)}) %copy-start) | copy-done | bytes 2097176
  19.6 1.5 %rims.1 = (f32[2,8,2048]{2,1,0:T(8,128)S(1)}, f32[2,8,2048]{2,1,0:T(8,128)S(1)}, f32[2,8,2048]{2,1,0:T(8,128)S(1)}, f32[2,40,2048]{2,1,0:T(8,128)S(1)}) custom-call(s32[5]{0:T(128)S(1)} %copy-done.4, f32[2,128,2048]{2,1,0:T(8,128)S(1)} %bitcast.31, f32[8,2048]{1,0:T(8,128)S(1)} %collective-permute-done.before, f32[16,2048]{1,0:T(8,128)S(1)} %collective-permute-done.1.after), custom_call_target="tpu_custom_call" | custom-call | flops 1000000 | bytes 3145728 | tf_op jit(solution)/shard_map/rims/pallas_call | solution.py:391
  21.1 2.8 %collective-permute-start.5 = (f32[2,8,2048]{2,1,0:T(8,128)S(1)}, f32[2,8,2048]{2,1,0:T(8,128)S(1)}, u32[]{:S(2)}, u32[]{:S(2)}) collective-permute-start(f32[2,8,2048]{2,1,0:T(8,128)S(1)} %get-tuple-element.34), channel_id=1, source_target_pairs={{0,48},{16,32},{32,16},{48,0},{64,112},{80,96},{96,80},{112,64},{1... | collective-permute-start | bytes 393224 | tf_op jit(solution)/shard_map/ppermute | solution.py:33
  24.4 1.1 %multiply_cosine_fusion = (f32[1,2,72,512]{3,2,1,0:T(8,128)S(1)}, f32[1,2,72,512]{3,2,1,0:T(8,128)S(1)}) fusion(f32[512]{0:T(512)S(1)} %iota_multiply_fusion.1, f32[2,72]{1,0:T(2,128)S(1)} %pad_maximum_fusion.3), kind=kLoop, calls=%fused_computation.3 | loop fusion | flops 73728 | bytes 592448 | tf_op jit(solution)/shard_map/cos | solution.py:414
  25.5 2.6 %collective-permute-start.3 = (f32[2,40,2048]{2,1,0:T(8,128)S(1)}, f32[2,40,2048]{2,1,0:T(8,128)S(1)}, u32[]{:S(2)}, u32[]{:S(2)}) collective-permute-start(f32[2,40,2048]{2,1,0:T(8,128)S(1)} %get-tuple-element.32), channel_id=1, source_target_pairs={{0,32},{16,48},{32,0},{48,16},{64,96},{80,112},{96,64},{112,80},{1... | collective-permute-start | bytes 1966088 | tf_op jit(solution)/shard_map/ppermute | solution.py:33
  28.2 2.8 %copy-done.2 = f32[2,3,512,512]{3,2,1,0:T(8,128)S(1)} copy-done((f32[2,3,512,512]{3,2,1,0:T(8,128)S(1)}, f32[2,3,512,512]{3,2,1,0:T(8,128)}, u32[]{:S(2)}) %copy-start.2) | copy-done | bytes 6291480
  31.0 3.0 %own.1 = (f32[1,80,3072]{2,1,0:T(8,128)S(1)}, bf16[1536,512]{1,0:T(8,128)(2,1)S(1)}, bf16[1536,512]{1,0:T(8,128)(2,1)S(1)}) custom-call(s32[5]{0:T(128)S(1)} %copy-done.4, f32[2,1536,512]{2,1,0:T(8,128)S(1)} %bitcast.33, f32[2,128,2048]{2,1,0:T(8,128)S(1)} %bitcast.32, f32[2,8,2048]{2,1,0:T(8,128)S(1)} %get-tuple-element.35.e0), custom_call_target="tpu_custom_call" | custom-call | flops 30000001024 | bytes 8388608 | tf_op jit(solution)/shard_map/own/pallas_call | solution.py:425
  34.0 7.7 %early.1 = (f32[2,80,3072]{2,1,0:T(8,128)S(1)}, bf16[1536,512]{1,0:T(8,128)(2,1)S(1)}, bf16[1536,512]{1,0:T(8,128)(2,1)S(1)}) custom-call(s32[5]{0:T(128)S(1)} %copy-done.4, s32[2,2,4]{2,1,0:T(2,128)S(1)} %add_clamp_fusion.offsets, f32[2,2,2,4]{3,2,1,0:T(2,128)S(1)} %copy-done.5, f32[1,80,3072]{2,1,0:T(8,128)S(1)} %get-tuple-element.36.full1_0, ...), custom_call_target="tpu_custom_call" | custom-call | flops 10000 | bytes 10000 | tf_op jit(solution)/shard_map/early/pallas_call | solution.py:430
  41.7 2.5 %collective-permute-done.5.e3 = f32[2,8,2048]{2,1,0:T(8,128)S(1)} collective-permute-done((f32[2,8,2048]{2,1,0:T(8,128)S(1)}, f32[2,8,2048]{2,1,0:T(8,128)S(1)}, u32[]{:S(2)}, u32[]{:S(2)}) %collective-permute-start.5) | collective-permute-done | bytes 131104 | tf_op jit(solution)/shard_map/ppermute | solution.py:33
  44.1 7.2 %middle.1 = (f32[2,32,2048]{2,1,0:T(8,128)S(1)}, f32[2,80,3072]{2,1,0:T(8,128)S(1)}, f32[1,80,3072]{2,1,0:T(8,128)S(1)}) custom-call(s32[5]{0:T(128)S(1)} %copy-done.4, s32[2,2,4]{2,1,0:T(2,128)S(1)} %add_clamp_fusion.offsets, f32[2,2,2,4]{3,2,1,0:T(2,128)S(1)} %copy-done.5, f32[2,40,2048]{2,1,0:T(8,128)S(1)} %collective-permute-done.3.m2, ...), custom_call_target="tpu_custom_call" | custom-call | flops 8999999488 | bytes 10485760 | tf_op jit(solution)/shard_map/middle/pallas_call | solution.py:436
  51.3 2.2 %collective-permute-start.9 = (f32[2,32,2048]{2,1,0:T(8,128)S(1)}, f32[2,32,2048]{2,1,0:T(8,128)S(1)}, u32[]{:S(2)}, u32[]{:S(2)}) collective-permute-start(f32[2,32,2048]{2,1,0:T(8,128)S(1)} %get-tuple-element.47), channel_id=1, source_target_pairs={{0,32},{16,48},{32,0},{48,16},{64,96},{80,112},{96,64},{112,80},{1... | collective-permute-start | bytes 1572872 | tf_op jit(solution)/shard_map/ppermute | solution.py:33
  53.5 4.5 %late.1 = (f32[2,32,2048]{2,1,0:T(8,128)S(1)}, f32[2,32,2048]{2,1,0:T(8,128)S(1)}) custom-call(s32[5]{0:T(128)S(1)} %copy-done.4, s32[2,2,4]{2,1,0:T(2,128)S(1)} %add_clamp_fusion.offsets, f32[2,2,2,4]{3,2,1,0:T(2,128)S(1)} %copy-done.5, f32[2,80,3072]{2,1,0:T(8,128)S(1)} %get-tuple-element.44.full1, f32[2,80,3072]{2,1,0:T(8,128)S(1)} %get-tuple-element.41.full2, ...), custom_call_target="tpu_custom_call" | custom-call | flops 7000000000 | bytes 4194304 | tf_op jit(solution)/shard_map/late/pallas_call | solution.py:442
  59.3 2.2 %rest.1.refs_1_ = f32[2,128,2048]{2,1,0:T(8,128)} custom-call(s32[5]{0:T(128)S(1)} %copy-done.4, s32[2,2,4]{2,1,0:T(2,128)S(1)} %add_clamp_fusion.offsets, f32[2,2,2,4]{3,2,1,0:T(2,128)S(1)} %copy-done.5, f32[2,80,3072]{2,1,0:T(8,128)S(1)} %get-tuple-element.41.full2, f32[1,80,3072]{2,1,0:T(8,128)S(1)} %get-tuple-element.48.full2_2, ...), custom_call_target="tpu_custom_call" | custom-call | flops 3000000000 | bytes 3145728 | tf_op jit(solution)/shard_map/rest/pallas_call | solution.py:449
  61.5 5.0 %collective-permute-done.9.refs_0_ = f32[2,32,2048]{2,1,0:T(8,128)S(1)} collective-permute-done((f32[2,32,2048]{2,1,0:T(8,128)S(1)}, f32[2,32,2048]{2,1,0:T(8,128)S(1)}, u32[]{:S(2)}, u32[]{:S(2)}) %collective-permute-start.9) | collective-permute-done | bytes 524320 | tf_op jit(solution)/shard_map/ppermute | solution.py:33
  66.5 1.4 %place.2.refs_2_ = f32[2,128,2048]{2,1,0:T(8,128)} custom-call(s32[5]{0:T(128)S(1)} %copy-done.4, f32[2,32,2048]{2,1,0:T(8,128)S(1)} %collective-permute-done.9.refs_0_, f32[2,128,2048]{2,1,0:T(8,128)} %rest.1.refs_1_), custom_call_target="tpu_custom_call", output_to_operand_aliasing={{}: (2, {})} | custom-call | flops 99999997952 | bytes 2097152 | tf_op jit(solution)/shard_map/place/pallas_call | solution.py:456
  68.0 8.9 %collective-permute-done.7.refs_0_ = f32[2,32,2048]{2,1,0:T(8,128)S(1)} collective-permute-done((f32[2,32,2048]{2,1,0:T(8,128)S(1)}, f32[2,32,2048]{2,1,0:T(8,128)S(1)}, u32[]{:S(2)}, u32[]{:S(2)}) %collective-permute-start.7) | collective-permute-done | bytes 524320 | tf_op jit(solution)/shard_map/ppermute | solution.py:33
  76.8 1.2 %collective-permute-done.8.refs_1_ = f32[2,32,2048]{2,1,0:T(8,128)S(1)} collective-permute-done((f32[2,32,2048]{2,1,0:T(8,128)S(1)}, f32[2,32,2048]{2,1,0:T(8,128)S(1)}, u32[]{:S(2)}, u32[]{:S(2)}) %collective-permute-start.8) | collective-permute-done | bytes 524320 | tf_op jit(solution)/shard_map/ppermute | solution.py:33
  78.0 1.6 %place.3 = f32[2,128,2048]{2,1,0:T(8,128)} custom-call(s32[5]{0:T(128)S(1)} %copy-done.4, f32[2,32,2048]{2,1,0:T(8,128)S(1)} %collective-permute-done.7.refs_0_, f32[2,32,2048]{2,1,0:T(8,128)S(1)} %collective-permute-done.8.refs_1_, f32[2,128,2048]{2,1,0:T(8,128)} %place.2.refs_2_), custom_call_target="tpu_custom_call", output_to_operand_aliasing={{}: (3, {})} | custom-call | flops 100000 | bytes 2097152 | tf_op jit(solution)/shard_map/place/pallas_call | solution.py:456
  (51 shorter events, 3.7 us)
Async XLA Ops:
  0.0 14.4 %copy-start.7 = (f32[2,2,128]{2,1,0:T(2,128)S(1)}, f32[2,2,128]{2,1,0:T(2,128)}, u32[]{:S(2)}) copy-start(f32[2,2,128]{2,1,0:T(2,128)} %rates_in.1) | copy-start | bytes 6148
  0.0 14.4 %copy-start.6 = (s32[2,2,8]{2,1,0:T(2,128)S(1)}, s32[2,2,8]{2,1,0:T(2,128)}, u32[]{:S(2)}) copy-start(s32[2,2,8]{2,1,0:T(2,128)} %offs_in.1) | copy-start | bytes 388
  0.7 17.3 %copy-start.4 = (s32[5]{0:T(128)S(1)}, s32[5]{0:T(128)}, u32[]{:S(2)}) copy-start(s32[5]{0:T(128)} %stack.50.where) | copy-start | bytes 64
  3.8 10.8 %collective-permute-start = (f32[8,2048]{1,0:T(8,128)}, f32[8,2048]{1,0:T(8,128)S(1)}, u32[]{:S(2)}, u32[]{:S(2)}) collective-permute-start(f32[8,2048]{1,0:T(8,128)} %get-tuple-element.27), channel_id=1, source_target_pairs={{0,1},{1,2},{2,3},{3,4},{4,5},{5,6},{6,7},{7,8},{8,9},{9,10},{10,1... | collective-permute-start | bytes 196616 | tf_op jit(solution)/shard_map/ppermute | solution.py:388
  9.2 8.0 %collective-permute-start.1 = (f32[16,2048]{1,0:T(8,128)}, f32[16,2048]{1,0:T(8,128)S(1)}, u32[]{:S(2)}, u32[]{:S(2)}) collective-permute-start(f32[16,2048]{1,0:T(8,128)} %get-tuple-element.28), channel_id=1, source_target_pairs={{1,0},{2,1},{3,2},{4,3},{5,4},{6,5},{7,6},{8,7},{9,8},{10,9},{11,1... | collective-permute-start | bytes 393224 | tf_op jit(solution)/shard_map/ppermute | solution.py:389
  11.1 14.5 %collective-permute-start.2 = (f32[2,32,2048]{2,1,0:T(8,128)}, f32[2,32,2048]{2,1,0:T(8,128)S(1)}, u32[]{:S(2)}, u32[]{:S(2)}) collective-permute-start(f32[2,32,2048]{2,1,0:T(8,128)} %get-tuple-element.30), channel_id=1, source_target_pairs={{0,16},{16,0},{32,48},{48,32},{64,80},{80,64},{96,112},{112,96},{1... | collective-permute-start | bytes 1572872 | tf_op jit(solution)/shard_map/ppermute | solution.py:33
  12.5 31.7 %collective-permute-start.4 = (f32[2,32,2048]{2,1,0:T(8,128)}, f32[2,32,2048]{2,1,0:T(8,128)S(1)}, u32[]{:S(2)}, u32[]{:S(2)}) collective-permute-start(f32[2,32,2048]{2,1,0:T(8,128)} %get-tuple-element.33), channel_id=1, source_target_pairs={{0,48},{16,32},{32,16},{48,0},{64,112},{80,96},{96,80},{112,64},{1... | collective-permute-start | bytes 1572872 | tf_op jit(solution)/shard_map/ppermute | solution.py:33
  18.0 1.6 %copy-start = (f32[2,1,128,2048]{3,2,1,0:T(8,128)S(1)}, f32[2,1,128,2048]{3,2,1,0:T(8,128)}, u32[]{:S(2)}) copy-start(f32[2,1,128,2048]{3,2,1,0:T(8,128)} %param.5) | copy-start | bytes 6291460
  21.1 7.0 %copy-start.1 = (f32[2,1,128,2048]{3,2,1,0:T(8,128)S(1)}, f32[2,1,128,2048]{3,2,1,0:T(8,128)}, u32[]{:S(2)}) copy-start(f32[2,1,128,2048]{3,2,1,0:T(8,128)} %param.5) | copy-start | bytes 6291460
  21.1 23.0 %collective-permute-start.5 = (f32[2,8,2048]{2,1,0:T(8,128)S(1)}, f32[2,8,2048]{2,1,0:T(8,128)S(1)}, u32[]{:S(2)}, u32[]{:S(2)}) collective-permute-start(f32[2,8,2048]{2,1,0:T(8,128)S(1)} %get-tuple-element.34), channel_id=1, source_target_pairs={{0,48},{16,32},{32,16},{48,0},{64,112},{80,96},{96,80},{112,64},{1... | collective-permute-start | bytes 393224 | tf_op jit(solution)/shard_map/ppermute | solution.py:33
  24.0 10.0 %collective-permute-start.6 = (f32[2,8,2048]{2,1,0:T(8,128)S(1)}, f32[2,8,2048]{2,1,0:T(8,128)S(1)}, u32[]{:S(2)}, u32[]{:S(2)}) collective-permute-start(f32[2,8,2048]{2,1,0:T(8,128)S(1)} %get-tuple-element.38), channel_id=1, source_target_pairs={{0,16},{16,0},{32,48},{48,32},{64,80},{80,64},{96,112},{112,96},{1... | collective-permute-start | bytes 393224 | tf_op jit(solution)/shard_map/ppermute | solution.py:33
  25.5 18.6 %collective-permute-start.3 = (f32[2,40,2048]{2,1,0:T(8,128)S(1)}, f32[2,40,2048]{2,1,0:T(8,128)S(1)}, u32[]{:S(2)}, u32[]{:S(2)}) collective-permute-start(f32[2,40,2048]{2,1,0:T(8,128)S(1)} %get-tuple-element.32), channel_id=1, source_target_pairs={{0,32},{16,48},{32,0},{48,16},{64,96},{80,112},{96,64},{112,80},{1... | collective-permute-start | bytes 1966088 | tf_op jit(solution)/shard_map/ppermute | solution.py:33
  28.2 2.8 %copy-start.2 = (f32[2,3,512,512]{3,2,1,0:T(8,128)S(1)}, f32[2,3,512,512]{3,2,1,0:T(8,128)}, u32[]{:S(2)}) copy-start(f32[2,3,512,512]{3,2,1,0:T(8,128)} %param.7) | copy-start | bytes 18874372
  31.0 3.0 %copy-start.3 = (f32[2,3,512,512]{3,2,1,0:T(8,128)S(1)}, f32[2,3,512,512]{3,2,1,0:T(8,128)}, u32[]{:S(2)}) copy-start(f32[2,3,512,512]{3,2,1,0:T(8,128)} %param.7) | copy-start | bytes 18874372
  31.0 3.0 %copy-start.5 = (f32[2,2,2,4]{3,2,1,0:T(2,128)S(1)}, f32[2,2,2,4]{3,2,1,0:T(2,128)}, u32[]{:S(2)}) copy-start(f32[2,2,2,4]{3,2,1,0:T(2,128)} %w_ref.7) | copy-start | bytes 388
  51.3 15.2 %collective-permute-start.9 = (f32[2,32,2048]{2,1,0:T(8,128)S(1)}, f32[2,32,2048]{2,1,0:T(8,128)S(1)}, u32[]{:S(2)}, u32[]{:S(2)}) collective-permute-start(f32[2,32,2048]{2,1,0:T(8,128)S(1)} %get-tuple-element.47), channel_id=1, source_target_pairs={{0,32},{16,48},{32,0},{48,16},{64,96},{80,112},{96,64},{112,80},{1... | collective-permute-start | bytes 1572872 | tf_op jit(solution)/shard_map/ppermute | solution.py:33
  58.0 18.8 %collective-permute-start.7 = (f32[2,32,2048]{2,1,0:T(8,128)S(1)}, f32[2,32,2048]{2,1,0:T(8,128)S(1)}, u32[]{:S(2)}, u32[]{:S(2)}) collective-permute-start(f32[2,32,2048]{2,1,0:T(8,128)S(1)} %get-tuple-element.45), channel_id=1, source_target_pairs={{0,16},{16,0},{32,48},{48,32},{64,80},{80,64},{96,112},{112,96},{1... | collective-permute-start | bytes 1572872 | tf_op jit(solution)/shard_map/ppermute | solution.py:33
  58.5 19.4 %collective-permute-start.8 = (f32[2,32,2048]{2,1,0:T(8,128)S(1)}, f32[2,32,2048]{2,1,0:T(8,128)S(1)}, u32[]{:S(2)}, u32[]{:S(2)}) collective-permute-start(f32[2,32,2048]{2,1,0:T(8,128)S(1)} %get-tuple-element.46), channel_id=1, source_target_pairs={{0,48},{16,32},{32,16},{48,0},{64,112},{80,96},{96,80},{112,64},{1... | collective-permute-start | bytes 1572872 | tf_op jit(solution)/shard_map/ppermute | solution.py:33

commit v4 on v3

--- a/solution.py
+++ b/solution.py
@@ -182,28 +182,18 @@
             for d, out in ((1, q1), (3, q3))
         ],
     )
-    lane = lax.broadcasted_iota(jnp.int32, (1, WIDTH), 1)
-
-    def line(*values):
-        out = jnp.zeros((1, WIDTH), jnp.float32)
-        for i, value in enumerate(values):
-            out = jnp.where(lane == i, value, out)
-        return out
-
     for copy in copies[:4]:
         copy.wait()
-
-    def offset(e, block):
-        return offs[e, block].astype(jnp.float32)
-
     tail[0:2] = edges[1, 0, 6:8]
     tail[2:4] = edges[1, 1, 6:8]
-    tail[4:5] = line(rates[0, 127], rates[1, 127], offset(0, 7), offset(1, 7))
-    tail[5:8] = jnp.zeros((3, WIDTH), jnp.float32)
+    tail[4:8] = jnp.zeros((4, WIDTH), jnp.float32)
     head[0:4] = edges[0, 0, 0:4]
     head[4:8] = edges[0, 1, 0:4]
-    head[8:9] = line(rates[0, 0], rates[0, 1], rates[1, 0], rates[1, 1], offset(0, 0), offset(1, 0))
-    head[9:16] = jnp.zeros((7, WIDTH), jnp.float32)
+    head[8:16] = jnp.zeros((8, WIDTH), jnp.float32)
+    for out, row in ((tail, 4), (head, 8)):
+        for e in range(2):
+            out[row + e : row + e + 1, 0:128] = rates[e : e + 1]
+            out[row + e : row + e + 1, 128:136] = offs[e : e + 1].astype(jnp.float32)
     for copy in copies[4:]:
         copy.wait()
 
@@ -323,20 +313,13 @@
 
 
 def place_kernel(distances, where, *refs):
-    pieces, (out, stages, sems, out_sems) = refs[: len(distances)], refs[-4:]
-    reads, writes = [], []
-    for i, d in enumerate(distances):
-        for n in range(2):
-            at = pl.ds(pl.multiple_of((where[4] ^ d) * QROWS + 16 * n, 16), 16)
-            half = stages.at[i, :, 16 * n : 16 * n + 16]
-            reads.append((pieces[i].at[:, 16 * n : 16 * n + 16], half))
-            writes.append((half, out.at[:, at]))
-    reads = fetch(sems, reads)
+    pieces, (out, sems) = refs[: len(distances)], refs[-2:]
     copies = []
-    for i, pair in enumerate(writes):
-        reads[i].wait()
-        copies += fetch(out_sems.at[i : i + 1], [pair])
-    for copy in copies:
+    for piece, d in zip(pieces, distances):
+        for n in (0, 16):
+            at = pl.ds(pl.multiple_of((where[4] ^ d) * QROWS + n, 16), 16)
+            copies += [(piece.at[c, n : n + 16], out.at[c, at]) for c in range(2)]
+    for copy in fetch(sems, copies):
         copy.wait()
 
 
@@ -379,9 +362,9 @@
     q1, q3, tail, head = call(
         pack_kernel, "pack", [piece_shape, piece_shape, ((8, WIDTH), f32), ((16, WIDTH), f32)],
         [HBM] * 2 + [SMEM] + [HBM], [VMEM] * 4,
-        [pltpu.VMEM((2, 2, 8, WIDTH), f32), pltpu.SMEM((2, 4 * QROWS), f32)]
-        + [pltpu.SMEM((2, 8), jnp.int32), dma((6,))],
-        10**6, 2**20, vmem=62,
+        [pltpu.VMEM((2, 2, 8, WIDTH), f32), pltpu.VMEM((2, 4 * QROWS), f32)]
+        + [pltpu.VMEM((2, 8), jnp.int32), dma((6,))],
+        10**6, 2**20, vmem=60,
     )(phase_rates, tile_offsets, where, image)
     m1 = exchange(q1, 1)
     m3 = exchange(q3, 3)
@@ -396,16 +379,15 @@
     )(where, image, before, after)
     e1 = exchange(p1, 1)
     e3 = exchange(p3, 3)
-    q2, m1, e0 = lax.optimization_barrier((q2, m1, e0))
+    q2, e0 = lax.optimization_barrier((q2, e0))
     m2 = exchange(q2, 2)
 
-    before_values, after_values = before[4, :4].reshape(2, 2), after[8, :6]
-    line = jnp.concatenate([before_values[0][:, None], phase_rates[0], after_values[:4].reshape(2, 2)], 1)
+    line = jnp.concatenate([before[4:6, 127:128], phase_rates[0], after[8:10, :2]], 1)
     line = lax.dynamic_slice_in_dim(line, mine * QROWS, QROWS + 3, 1)
     rates_b = lax.dynamic_slice_in_dim(phase_rates[1], mine * QROWS, QROWS, 1)
     rates = jnp.concatenate([line[:, 1:], jnp.zeros((2, 5), f32), line[:, :1], rates_b], 1)
     offs = tile_offsets[0].astype(f32)
-    line = jnp.concatenate([before_values[1][:, None], offs, after_values[4:][:, None]], 1)
+    line = jnp.concatenate([before[4:6, 135:136], offs, after[8:10, 128:129]], 1)
     line = lax.dynamic_slice_in_dim(line, mine * 2, 4, 1).astype(jnp.int32)
     offs_a = jnp.stack([line[:, 1], line[:, 2], line[:, 3], line[:, 0]], 1)
     offs_b = jnp.pad(lax.dynamic_slice_in_dim(tile_offsets[1], mine * 2, 2, 1), ((0, 0), (0, 2)))
@@ -455,8 +437,7 @@
     for distances, pieces, flops in (((2,), (r2,), 10**11), ((1, 3), (r1, r3), 10**5)):
         (result,) = call(
             functools.partial(place_kernel, distances), "place", [(result.shape, f32)],
-            [SMEM] + [HBM] * (len(pieces) + 1), [HBM],
-            [pltpu.VMEM((len(pieces), *piece_shape[0]), f32)] + [dma((2 * len(pieces),))] * 2,
+            [SMEM] + [VMEM] * len(pieces) + [HBM], [HBM], [dma((4 * len(pieces),))],
             flops, 2**21, {1 + len(pieces): 0},
         )(where, *pieces, result)
     return result[:, None]

time: 80 us -> 80.1 us (level)
  waiting for transfers between devices: 19.8 us -> 23.5 us
  local copies, waits for them, and re-layouts: 6.23 us -> 4.15 us
  starting transfers between devices: 19.4 us -> 17.7 us
    ppermute x8, waiting for transfers between devices: 17.5 us -> 20.6 us  [exchange(): return lax.ppermute(value, 'grp', [(i, i ^ distance) for i in range(count)])]
    ppermute x8, starting transfers between devices: 12.2 us -> 10.5 us  [exchange(): return lax.ppermute(value, 'grp', [(i, i ^ distance) for i in range(count)])]
    unnamed x16 -> x14, local copies, waits for them, and re-layouts: 4.4 us -> 2.81 us
  transfers between devices with their start and end apart: 10 -> 10, of which waited for: 5 -> 6; matrix products, arithmetic and copies ran while one was open for 4% -> 3% of each run, Pallas kernels for 26% -> 26%
where the time goes in v4:
time: 80.1 us; the launch traced here: 79.7 us
  Pallas kernels  32.3 us (40%)
  waiting for transfers between devices  23.5 us (29%)
  starting transfers between devices  17.7 us (22%)
  local copies, waits for them, and re-layouts  4.15 us (5%)
  other arithmetic  1.66 us (2%)
    ppermute x8, waiting for transfers between devices, exchange(): return lax.ppermute(value, 'grp', [(i, i ^ distance) for i in range(count)])  20.6 us
    ppermute x8, starting transfers between devices, exchange(): return lax.ppermute(value, 'grp', [(i, i ^ distance) for i in range(count)])  10.5 us
    pallas_call x1, Pallas kernels, per_device(): call(early_kernel, 'early', [two, matrix_shape, matrix_shape], [SMEM] * 3...  7.72 us
    pallas_call x1, Pallas kernels, per_device(): call(middle_kernel, 'middle', [piece_shape, two, one], [SMEM] * 3 + [VMEM...  7.21 us
    ppermute x1, starting transfers between devices, per_device(): before = lax.ppermute(tail, 'beam', [(i, i + 1) for i in range(beams - 1)])  5.32 us
    pallas_call x1, Pallas kernels, per_device(): call(late_kernel, 'late', [piece_shape] * 2, [SMEM] * 3 + [VMEM] * 6, [VM...  4.5 us
    pallas_call x1, Pallas kernels, per_device(): call(pack_kernel, 'pack', [piece_shape, piece_shape, ((8, WIDTH), f32), (...  3.23 us
    pallas_call x1, Pallas kernels, per_device(): call(own_kernel, 'own', [one, matrix_shape, matrix_shape], [SMEM] + [HBM]...  2.95 us
  transfers between devices with their start and end apart: 10, of which 6 were waited for; matrix products, arithmetic and copies ran while one was open for 3% of the time, Pallas kernels for 26%

profile of v4, /device:TPU:97, one launch (start us, length us, event | category | flops | bytes accessed | tf_op | source)
XLA Modules:
  0.0 79.7 jit_solution(13012981337657102166)
XLA Ops:
  0.0 0.6 stack.50.where
  0.6 3.2 %pack.1 = (f32[2,32,2048]{2,1,0:T(8,128)}, f32[2,32,2048]{2,1,0:T(8,128)}, f32[8,2048]{1,0:T(8,128)}, f32[16,2048]{1,0:T(8,128)}) custom-call(f32[2,2,128]{2,1,0:T(2,128)} %rates_in.1, s32[2,2,8]{2,1,0:T(2,128)} %offs_in.1, s32[5]{0:T(128)} %stack.50.where, f32[2,128,2048]{2,1,0:T(8,128)} %bitcast.24), custom_call_target="tpu_custom_call" | custom-call | flops 1000000 | bytes 1048576 | tf_op jit(solution)/shard_map/pack/pallas_call | solution.py:362
  3.9 5.3 %collective-permute-start = (f32[8,2048]{1,0:T(8,128)}, f32[8,2048]{1,0:T(8,128)S(1)}, u32[]{:S(2)}, u32[]{:S(2)}) collective-permute-start(f32[8,2048]{1,0:T(8,128)} %get-tuple-element.26), channel_id=1, source_target_pairs={{0,1},{1,2},{2,3},{3,4},{4,5},{5,6},{6,7},{7,8},{8,9},{9,10},{10,1... | collective-permute-start | bytes 196616 | tf_op jit(solution)/shard_map/ppermute | solution.py:371
  9.2 1.9 %collective-permute-start.1 = (f32[16,2048]{1,0:T(8,128)}, f32[16,2048]{1,0:T(8,128)S(1)}, u32[]{:S(2)}, u32[]{:S(2)}) collective-permute-start(f32[16,2048]{1,0:T(8,128)} %get-tuple-element.27), channel_id=1, source_target_pairs={{1,0},{2,1},{3,2},{4,3},{5,4},{6,5},{7,6},{8,7},{9,8},{10,9},{11,1... | collective-permute-start | bytes 393224 | tf_op jit(solution)/shard_map/ppermute | solution.py:372
  11.1 2.8 %collective-permute-start.3 = (f32[2,32,2048]{2,1,0:T(8,128)}, f32[2,32,2048]{2,1,0:T(8,128)S(1)}, u32[]{:S(2)}, u32[]{:S(2)}) collective-permute-start(f32[2,32,2048]{2,1,0:T(8,128)} %get-tuple-element.31), channel_id=1, source_target_pairs={{0,48},{16,32},{32,16},{48,0},{64,112},{80,96},{96,80},{112,64},{1... | collective-permute-start | bytes 1572872 | tf_op jit(solution)/shard_map/ppermute | solution.py:33
  14.3 2.9 %collective-permute-done.1.after = f32[16,2048]{1,0:T(8,128)S(1)} collective-permute-done((f32[16,2048]{1,0:T(8,128)}, f32[16,2048]{1,0:T(8,128)S(1)}, u32[]{:S(2)}, u32[]{:S(2)}) %collective-permute-start.1) | collective-permute-done | bytes 131104 | tf_op jit(solution)/shard_map/ppermute | solution.py:372
  17.8 1.5 %rims.1 = (f32[2,8,2048]{2,1,0:T(8,128)S(1)}, f32[2,8,2048]{2,1,0:T(8,128)S(1)}, f32[2,8,2048]{2,1,0:T(8,128)S(1)}, f32[2,40,2048]{2,1,0:T(8,128)S(1)}) custom-call(s32[5]{0:T(128)S(1)} %copy-done.3, f32[2,128,2048]{2,1,0:T(8,128)S(1)} %bitcast.25, f32[8,2048]{1,0:T(8,128)S(1)} %collective-permute-done.before, f32[16,2048]{1,0:T(8,128)S(1)} %collective-permute-done.1.after), custom_call_target="tpu_custom_call" | custom-call | flops 1000000 | bytes 3145728 | tf_op jit(solution)/shard_map/rims/pallas_call | solution.py:374
  19.3 2.8 %collective-permute-start.4 = (f32[2,8,2048]{2,1,0:T(8,128)S(1)}, f32[2,8,2048]{2,1,0:T(8,128)S(1)}, u32[]{:S(2)}, u32[]{:S(2)}) collective-permute-start(f32[2,8,2048]{2,1,0:T(8,128)S(1)} %get-tuple-element.32), channel_id=1, source_target_pairs={{0,48},{16,32},{32,16},{48,0},{64,112},{80,96},{96,80},{112,64},{1... | collective-permute-start | bytes 393224 | tf_op jit(solution)/shard_map/ppermute | solution.py:33
  22.2 1.3 %collective-permute-start.2 = (f32[2,40,2048]{2,1,0:T(8,128)S(1)}, f32[2,40,2048]{2,1,0:T(8,128)S(1)}, u32[]{:S(2)}, u32[]{:S(2)}) collective-permute-start(f32[2,40,2048]{2,1,0:T(8,128)S(1)} %get-tuple-element.30), channel_id=1, source_target_pairs={{0,32},{16,48},{32,0},{48,16},{64,96},{80,112},{96,64},{112,80},{1... | collective-permute-start | bytes 1966088 | tf_op jit(solution)/shard_map/ppermute | solution.py:33
  23.5 2.8 %copy-done.1 = f32[2,3,512,512]{3,2,1,0:T(8,128)S(1)} copy-done((f32[2,3,512,512]{3,2,1,0:T(8,128)S(1)}, f32[2,3,512,512]{3,2,1,0:T(8,128)}, u32[]{:S(2)}) %copy-start.1) | copy-done | bytes 6291480
  26.2 3.0 %own.1 = (f32[1,80,3072]{2,1,0:T(8,128)S(1)}, bf16[1536,512]{1,0:T(8,128)(2,1)S(1)}, bf16[1536,512]{1,0:T(8,128)(2,1)S(1)}) custom-call(s32[5]{0:T(128)S(1)} %copy-done.3, f32[2,1536,512]{2,1,0:T(8,128)S(1)} %bitcast.27, f32[2,128,2048]{2,1,0:T(8,128)S(1)} %bitcast.26, f32[2,8,2048]{2,1,0:T(8,128)S(1)} %get-tuple-element.33.e0), custom_call_target="tpu_custom_call" | custom-call | flops 30000001024 | bytes 8388608 | tf_op jit(solution)/shard_map/own/pallas_call | solution.py:407
  29.6 1.1 %multiply_cosine_fusion = (f32[1,2,72,512]{3,2,1,0:T(8,128)S(1)}, f32[1,2,72,512]{3,2,1,0:T(8,128)S(1)}) fusion(f32[512]{0:T(512)S(1)} %iota_multiply_fusion.1, f32[2,72]{1,0:T(2,128)S(1)} %pad_maximum_fusion.3), kind=kLoop, calls=%fused_computation.3 | loop fusion | flops 73728 | bytes 592448 | tf_op jit(solution)/shard_map/cos | solution.py:396
  30.9 7.7 %early.1 = (f32[2,80,3072]{2,1,0:T(8,128)S(1)}, bf16[1536,512]{1,0:T(8,128)(2,1)S(1)}, bf16[1536,512]{1,0:T(8,128)(2,1)S(1)}) custom-call(s32[5]{0:T(128)S(1)} %copy-done.3, s32[2,2,4]{2,1,0:T(2,128)S(1)} %add_clamp_fusion.offsets, f32[2,2,2,4]{3,2,1,0:T(2,128)S(1)} %copy-done.4, f32[1,80,3072]{2,1,0:T(8,128)S(1)} %get-tuple-element.34.full1_0, ...), custom_call_target="tpu_custom_call" | custom-call | flops 10000 | bytes 10000 | tf_op jit(solution)/shard_map/early/pallas_call | solution.py:412
  38.7 5.4 %collective-permute-done.2.m2 = f32[2,40,2048]{2,1,0:T(8,128)S(1)} collective-permute-done((f32[2,40,2048]{2,1,0:T(8,128)S(1)}, f32[2,40,2048]{2,1,0:T(8,128)S(1)}, u32[]{:S(2)}, u32[]{:S(2)}) %collective-permute-start.2) | collective-permute-done | bytes 655392 | tf_op jit(solution)/shard_map/ppermute | solution.py:33
  44.1 7.2 %middle.1 = (f32[2,32,2048]{2,1,0:T(8,128)S(1)}, f32[2,80,3072]{2,1,0:T(8,128)S(1)}, f32[1,80,3072]{2,1,0:T(8,128)S(1)}) custom-call(s32[5]{0:T(128)S(1)} %copy-done.3, s32[2,2,4]{2,1,0:T(2,128)S(1)} %add_clamp_fusion.offsets, f32[2,2,2,4]{3,2,1,0:T(2,128)S(1)} %copy-done.4, f32[2,40,2048]{2,1,0:T(8,128)S(1)} %collective-permute-done.2.m2, ...), custom_call_target="tpu_custom_call" | custom-call | flops 8999999488 | bytes 10485760 | tf_op jit(solution)/shard_map/middle/pallas_call | solution.py:418
  51.3 1.8 %collective-permute-start.9 = (f32[2,32,2048]{2,1,0:T(8,128)S(1)}, f32[2,32,2048]{2,1,0:T(8,128)S(1)}, u32[]{:S(2)}, u32[]{:S(2)}) collective-permute-start(f32[2,32,2048]{2,1,0:T(8,128)S(1)} %get-tuple-element.45), channel_id=1, source_target_pairs={{0,32},{16,48},{32,0},{48,16},{64,96},{80,112},{96,64},{112,80},{1... | collective-permute-start | bytes 1572872 | tf_op jit(solution)/shard_map/ppermute | solution.py:33
  53.1 4.5 %late.1 = (f32[2,32,2048]{2,1,0:T(8,128)S(1)}, f32[2,32,2048]{2,1,0:T(8,128)S(1)}) custom-call(s32[5]{0:T(128)S(1)} %copy-done.3, s32[2,2,4]{2,1,0:T(2,128)S(1)} %add_clamp_fusion.offsets, f32[2,2,2,4]{3,2,1,0:T(2,128)S(1)} %copy-done.4, f32[2,80,3072]{2,1,0:T(8,128)S(1)} %get-tuple-element.42.full1, f32[2,80,3072]{2,1,0:T(8,128)S(1)} %get-tuple-element.39.full2, ...), custom_call_target="tpu_custom_call" | custom-call | flops 7000000000 | bytes 4194304 | tf_op jit(solution)/shard_map/late/pallas_call | solution.py:424
  57.6 1.7 %collective-permute-start.7 = (f32[2,32,2048]{2,1,0:T(8,128)S(1)}, f32[2,32,2048]{2,1,0:T(8,128)S(1)}, u32[]{:S(2)}, u32[]{:S(2)}) collective-permute-start(f32[2,32,2048]{2,1,0:T(8,128)S(1)} %get-tuple-element.43), channel_id=1, source_target_pairs={{0,16},{16,0},{32,48},{48,32},{64,80},{80,64},{96,112},{112,96},{1... | collective-permute-start | bytes 1572872 | tf_op jit(solution)/shard_map/ppermute | solution.py:33
  59.3 2.2 %rest.1.refs_1_ = f32[2,128,2048]{2,1,0:T(8,128)} custom-call(s32[5]{0:T(128)S(1)} %copy-done.3, s32[2,2,4]{2,1,0:T(2,128)S(1)} %add_clamp_fusion.offsets, f32[2,2,2,4]{3,2,1,0:T(2,128)S(1)} %copy-done.4, f32[2,80,3072]{2,1,0:T(8,128)S(1)} %get-tuple-element.39.full2, f32[1,80,3072]{2,1,0:T(8,128)S(1)} %get-tuple-element.46.full2_2, ...), custom_call_target="tpu_custom_call" | custom-call | flops 3000000000 | bytes 3145728 | tf_op jit(solution)/shard_map/rest/pallas_call | solution.py:431
  61.6 4.5 %collective-permute-done.9.refs_0_ = f32[2,32,2048]{2,1,0:T(8,128)S(1)} collective-permute-done((f32[2,32,2048]{2,1,0:T(8,128)S(1)}, f32[2,32,2048]{2,1,0:T(8,128)S(1)}, u32[]{:S(2)}, u32[]{:S(2)}) %collective-permute-start.9) | collective-permute-done | bytes 524320 | tf_op jit(solution)/shard_map/ppermute | solution.py:33
  66.1 1.4 %place.2.refs_2_ = f32[2,128,2048]{2,1,0:T(8,128)} custom-call(s32[5]{0:T(128)S(1)} %copy-done.3, f32[2,32,2048]{2,1,0:T(8,128)S(1)} %collective-permute-done.9.refs_0_, f32[2,128,2048]{2,1,0:T(8,128)} %rest.1.refs_1_), custom_call_target="tpu_custom_call", output_to_operand_aliasing={{}: (2, {})} | custom-call | flops 99999997952 | bytes 2097152 | tf_op jit(solution)/shard_map/place/pallas_call | solution.py:438
  67.5 10.2 %collective-permute-done.7.refs_0_ = f32[2,32,2048]{2,1,0:T(8,128)S(1)} collective-permute-done((f32[2,32,2048]{2,1,0:T(8,128)S(1)}, f32[2,32,2048]{2,1,0:T(8,128)S(1)}, u32[]{:S(2)}, u32[]{:S(2)}) %collective-permute-start.7) | collective-permute-done | bytes 524320 | tf_op jit(solution)/shard_map/ppermute | solution.py:33
  77.7 0.3 collective-permute-done.8.refs_1_
  78.0 1.6 %place.3 = f32[2,128,2048]{2,1,0:T(8,128)} custom-call(s32[5]{0:T(128)S(1)} %copy-done.3, f32[2,32,2048]{2,1,0:T(8,128)S(1)} %collective-permute-done.7.refs_0_, f32[2,32,2048]{2,1,0:T(8,128)S(1)} %collective-permute-done.8.refs_1_, f32[2,128,2048]{2,1,0:T(8,128)} %place.2.refs_2_), custom_call_target="tpu_custom_call", output_to_operand_aliasing={{}: (3, {})} | custom-call | flops 100000 | bytes 2097152 | tf_op jit(solution)/shard_map/place/pallas_call | solution.py:438
  (45 shorter events, 1.5 us)
Async XLA Ops:
  0.0 14.0 %copy-start.6 = (f32[2,2,128]{2,1,0:T(2,128)S(1)}, f32[2,2,128]{2,1,0:T(2,128)}, u32[]{:S(2)}) copy-start(f32[2,2,128]{2,1,0:T(2,128)} %rates_in.1) | copy-start | bytes 6148
  0.0 14.0 %copy-start.5 = (s32[2,2,8]{2,1,0:T(2,128)S(1)}, s32[2,2,8]{2,1,0:T(2,128)}, u32[]{:S(2)}) copy-start(s32[2,2,8]{2,1,0:T(2,128)} %offs_in.1) | copy-start | bytes 388
  0.0 17.8 %copy-start = (f32[2,1,128,2048]{3,2,1,0:T(8,128)S(1)}, f32[2,1,128,2048]{3,2,1,0:T(8,128)}, u32[]{:S(2)}) copy-start(f32[2,1,128,2048]{3,2,1,0:T(8,128)} %param.5) | copy-start | bytes 6291460
  0.6 17.1 %copy-start.3 = (s32[5]{0:T(128)S(1)}, s32[5]{0:T(128)}, u32[]{:S(2)}) copy-start(s32[5]{0:T(128)} %stack.50.where) | copy-start | bytes 64
  3.9 10.4 %collective-permute-start = (f32[8,2048]{1,0:T(8,128)}, f32[8,2048]{1,0:T(8,128)S(1)}, u32[]{:S(2)}, u32[]{:S(2)}) collective-permute-start(f32[8,2048]{1,0:T(8,128)} %get-tuple-element.26), channel_id=1, source_target_pairs={{0,1},{1,2},{2,3},{3,4},{4,5},{5,6},{6,7},{7,8},{8,9},{9,10},{10,1... | collective-permute-start | bytes 196616 | tf_op jit(solution)/shard_map/ppermute | solution.py:371
  9.2 8.0 %collective-permute-start.1 = (f32[16,2048]{1,0:T(8,128)}, f32[16,2048]{1,0:T(8,128)S(1)}, u32[]{:S(2)}, u32[]{:S(2)}) collective-permute-start(f32[16,2048]{1,0:T(8,128)} %get-tuple-element.27), channel_id=1, source_target_pairs={{1,0},{2,1},{3,2},{4,3},{5,4},{6,5},{7,6},{8,7},{9,8},{10,9},{11,1... | collective-permute-start | bytes 393224 | tf_op jit(solution)/shard_map/ppermute | solution.py:372
  11.1 27.5 %collective-permute-start.3 = (f32[2,32,2048]{2,1,0:T(8,128)}, f32[2,32,2048]{2,1,0:T(8,128)S(1)}, u32[]{:S(2)}, u32[]{:S(2)}) collective-permute-start(f32[2,32,2048]{2,1,0:T(8,128)} %get-tuple-element.31), channel_id=1, source_target_pairs={{0,48},{16,32},{32,16},{48,0},{64,112},{80,96},{96,80},{112,64},{1... | collective-permute-start | bytes 1572872 | tf_op jit(solution)/shard_map/ppermute | solution.py:33
  14.0 17.0 %collective-permute-start.5 = (f32[2,32,2048]{2,1,0:T(8,128)}, f32[2,32,2048]{2,1,0:T(8,128)S(1)}, u32[]{:S(2)}, u32[]{:S(2)}) collective-permute-start(f32[2,32,2048]{2,1,0:T(8,128)} %get-tuple-element.35), channel_id=1, source_target_pairs={{0,16},{16,0},{32,48},{48,32},{64,80},{80,64},{96,112},{112,96},{1... | collective-permute-start | bytes 1572872 | tf_op jit(solution)/shard_map/ppermute | solution.py:33
  19.3 19.3 %collective-permute-start.4 = (f32[2,8,2048]{2,1,0:T(8,128)S(1)}, f32[2,8,2048]{2,1,0:T(8,128)S(1)}, u32[]{:S(2)}, u32[]{:S(2)}) collective-permute-start(f32[2,8,2048]{2,1,0:T(8,128)S(1)} %get-tuple-element.32), channel_id=1, source_target_pairs={{0,48},{16,32},{32,16},{48,0},{64,112},{80,96},{96,80},{112,64},{1... | collective-permute-start | bytes 393224 | tf_op jit(solution)/shard_map/ppermute | solution.py:33
  22.2 8.8 %collective-permute-start.6 = (f32[2,8,2048]{2,1,0:T(8,128)S(1)}, f32[2,8,2048]{2,1,0:T(8,128)S(1)}, u32[]{:S(2)}, u32[]{:S(2)}) collective-permute-start(f32[2,8,2048]{2,1,0:T(8,128)S(1)} %get-tuple-element.36), channel_id=1, source_target_pairs={{0,16},{16,0},{32,48},{48,32},{64,80},{80,64},{96,112},{112,96},{1... | collective-permute-start | bytes 393224 | tf_op jit(solution)/shard_map/ppermute | solution.py:33
  22.2 21.9 %collective-permute-start.2 = (f32[2,40,2048]{2,1,0:T(8,128)S(1)}, f32[2,40,2048]{2,1,0:T(8,128)S(1)}, u32[]{:S(2)}, u32[]{:S(2)}) collective-permute-start(f32[2,40,2048]{2,1,0:T(8,128)S(1)} %get-tuple-element.30), channel_id=1, source_target_pairs={{0,32},{16,48},{32,0},{48,16},{64,96},{80,112},{96,64},{112,80},{1... | collective-permute-start | bytes 1966088 | tf_op jit(solution)/shard_map/ppermute | solution.py:33
  23.4 2.8 %copy-start.1 = (f32[2,3,512,512]{3,2,1,0:T(8,128)S(1)}, f32[2,3,512,512]{3,2,1,0:T(8,128)}, u32[]{:S(2)}) copy-start(f32[2,3,512,512]{3,2,1,0:T(8,128)} %param.7) | copy-start | bytes 18874372
  26.2 4.7 %copy-start.2 = (f32[2,3,512,512]{3,2,1,0:T(8,128)S(1)}, f32[2,3,512,512]{3,2,1,0:T(8,128)}, u32[]{:S(2)}) copy-start(f32[2,3,512,512]{3,2,1,0:T(8,128)} %param.7) | copy-start | bytes 18874372
  29.2 1.7 %copy-start.4 = (f32[2,2,2,4]{3,2,1,0:T(2,128)S(1)}, f32[2,2,2,4]{3,2,1,0:T(2,128)}, u32[]{:S(2)}) copy-start(f32[2,2,2,4]{3,2,1,0:T(2,128)} %w_ref.7) | copy-start | bytes 388
  51.3 14.8 %collective-permute-start.9 = (f32[2,32,2048]{2,1,0:T(8,128)S(1)}, f32[2,32,2048]{2,1,0:T(8,128)S(1)}, u32[]{:S(2)}, u32[]{:S(2)}) collective-permute-start(f32[2,32,2048]{2,1,0:T(8,128)S(1)} %get-tuple-element.45), channel_id=1, source_target_pairs={{0,32},{16,48},{32,0},{48,16},{64,96},{80,112},{96,64},{112,80},{1... | collective-permute-start | bytes 1572872 | tf_op jit(solution)/shard_map/ppermute | solution.py:33
  57.6 20.1 %collective-permute-start.7 = (f32[2,32,2048]{2,1,0:T(8,128)S(1)}, f32[2,32,2048]{2,1,0:T(8,128)S(1)}, u32[]{:S(2)}, u32[]{:S(2)}) collective-permute-start(f32[2,32,2048]{2,1,0:T(8,128)S(1)} %get-tuple-element.43), channel_id=1, source_target_pairs={{0,16},{16,0},{32,48},{48,32},{64,80},{80,64},{96,112},{112,96},{1... | collective-permute-start | bytes 1572872 | tf_op jit(solution)/shard_map/ppermute | solution.py:33
  59.3 18.6 %collective-permute-start.8 = (f32[2,32,2048]{2,1,0:T(8,128)S(1)}, f32[2,32,2048]{2,1,0:T(8,128)S(1)}, u32[]{:S(2)}, u32[]{:S(2)}) collective-permute-start(f32[2,32,2048]{2,1,0:T(8,128)S(1)} %get-tuple-element.44), channel_id=1, source_target_pairs={{0,48},{16,32},{32,16},{48,0},{64,112},{80,96},{96,80},{112,64},{1... | collective-permute-start | bytes 1572872 | tf_op jit(solution)/shard_map/ppermute | solution.py:33

commit v5 on v4

--- a/solution.py
+++ b/solution.py
@@ -262,18 +262,22 @@
     range_products(high, low, th2, tl2, full2, 2)
 
 
+def third_kernel(m3, e3, th1, tl1, full1_3, high, low):
+    fill(m3, e3, high.at[0], low.at[0])
+    range_products(high, low, th1, tl1, full1_3, 1)
+
+
 def middle_kernel(
-    where, offsets, w_ref, m2, m3, e3, full2, th1, tl1, th2, tl2, within, across,
-    d2, full1, full2_2,
+    where, offsets, w_ref, m2, full1_3, full2, th1, tl1, th2, tl2, within, across,
+    d2, full1_2, full2_2,
     high, low,
 ):
     phases = (within, across)
     bit, bit2 = where[0], where[1]
     high[0], low[0] = split(m2[...].reshape(2 * ROWS, WIDTH))
-    fill(m3, e3, high.at[1], low.at[1])
-    range_products(high, low, th1, tl1, full1, 2)
+    range_products(high, low, th1, tl1, full1_2, 1)
     first_merges(
-        (full1.at[0], full1.at[1]), (bit, 1 - bit), (bit,),
+        (full1_2.at[0], full1_3.at[0]), (bit, 1 - bit), (bit,),
         where, offsets, w_ref, phases, high, low,
     )
     range_products(high, low, th2, tl2, full2_2, 1)
@@ -284,14 +288,14 @@
 
 
 def late_kernel(
-    where, offsets, w_ref, full1, full2, th2, tl2, within, across,
+    where, offsets, w_ref, full1_2, full1_3, full2, th2, tl2, within, across,
     d1, d3,
     high, low, full2_3,
 ):
     phases = (within, across)
     bit, bit2 = where[0], where[1]
     first_merges(
-        (full1.at[0], full1.at[1]), (bit, 1 - bit), (1 - bit,),
+        (full1_2.at[0], full1_3.at[0]), (bit, 1 - bit), (1 - bit,),
         where, offsets, w_ref, phases, high, low,
     )
     range_products(high, low, th2, tl2, full2_3, 1)
@@ -415,17 +419,20 @@
         halves_scratch(2) + [full_scratch(1), matrix_f32, dma((1,))],
         10**4, 10**4, vmem=28,
     )(*scalars, full1_0, m1, e1, t1h, t1l, matrices, within, across)
-    d2, full1, full2_2 = call(
-        middle_kernel, "middle", [piece_shape, two, one],
-        [SMEM] * 3 + [VMEM] * 10, [VMEM] * 3, halves_scratch(2),
+    (full1_3,) = call(
+        third_kernel, "third", [one], [VMEM] * 4, [VMEM], halves_scratch(1), 10**4, 10**4, vmem=12
+    )(m3, e3, t1h, t1l)
+    d2, full1_2, full2_2 = call(
+        middle_kernel, "middle", [piece_shape, one, one],
+        [SMEM] * 3 + [VMEM] * 9, [VMEM] * 3, halves_scratch(1),
         9 * 10**9, 10 * 2**20, vmem=24,
-    )(*scalars, m2, m3, e3, full2, t1h, t1l, t2h, t2l, within, across)
+    )(*scalars, m2, full1_3, full2, t1h, t1l, t2h, t2l, within, across)
     r2 = exchange(d2, 2)
     d1, d3 = call(
-        late_kernel, "late", [piece_shape] * 2, [SMEM] * 3 + [VMEM] * 6, [VMEM] * 2,
+        late_kernel, "late", [piece_shape] * 2, [SMEM] * 3 + [VMEM] * 7, [VMEM] * 2,
         halves_scratch(1) + [full_scratch(1)],
         7 * 10**9, 4 * 2**20, vmem=20,
-    )(*scalars, full1, full2, t2h, t2l, within, across)
+    )(*scalars, full1_2, full1_3, full2, t2h, t2l, within, across)
     r1 = exchange(d1, 1)
     r3 = exchange(d3, 3)
     (result,) = call(

time: 80.1 us -> 78.6 us (0.981)
  waiting for transfers between devices: 23.5 us -> 21.9 us
    ppermute x8, waiting for transfers between devices: 20.6 us -> 19 us  [exchange(): return lax.ppermute(value, 'grp', [(i, i ^ distance) for i in range(count)])]
    pallas_call x2 -> x3, Pallas kernels: 11.7 us -> 11.8 us  [the longest x1 5.68 us: per_device(): call(middle_kernel, 'middle', [piece_shape, one, one], [SMEM] * 3 + [VMEM...]
  transfers between devices with their start and end apart: 10 -> 10, of which waited for: 6 -> 5; matrix products, arithmetic and copies ran while one was open for 3% -> 3% of each run, Pallas kernels for 26% -> 28%
where the time goes in v5:
time: 78.6 us; the launch traced here: 78.2 us
  Pallas kernels  32.4 us (41%)
  waiting for transfers between devices  21.9 us (28%)
  starting transfers between devices  17.7 us (23%)
  local copies, waits for them, and re-layouts  4.15 us (5%)
  other arithmetic  1.66 us (2%)
    ppermute x8, waiting for transfers between devices, exchange(): return lax.ppermute(value, 'grp', [(i, i ^ distance) for i in range(count)])  19 us
    ppermute x8, starting transfers between devices, exchange(): return lax.ppermute(value, 'grp', [(i, i ^ distance) for i in range(count)])  10.5 us
    pallas_call x1, Pallas kernels, per_device(): call(early_kernel, 'early', [two, matrix_shape, matrix_shape], [SMEM] * 3...  7.71 us
    pallas_call x1, Pallas kernels, per_device(): call(middle_kernel, 'middle', [piece_shape, one, one], [SMEM] * 3 + [VMEM...  5.68 us
    ppermute x1, starting transfers between devices, per_device(): before = lax.ppermute(tail, 'beam', [(i, i + 1) for i in range(beams - 1)])  5.32 us
    pallas_call x1, Pallas kernels, per_device(): call(late_kernel, 'late', [piece_shape] * 2, [SMEM] * 3 + [VMEM] * 7, [VM...  4.51 us
    pallas_call x1, Pallas kernels, per_device(): call(pack_kernel, 'pack', [piece_shape, piece_shape, ((8, WIDTH), f32), (...  3.23 us
    pallas_call x1, Pallas kernels, per_device(): call(own_kernel, 'own', [one, matrix_shape, matrix_shape], [SMEM] + [HBM]...  2.95 us
  transfers between devices with their start and end apart: 10, of which 5 were waited for; matrix products, arithmetic and copies ran while one was open for 3% of the time, Pallas kernels for 28%

profile of v5, /device:TPU:97, one launch (start us, length us, event | category | flops | bytes accessed | tf_op | source)
XLA Modules:
  0.0 78.2 jit_solution(8504960354560859980)
XLA Ops:
  0.0 0.6 stack.50.where
  0.6 3.2 %pack.1 = (f32[2,32,2048]{2,1,0:T(8,128)}, f32[2,32,2048]{2,1,0:T(8,128)}, f32[8,2048]{1,0:T(8,128)}, f32[16,2048]{1,0:T(8,128)}) custom-call(f32[2,2,128]{2,1,0:T(2,128)} %rates_in.1, s32[2,2,8]{2,1,0:T(2,128)} %offs_in.1, s32[5]{0:T(128)} %stack.50.where, f32[2,128,2048]{2,1,0:T(8,128)} %bitcast.24), custom_call_target="tpu_custom_call" | custom-call | flops 1000000 | bytes 1048576 | tf_op jit(solution)/shard_map/pack/pallas_call | solution.py:366
  3.9 5.3 %collective-permute-start = (f32[8,2048]{1,0:T(8,128)}, f32[8,2048]{1,0:T(8,128)S(1)}, u32[]{:S(2)}, u32[]{:S(2)}) collective-permute-start(f32[8,2048]{1,0:T(8,128)} %get-tuple-element.26), channel_id=1, source_target_pairs={{0,1},{1,2},{2,3},{3,4},{4,5},{5,6},{6,7},{7,8},{8,9},{9,10},{10,1... | collective-permute-start | bytes 196616 | tf_op jit(solution)/shard_map/ppermute | solution.py:375
  9.2 1.9 %collective-permute-start.1 = (f32[16,2048]{1,0:T(8,128)}, f32[16,2048]{1,0:T(8,128)S(1)}, u32[]{:S(2)}, u32[]{:S(2)}) collective-permute-start(f32[16,2048]{1,0:T(8,128)} %get-tuple-element.27), channel_id=1, source_target_pairs={{1,0},{2,1},{3,2},{4,3},{5,4},{6,5},{7,6},{8,7},{9,8},{10,9},{11,1... | collective-permute-start | bytes 393224 | tf_op jit(solution)/shard_map/ppermute | solution.py:376
  11.1 2.8 %collective-permute-start.3 = (f32[2,32,2048]{2,1,0:T(8,128)}, f32[2,32,2048]{2,1,0:T(8,128)S(1)}, u32[]{:S(2)}, u32[]{:S(2)}) collective-permute-start(f32[2,32,2048]{2,1,0:T(8,128)} %get-tuple-element.31), channel_id=1, source_target_pairs={{0,48},{16,32},{32,16},{48,0},{64,112},{80,96},{96,80},{112,64},{1... | collective-permute-start | bytes 1572872 | tf_op jit(solution)/shard_map/ppermute | solution.py:33
  14.3 2.9 %collective-permute-done.1.after = f32[16,2048]{1,0:T(8,128)S(1)} collective-permute-done((f32[16,2048]{1,0:T(8,128)}, f32[16,2048]{1,0:T(8,128)S(1)}, u32[]{:S(2)}, u32[]{:S(2)}) %collective-permute-start.1) | collective-permute-done | bytes 131104 | tf_op jit(solution)/shard_map/ppermute | solution.py:376
  17.8 1.5 %rims.1 = (f32[2,8,2048]{2,1,0:T(8,128)S(1)}, f32[2,8,2048]{2,1,0:T(8,128)S(1)}, f32[2,8,2048]{2,1,0:T(8,128)S(1)}, f32[2,40,2048]{2,1,0:T(8,128)S(1)}) custom-call(s32[5]{0:T(128)S(1)} %copy-done.3, f32[2,128,2048]{2,1,0:T(8,128)S(1)} %bitcast.25, f32[8,2048]{1,0:T(8,128)S(1)} %collective-permute-done.before, f32[16,2048]{1,0:T(8,128)S(1)} %collective-permute-done.1.after), custom_call_target="tpu_custom_call" | custom-call | flops 1000000 | bytes 3145728 | tf_op jit(solution)/shard_map/rims/pallas_call | solution.py:378
  19.3 2.8 %collective-permute-start.4 = (f32[2,8,2048]{2,1,0:T(8,128)S(1)}, f32[2,8,2048]{2,1,0:T(8,128)S(1)}, u32[]{:S(2)}, u32[]{:S(2)}) collective-permute-start(f32[2,8,2048]{2,1,0:T(8,128)S(1)} %get-tuple-element.32), channel_id=1, source_target_pairs={{0,48},{16,32},{32,16},{48,0},{64,112},{80,96},{96,80},{112,64},{1... | collective-permute-start | bytes 393224 | tf_op jit(solution)/shard_map/ppermute | solution.py:33
  22.2 1.3 %collective-permute-start.2 = (f32[2,40,2048]{2,1,0:T(8,128)S(1)}, f32[2,40,2048]{2,1,0:T(8,128)S(1)}, u32[]{:S(2)}, u32[]{:S(2)}) collective-permute-start(f32[2,40,2048]{2,1,0:T(8,128)S(1)} %get-tuple-element.30), channel_id=1, source_target_pairs={{0,32},{16,48},{32,0},{48,16},{64,96},{80,112},{96,64},{112,80},{1... | collective-permute-start | bytes 1966088 | tf_op jit(solution)/shard_map/ppermute | solution.py:33
  23.5 2.8 %copy-done.1 = f32[2,3,512,512]{3,2,1,0:T(8,128)S(1)} copy-done((f32[2,3,512,512]{3,2,1,0:T(8,128)S(1)}, f32[2,3,512,512]{3,2,1,0:T(8,128)}, u32[]{:S(2)}) %copy-start.1) | copy-done | bytes 6291480
  26.2 3.0 %own.1 = (f32[1,80,3072]{2,1,0:T(8,128)S(1)}, bf16[1536,512]{1,0:T(8,128)(2,1)S(1)}, bf16[1536,512]{1,0:T(8,128)(2,1)S(1)}) custom-call(s32[5]{0:T(128)S(1)} %copy-done.3, f32[2,1536,512]{2,1,0:T(8,128)S(1)} %bitcast.27, f32[2,128,2048]{2,1,0:T(8,128)S(1)} %bitcast.26, f32[2,8,2048]{2,1,0:T(8,128)S(1)} %get-tuple-element.33.e0), custom_call_target="tpu_custom_call" | custom-call | flops 30000001024 | bytes 8388608 | tf_op jit(solution)/shard_map/own/pallas_call | solution.py:411
  29.6 1.1 %multiply_cosine_fusion = (f32[1,2,72,512]{3,2,1,0:T(8,128)S(1)}, f32[1,2,72,512]{3,2,1,0:T(8,128)S(1)}) fusion(f32[512]{0:T(512)S(1)} %iota_multiply_fusion.1, f32[2,72]{1,0:T(2,128)S(1)} %pad_maximum_fusion.3), kind=kLoop, calls=%fused_computation.3 | loop fusion | flops 73728 | bytes 592448 | tf_op jit(solution)/shard_map/cos | solution.py:400
  30.8 1.6 %third.1.full1_3 = f32[1,80,3072]{2,1,0:T(8,128)S(1)} custom-call(f32[2,32,2048]{2,1,0:T(8,128)S(1)} %collective-permute-done.3.m3, f32[2,8,2048]{2,1,0:T(8,128)S(1)} %collective-permute-done.4.e3, bf16[1536,512]{1,0:T(8,128)(2,1)S(1)} %get-tuple-element.34.th1, bf16[1536,512]{1,0:T(8,128)(2,1)S(1)} %get-tuple-element.35.tl1), custom_call_target="tpu_custom_call" | custom-call | flops 10000 | bytes 10000 | tf_op jit(solution)/shard_map/third/pallas_call | solution.py:422
  32.4 7.7 %early.1 = (f32[2,80,3072]{2,1,0:T(8,128)S(1)}, bf16[1536,512]{1,0:T(8,128)(2,1)S(1)}, bf16[1536,512]{1,0:T(8,128)(2,1)S(1)}) custom-call(s32[5]{0:T(128)S(1)} %copy-done.3, s32[2,2,4]{2,1,0:T(2,128)S(1)} %add_clamp_fusion.offsets, f32[2,2,2,4]{3,2,1,0:T(2,128)S(1)} %copy-done.4, f32[1,80,3072]{2,1,0:T(8,128)S(1)} %get-tuple-element.36.full1_0, ...), custom_call_target="tpu_custom_call" | custom-call | flops 10000 | bytes 10000 | tf_op jit(solution)/shard_map/early/pallas_call | solution.py:416
  40.1 3.9 %collective-permute-done.2.m2 = f32[2,40,2048]{2,1,0:T(8,128)S(1)} collective-permute-done((f32[2,40,2048]{2,1,0:T(8,128)S(1)}, f32[2,40,2048]{2,1,0:T(8,128)S(1)}, u32[]{:S(2)}, u32[]{:S(2)}) %collective-permute-start.2) | collective-permute-done | bytes 655392 | tf_op jit(solution)/shard_map/ppermute | solution.py:33
  44.1 5.7 %middle.1 = (f32[2,32,2048]{2,1,0:T(8,128)S(1)}, f32[1,80,3072]{2,1,0:T(8,128)S(1)}, f32[1,80,3072]{2,1,0:T(8,128)S(1)}) custom-call(s32[5]{0:T(128)S(1)} %copy-done.3, s32[2,2,4]{2,1,0:T(2,128)S(1)} %add_clamp_fusion.offsets, f32[2,2,2,4]{3,2,1,0:T(2,128)S(1)} %copy-done.4, f32[2,40,2048]{2,1,0:T(8,128)S(1)} %collective-permute-done.2.m2, ...), custom_call_target="tpu_custom_call" | custom-call | flops 8999999488 | bytes 10485760 | tf_op jit(solution)/shard_map/middle/pallas_call | solution.py:425
  49.8 1.8 %collective-permute-start.9 = (f32[2,32,2048]{2,1,0:T(8,128)S(1)}, f32[2,32,2048]{2,1,0:T(8,128)S(1)}, u32[]{:S(2)}, u32[]{:S(2)}) collective-permute-start(f32[2,32,2048]{2,1,0:T(8,128)S(1)} %get-tuple-element.45), channel_id=1, source_target_pairs={{0,32},{16,48},{32,0},{48,16},{64,96},{80,112},{96,64},{112,80},{1... | collective-permute-start | bytes 1572872 | tf_op jit(solution)/shard_map/ppermute | solution.py:33
  51.5 4.5 %late.1 = (f32[2,32,2048]{2,1,0:T(8,128)S(1)}, f32[2,32,2048]{2,1,0:T(8,128)S(1)}) custom-call(s32[5]{0:T(128)S(1)} %copy-done.3, s32[2,2,4]{2,1,0:T(2,128)S(1)} %add_clamp_fusion.offsets, f32[2,2,2,4]{3,2,1,0:T(2,128)S(1)} %copy-done.4, f32[1,80,3072]{2,1,0:T(8,128)S(1)} %get-tuple-element.42.full1_2, f32[1,80,3072]{2,1,0:T(8,128)S(1)} %third.1.full1_3, ...), custom_call_target="tpu_custom_call" | custom-call | flops 7000000000 | bytes 4194304 | tf_op jit(solution)/shard_map/late/pallas_call | solution.py:431
  56.1 1.7 %collective-permute-start.7 = (f32[2,32,2048]{2,1,0:T(8,128)S(1)}, f32[2,32,2048]{2,1,0:T(8,128)S(1)}, u32[]{:S(2)}, u32[]{:S(2)}) collective-permute-start(f32[2,32,2048]{2,1,0:T(8,128)S(1)} %get-tuple-element.43), channel_id=1, source_target_pairs={{0,16},{16,0},{32,48},{48,32},{64,80},{80,64},{96,112},{112,96},{1... | collective-permute-start | bytes 1572872 | tf_op jit(solution)/shard_map/ppermute | solution.py:33
  57.8 2.2 %rest.1.refs_1_ = f32[2,128,2048]{2,1,0:T(8,128)} custom-call(s32[5]{0:T(128)S(1)} %copy-done.3, s32[2,2,4]{2,1,0:T(2,128)S(1)} %add_clamp_fusion.offsets, f32[2,2,2,4]{3,2,1,0:T(2,128)S(1)} %copy-done.4, f32[2,80,3072]{2,1,0:T(8,128)S(1)} %get-tuple-element.39.full2, f32[1,80,3072]{2,1,0:T(8,128)S(1)} %get-tuple-element.46.full2_2, ...), custom_call_target="tpu_custom_call" | custom-call | flops 3000000000 | bytes 3145728 | tf_op jit(solution)/shard_map/rest/pallas_call | solution.py:438
  60.1 4.5 %collective-permute-done.9.refs_0_ = f32[2,32,2048]{2,1,0:T(8,128)S(1)} collective-permute-done((f32[2,32,2048]{2,1,0:T(8,128)S(1)}, f32[2,32,2048]{2,1,0:T(8,128)S(1)}, u32[]{:S(2)}, u32[]{:S(2)}) %collective-permute-start.9) | collective-permute-done | bytes 524320 | tf_op jit(solution)/shard_map/ppermute | solution.py:33
  64.5 1.4 %place.2.refs_2_ = f32[2,128,2048]{2,1,0:T(8,128)} custom-call(s32[5]{0:T(128)S(1)} %copy-done.3, f32[2,32,2048]{2,1,0:T(8,128)S(1)} %collective-permute-done.9.refs_0_, f32[2,128,2048]{2,1,0:T(8,128)} %rest.1.refs_1_), custom_call_target="tpu_custom_call", output_to_operand_aliasing={{}: (2, {})} | custom-call | flops 99999997952 | bytes 2097152 | tf_op jit(solution)/shard_map/place/pallas_call | solution.py:445
  65.9 10.2 %collective-permute-done.7.refs_0_ = f32[2,32,2048]{2,1,0:T(8,128)S(1)} collective-permute-done((f32[2,32,2048]{2,1,0:T(8,128)S(1)}, f32[2,32,2048]{2,1,0:T(8,128)S(1)}, u32[]{:S(2)}, u32[]{:S(2)}) %collective-permute-start.7) | collective-permute-done | bytes 524320 | tf_op jit(solution)/shard_map/ppermute | solution.py:33
  76.4 1.6 %place.3 = f32[2,128,2048]{2,1,0:T(8,128)} custom-call(s32[5]{0:T(128)S(1)} %copy-done.3, f32[2,32,2048]{2,1,0:T(8,128)S(1)} %collective-permute-done.7.refs_0_, f32[2,32,2048]{2,1,0:T(8,128)S(1)} %collective-permute-done.8.refs_1_, f32[2,128,2048]{2,1,0:T(8,128)} %place.2.refs_2_), custom_call_target="tpu_custom_call", output_to_operand_aliasing={{}: (3, {})} | custom-call | flops 100000 | bytes 2097152 | tf_op jit(solution)/shard_map/place/pallas_call | solution.py:445
  (46 shorter events, 1.6 us)
Async XLA Ops:
  0.0 14.0 %copy-start.6 = (f32[2,2,128]{2,1,0:T(2,128)S(1)}, f32[2,2,128]{2,1,0:T(2,128)}, u32[]{:S(2)}) copy-start(f32[2,2,128]{2,1,0:T(2,128)} %rates_in.1) | copy-start | bytes 6148
  0.0 14.0 %copy-start.5 = (s32[2,2,8]{2,1,0:T(2,128)S(1)}, s32[2,2,8]{2,1,0:T(2,128)}, u32[]{:S(2)}) copy-start(s32[2,2,8]{2,1,0:T(2,128)} %offs_in.1) | copy-start | bytes 388
  0.0 17.8 %copy-start = (f32[2,1,128,2048]{3,2,1,0:T(8,128)S(1)}, f32[2,1,128,2048]{3,2,1,0:T(8,128)}, u32[]{:S(2)}) copy-start(f32[2,1,128,2048]{3,2,1,0:T(8,128)} %param.5) | copy-start | bytes 6291460
  0.6 17.1 %copy-start.3 = (s32[5]{0:T(128)S(1)}, s32[5]{0:T(128)}, u32[]{:S(2)}) copy-start(s32[5]{0:T(128)} %stack.50.where) | copy-start | bytes 64
  3.9 10.4 %collective-permute-start = (f32[8,2048]{1,0:T(8,128)}, f32[8,2048]{1,0:T(8,128)S(1)}, u32[]{:S(2)}, u32[]{:S(2)}) collective-permute-start(f32[8,2048]{1,0:T(8,128)} %get-tuple-element.26), channel_id=1, source_target_pairs={{0,1},{1,2},{2,3},{3,4},{4,5},{5,6},{6,7},{7,8},{8,9},{9,10},{10,1... | collective-permute-start | bytes 196616 | tf_op jit(solution)/shard_map/ppermute | solution.py:375
  9.2 8.0 %collective-permute-start.1 = (f32[16,2048]{1,0:T(8,128)}, f32[16,2048]{1,0:T(8,128)S(1)}, u32[]{:S(2)}, u32[]{:S(2)}) collective-permute-start(f32[16,2048]{1,0:T(8,128)} %get-tuple-element.27), channel_id=1, source_target_pairs={{1,0},{2,1},{3,2},{4,3},{5,4},{6,5},{7,6},{8,7},{9,8},{10,9},{11,1... | collective-permute-start | bytes 393224 | tf_op jit(solution)/shard_map/ppermute | solution.py:376
  11.1 19.6 %collective-permute-start.3 = (f32[2,32,2048]{2,1,0:T(8,128)}, f32[2,32,2048]{2,1,0:T(8,128)S(1)}, u32[]{:S(2)}, u32[]{:S(2)}) collective-permute-start(f32[2,32,2048]{2,1,0:T(8,128)} %get-tuple-element.31), channel_id=1, source_target_pairs={{0,48},{16,32},{32,16},{48,0},{64,112},{80,96},{96,80},{112,64},{1... | collective-permute-start | bytes 1572872 | tf_op jit(solution)/shard_map/ppermute | solution.py:33
  14.0 18.4 %collective-permute-start.5 = (f32[2,32,2048]{2,1,0:T(8,128)}, f32[2,32,2048]{2,1,0:T(8,128)S(1)}, u32[]{:S(2)}, u32[]{:S(2)}) collective-permute-start(f32[2,32,2048]{2,1,0:T(8,128)} %get-tuple-element.37), channel_id=1, source_target_pairs={{0,16},{16,0},{32,48},{48,32},{64,80},{80,64},{96,112},{112,96},{1... | collective-permute-start | bytes 1572872 | tf_op jit(solution)/shard_map/ppermute | solution.py:33
  19.3 11.4 %collective-permute-start.4 = (f32[2,8,2048]{2,1,0:T(8,128)S(1)}, f32[2,8,2048]{2,1,0:T(8,128)S(1)}, u32[]{:S(2)}, u32[]{:S(2)}) collective-permute-start(f32[2,8,2048]{2,1,0:T(8,128)S(1)} %get-tuple-element.32), channel_id=1, source_target_pairs={{0,48},{16,32},{32,16},{48,0},{64,112},{80,96},{96,80},{112,64},{1... | collective-permute-start | bytes 393224 | tf_op jit(solution)/shard_map/ppermute | solution.py:33
  22.2 10.2 %collective-permute-start.6 = (f32[2,8,2048]{2,1,0:T(8,128)S(1)}, f32[2,8,2048]{2,1,0:T(8,128)S(1)}, u32[]{:S(2)}, u32[]{:S(2)}) collective-permute-start(f32[2,8,2048]{2,1,0:T(8,128)S(1)} %get-tuple-element.38), channel_id=1, source_target_pairs={{0,16},{16,0},{32,48},{48,32},{64,80},{80,64},{96,112},{112,96},{1... | collective-permute-start | bytes 393224 | tf_op jit(solution)/shard_map/ppermute | solution.py:33
  22.2 21.9 %collective-permute-start.2 = (f32[2,40,2048]{2,1,0:T(8,128)S(1)}, f32[2,40,2048]{2,1,0:T(8,128)S(1)}, u32[]{:S(2)}, u32[]{:S(2)}) collective-permute-start(f32[2,40,2048]{2,1,0:T(8,128)S(1)} %get-tuple-element.30), channel_id=1, source_target_pairs={{0,32},{16,48},{32,0},{48,16},{64,96},{80,112},{96,64},{112,80},{1... | collective-permute-start | bytes 1966088 | tf_op jit(solution)/shard_map/ppermute | solution.py:33
  23.4 2.8 %copy-start.1 = (f32[2,3,512,512]{3,2,1,0:T(8,128)S(1)}, f32[2,3,512,512]{3,2,1,0:T(8,128)}, u32[]{:S(2)}) copy-start(f32[2,3,512,512]{3,2,1,0:T(8,128)} %param.7) | copy-start | bytes 18874372
  29.6 2.8 %copy-start.2 = (f32[2,3,512,512]{3,2,1,0:T(8,128)S(1)}, f32[2,3,512,512]{3,2,1,0:T(8,128)}, u32[]{:S(2)}) copy-start(f32[2,3,512,512]{3,2,1,0:T(8,128)} %param.7) | copy-start | bytes 18874372
  30.8 1.6 %copy-start.4 = (f32[2,2,2,4]{3,2,1,0:T(2,128)S(1)}, f32[2,2,2,4]{3,2,1,0:T(2,128)}, u32[]{:S(2)}) copy-start(f32[2,2,2,4]{3,2,1,0:T(2,128)} %w_ref.7) | copy-start | bytes 388
  49.8 14.8 %collective-permute-start.9 = (f32[2,32,2048]{2,1,0:T(8,128)S(1)}, f32[2,32,2048]{2,1,0:T(8,128)S(1)}, u32[]{:S(2)}, u32[]{:S(2)}) collective-permute-start(f32[2,32,2048]{2,1,0:T(8,128)S(1)} %get-tuple-element.45), channel_id=1, source_target_pairs={{0,32},{16,48},{32,0},{48,16},{64,96},{80,112},{96,64},{112,80},{1... | collective-permute-start | bytes 1572872 | tf_op jit(solution)/shard_map/ppermute | solution.py:33
  56.1 20.1 %collective-permute-start.7 = (f32[2,32,2048]{2,1,0:T(8,128)S(1)}, f32[2,32,2048]{2,1,0:T(8,128)S(1)}, u32[]{:S(2)}, u32[]{:S(2)}) collective-permute-start(f32[2,32,2048]{2,1,0:T(8,128)S(1)} %get-tuple-element.43), channel_id=1, source_target_pairs={{0,16},{16,0},{32,48},{48,32},{64,80},{80,64},{96,112},{112,96},{1... | collective-permute-start | bytes 1572872 | tf_op jit(solution)/shard_map/ppermute | solution.py:33
  57.8 18.6 %collective-permute-start.8 = (f32[2,32,2048]{2,1,0:T(8,128)S(1)}, f32[2,32,2048]{2,1,0:T(8,128)S(1)}, u32[]{:S(2)}, u32[]{:S(2)}) collective-permute-start(f32[2,32,2048]{2,1,0:T(8,128)S(1)} %get-tuple-element.44), channel_id=1, source_target_pairs={{0,48},{16,32},{32,16},{48,0},{64,112},{80,96},{96,80},{112,64},{1... | collective-permute-start | bytes 1572872 | tf_op jit(solution)/shard_map/ppermute | solution.py:33
